TPU v7x, 32 devices: a whole 2x2x4 slice. The times are simulated.
32 devices in a mesh: ctx: 8 (over y, x, core), fsdp: 4 (over z).
Axes of the slice: x: 2, y: 2, z: 4, core: 2. Of those that a mesh axis runs over, the one named last changes fastest.
Arguments:
- tokens: bfloat16 [4, 2048, 2048], P('fsdp', 'ctx'), may hold values from -6 to 6
- doc_ids: int32 [4, 2048], P('fsdp'), may hold values from 0 to 2, as said below
- block_pairs: int32 [8], replicated, may hold values from 0 to 7, each once
- ln1_gain: bfloat16 [2048], P('fsdp'), may hold values from 0.099609375 to 1.8984375
- ln1_bias: bfloat16 [2048], P('fsdp'), may hold values from -1.5 to 1.5
- w_qkv: bfloat16 [2048, 6144], P('fsdp'), may hold values from -0.125 to 0.125
- b_qkv: bfloat16 [6144], P('fsdp'), may hold values from -1.5 to 1.5
- w_out: bfloat16 [2048, 2048], P('fsdp'), may hold values from -1 to 1
- ln2_gain: bfloat16 [2048], P('fsdp'), may hold values from 0.099609375 to 1.8984375
- ln2_bias: bfloat16 [2048], P('fsdp'), may hold values from -1.5 to 1.5
- w_gate: bfloat16 [2048, 5632], P('fsdp'), may hold values from -0.125 to 0.125
- w_up: bfloat16 [2048, 5632], P('fsdp'), may hold values from -0.125 to 0.125
- w_down: bfloat16 [5632, 2048], P('fsdp'), may hold values from -0.078125 to 0.078125
- cotangent: bfloat16 [4, 2048, 2048], P('fsdp', 'ctx'), may hold values from -6 to 6
Outputs:
- layer_out: bfloat16 [4, 2048, 2048], P('fsdp', 'ctx')
- grad_tokens: float32 [4, 2048, 2048], P('fsdp', 'ctx')
- grad_ln1_gain: float32 [2048], P('fsdp')
- grad_ln1_bias: float32 [2048], P('fsdp')
- grad_w_qkv: float32 [2048, 6144], P('fsdp')
- grad_b_qkv: float32 [6144], P('fsdp')
- grad_w_out: float32 [2048, 2048], P('fsdp')
- grad_ln2_gain: float32 [2048], P('fsdp')
- grad_ln2_bias: float32 [2048], P('fsdp')
- grad_w_gate: float32 [2048, 5632], P('fsdp')
- grad_w_up: float32 [2048, 5632], P('fsdp')
- grad_w_down: float32 [5632, 2048], P('fsdp')
Inputs may be any that keep to these rules, and one draw needn't show every extreme that they name: In each pack doc_ids never falls, starts at 0 and names three documents; one of them covers the first or the last half of the pack's places. Each value once; ctx device c holds in its first 128 rows the block of places block_pairs[c] and in its last ones block 15 - block_pairs[c], blocks of 128 places.
All inputs are finite; a program needn't handle non-finite values.
Results may differ from a plain program's by a relative error of at most 0.02.
Values may be sent and summed in bfloat16 or wider, within the bound.
A program may use at most 704 MiB of HBM per device.

v0:
```python
import jax
import jax.numpy as jnp
from jax import lax
from jax.sharding import PartitionSpec as P

HEAD = 64
ROT = 16


NORM_EPSILON = 1e-05
ROTARY_BASE = 10000.0
MASKED_SCORE = -1e30


def norm_rows(values, gain_row, shift_row):
    centered = values - jnp.mean(values, -1, keepdims=True)
    inverse = lax.rsqrt(jnp.mean(centered * centered, -1, keepdims=True) + NORM_EPSILON)
    unit_rows = centered * inverse
    return (unit_rows * gain_row + shift_row, unit_rows, inverse)


def norm_back(grad_rows, unit_rows, inverse, gain_row):
    scaled = grad_rows * gain_row
    return inverse * (
        scaled
        - jnp.mean(scaled, -1, keepdims=True)
        - unit_rows * jnp.mean(scaled * unit_rows, -1, keepdims=True)
    )


def row_places(row_ids, block_pairs, rows_here, axis_size):
    half_rows = rows_here // 2
    owners = row_ids // rows_here
    second = row_ids // half_rows % 2
    matches = owners[:, None] == jnp.arange(axis_size, dtype=jnp.int32)[None, :]
    first_block = jnp.sum(jnp.where(matches, block_pairs[None, :], 0), 1)
    blocks = jnp.where(second == 0, first_block, 2 * axis_size - 1 - first_block)
    return blocks * half_rows + row_ids % half_rows


def rotate(heads_in, angles, turn_sign):
    half_rot = ROT // 2
    cosine = jnp.cos(angles)[:, None, :]
    sine_row = turn_sign * jnp.sin(angles)[:, None, :]
    front_half = heads_in[..., :half_rot]
    behind = heads_in[..., half_rot:ROT]
    return jnp.concatenate(
        [
            front_half * cosine - behind * sine_row,
            behind * cosine + front_half * sine_row,
            heads_in[..., ROT:],
        ],
        -1,
    )


def inner(left_side, right_side):
    return lax.dot_general(
        left_side, right_side, (((0,), (0,)), ((), ())), preferred_element_type=jnp.float32
    )


def times_transposed(left_side, right_side):
    return lax.dot_general(
        left_side, right_side, (((1,), (1,)), ((), ())), preferred_element_type=jnp.float32
    )


def body(
    tokens,
    doc_ids,
    block_pairs,
    ln1_gain,
    ln1_bias,
    w_qkv,
    b_qkv,
    w_out,
    ln2_gain,
    ln2_bias,
    w_gate,
    w_up,
    w_down,
    cotangent,
):
    rows_here = tokens.shape[1]
    model_width = tokens.shape[2]
    head_count = model_width // HEAD
    ctx_size = lax.axis_size("ctx")
    seq_rows = rows_here * ctx_size
    position = lax.axis_index("ctx")
    score_scale = HEAD ** (-0.5)
    key_places = row_places(jnp.arange(seq_rows, dtype=jnp.int32), block_pairs, rows_here, ctx_size)
    key_docs = jnp.take(doc_ids[0], key_places)
    query_places = lax.dynamic_slice_in_dim(key_places, position * rows_here, rows_here)
    query_docs = lax.dynamic_slice_in_dim(key_docs, position * rows_here, rows_here)
    inverse_freq = ROTARY_BASE ** (-jnp.arange(ROT // 2, dtype=jnp.float32) * 2.0 / ROT)
    angles = query_places.astype(jnp.float32)[:, None] * inverse_freq[None, :]
    block_rows = min(512, seq_rows)
    block_count = seq_rows // block_rows
    place_blocks = key_places.reshape(block_count, block_rows)
    doc_blocks = key_docs.reshape(block_count, block_rows)
    tokens_in = tokens[0].astype(jnp.float32)
    gain_one, shift_one, qkv_full, bias_full, out_full = (
        lax.all_gather(ln1_gain, "fsdp", axis=0, tiled=True),
        lax.all_gather(ln1_bias, "fsdp", axis=0, tiled=True),
        lax.all_gather(w_qkv, "fsdp", axis=0, tiled=True),
        lax.all_gather(b_qkv, "fsdp", axis=0, tiled=True),
        lax.all_gather(w_out, "fsdp", axis=0, tiled=True),
    )
    normed, unit_one, inverse_one = norm_rows(
        tokens_in, gain_one.astype(jnp.float32), shift_one.astype(jnp.float32)
    )
    normed_low = normed.astype(jnp.bfloat16)
    projected = jnp.dot(
        normed_low, qkv_full, preferred_element_type=jnp.float32
    ) + bias_full.astype(jnp.float32)
    split_heads = projected.reshape(rows_here, 3, head_count, HEAD)
    queries = rotate(split_heads[:, 0], angles, 1.0).astype(jnp.bfloat16)
    key_rows = (
        rotate(split_heads[:, 1], angles, 1.0).astype(jnp.bfloat16).reshape(rows_here, model_width)
    )
    value_rows = split_heads[:, 2].astype(jnp.bfloat16).reshape(rows_here, model_width)
    keys_all, values_all = (
        lax.all_gather(key_rows, "ctx", axis=0, tiled=True),
        lax.all_gather(value_rows, "ctx", axis=0, tiled=True),
    )
    key_blocks = keys_all.reshape(block_count, block_rows, head_count, HEAD)
    value_blocks = values_all.reshape(block_count, block_rows, head_count, HEAD)

    def block_scores(key_block, place_block, doc_block):
        raw_scores = jnp.einsum(
            "qhd,khd->hqk", queries, key_block, preferred_element_type=jnp.float32
        )
        allowed = (query_places[:, None] >= place_block[None, :]) & (
            query_docs[:, None] == doc_block[None, :]
        )
        return (raw_scores * score_scale, allowed[None])

    def max_and_total(carried, block_args):
        running_max, running_total = carried
        scaled, allowed = block_scores(block_args[0], block_args[1], block_args[2])
        scores = jnp.where(allowed, scaled, MASKED_SCORE)
        new_max = jnp.maximum(running_max, jnp.max(scores, -1))
        exps = jnp.where(allowed, jnp.exp(scores - new_max[..., None]), 0.0)
        running_total = running_total * jnp.exp(running_max - new_max) + jnp.sum(exps, -1)
        return ((new_max, running_total), None)

    start_max = jnp.full((head_count, rows_here), MASKED_SCORE, jnp.float32)
    start_total = jnp.zeros((head_count, rows_here), jnp.float32)
    (row_max, row_total), unused = lax.scan(
        max_and_total, (start_max, start_total), (key_blocks, place_blocks, doc_blocks)
    )
    log_total = row_max + jnp.log(row_total)

    def weigh_values(summed, block_args):
        key_block, value_block, place_block, doc_block = block_args
        scaled, allowed = block_scores(key_block, place_block, doc_block)
        soft_weights = jnp.where(allowed, jnp.exp(scaled - log_total[..., None]), 0.0)
        summed = summed + jnp.einsum(
            "hqk,khd->qhd",
            soft_weights.astype(jnp.bfloat16),
            value_block,
            preferred_element_type=jnp.float32,
        )
        return (summed, None)

    attended, unused = lax.scan(
        weigh_values,
        jnp.zeros((rows_here, head_count, HEAD), jnp.float32),
        (key_blocks, value_blocks, place_blocks, doc_blocks),
    )
    mixed_heads = attended.reshape(rows_here, model_width).astype(jnp.bfloat16)
    residual = tokens_in + jnp.dot(mixed_heads, out_full, preferred_element_type=jnp.float32)
    gain_two, shift_two, gate_full, up_full, down_full = (
        lax.all_gather(ln2_gain, "fsdp", axis=0, tiled=True),
        lax.all_gather(ln2_bias, "fsdp", axis=0, tiled=True),
        lax.all_gather(w_gate, "fsdp", axis=0, tiled=True),
        lax.all_gather(w_up, "fsdp", axis=0, tiled=True),
        lax.all_gather(w_down, "fsdp", axis=0, tiled=True),
    )
    normed_two, unit_two, inverse_two = norm_rows(
        residual, gain_two.astype(jnp.float32), shift_two.astype(jnp.float32)
    )
    normed_two_low = normed_two.astype(jnp.bfloat16)
    gate_value = jnp.dot(normed_two_low, gate_full, preferred_element_type=jnp.float32)
    up_value = jnp.dot(normed_two_low, up_full, preferred_element_type=jnp.float32)
    sigmoid_gate = jax.nn.sigmoid(gate_value)
    silu_gate = gate_value * sigmoid_gate
    hidden = (silu_gate * up_value).astype(jnp.bfloat16)
    layer_out = residual + jnp.dot(hidden, down_full, preferred_element_type=jnp.float32)
    grad_out = cotangent[0]
    gain_back, gate_back, up_back, down_back = (
        lax.all_gather(ln2_gain, "fsdp", axis=0, tiled=True),
        lax.all_gather(w_gate, "fsdp", axis=0, tiled=True),
        lax.all_gather(w_up, "fsdp", axis=0, tiled=True),
        lax.all_gather(w_down, "fsdp", axis=0, tiled=True),
    )
    grad_hidden = times_transposed(grad_out, down_back)
    grad_down = inner(hidden, grad_out)
    grad_gate = (
        grad_hidden * up_value * sigmoid_gate * (1.0 + gate_value * (1.0 - sigmoid_gate))
    ).astype(jnp.bfloat16)
    grad_up = (grad_hidden * silu_gate).astype(jnp.bfloat16)
    grad_gate_w = inner(normed_two_low, grad_gate)
    grad_up_w = inner(normed_two_low, grad_up)
    grad_normed_two = times_transposed(grad_gate, gate_back) + times_transposed(grad_up, up_back)
    grad_gain_two = jnp.sum(grad_normed_two * unit_two, 0)
    grad_shift_two = jnp.sum(grad_normed_two, 0)
    grad_residual = grad_out.astype(jnp.float32) + norm_back(
        grad_normed_two, unit_two, inverse_two, gain_back.astype(jnp.float32)
    )
    down_part = lax.psum_scatter(
        grad_down.astype(jnp.bfloat16), "fsdp", scatter_dimension=0, tiled=True
    )
    gate_part, up_part, gain_two_part, shift_two_part = (
        lax.psum_scatter(
            grad_gate_w.astype(jnp.bfloat16), "fsdp", scatter_dimension=0, tiled=True
        ).astype(jnp.float32),
        lax.psum_scatter(
            grad_up_w.astype(jnp.bfloat16), "fsdp", scatter_dimension=0, tiled=True
        ).astype(jnp.float32),
        lax.psum_scatter(
            grad_gain_two.astype(jnp.bfloat16), "fsdp", scatter_dimension=0, tiled=True
        ).astype(jnp.float32),
        lax.psum_scatter(
            grad_shift_two.astype(jnp.bfloat16), "fsdp", scatter_dimension=0, tiled=True
        ).astype(jnp.float32),
    )
    grad_branch = grad_residual.astype(jnp.bfloat16)
    gain_one_back, qkv_back, out_back = (
        lax.all_gather(ln1_gain, "fsdp", axis=0, tiled=True),
        lax.all_gather(w_qkv, "fsdp", axis=0, tiled=True),
        lax.all_gather(w_out, "fsdp", axis=0, tiled=True),
    )
    grad_out_w = inner(mixed_heads, grad_branch)
    grad_mixed = (
        times_transposed(grad_branch, out_back)
        .astype(jnp.bfloat16)
        .reshape(rows_here, head_count, HEAD)
    )
    row_delta = jnp.transpose(jnp.sum(grad_mixed.astype(jnp.float32) * attended, -1))

    def back_block(grad_queries, block_args):
        key_block, value_block, place_block, doc_block = block_args
        scaled, allowed = block_scores(key_block, place_block, doc_block)
        soft_weights = jnp.where(allowed, jnp.exp(scaled - log_total[..., None]), 0.0)
        grad_value = jnp.einsum(
            "hqk,qhd->khd",
            soft_weights.astype(jnp.bfloat16),
            grad_mixed,
            preferred_element_type=jnp.float32,
        )
        grad_soft = jnp.einsum(
            "qhd,khd->hqk", grad_mixed, value_block, preferred_element_type=jnp.float32
        )
        grad_raw = (soft_weights * (grad_soft - row_delta[..., None]) * score_scale).astype(
            jnp.bfloat16
        )
        grad_queries = grad_queries + jnp.einsum(
            "hqk,khd->qhd", grad_raw, key_block, preferred_element_type=jnp.float32
        )
        grad_key = jnp.einsum("hqk,qhd->khd", grad_raw, queries, preferred_element_type=jnp.float32)
        return (
            grad_queries,
            (
                grad_key.reshape(block_rows, model_width),
                grad_value.reshape(block_rows, model_width),
            ),
        )

    grad_queries, key_value_grads = lax.scan(
        back_block,
        jnp.zeros((rows_here, head_count, HEAD), jnp.float32),
        (key_blocks, value_blocks, place_blocks, doc_blocks),
    )
    grad_key_rows, grad_value_rows = (
        lax.psum_scatter(
            key_value_grads[0].reshape(seq_rows, model_width).astype(jnp.bfloat16),
            "ctx",
            scatter_dimension=0,
            tiled=True,
        ).astype(jnp.float32),
        lax.psum_scatter(
            key_value_grads[1].reshape(seq_rows, model_width).astype(jnp.bfloat16),
            "ctx",
            scatter_dimension=0,
            tiled=True,
        ).astype(jnp.float32),
    )
    grad_projected = (
        jnp.stack(
            [
                rotate(grad_queries, angles, -1.0),
                rotate(grad_key_rows.reshape(rows_here, head_count, HEAD), angles, -1.0),
                grad_value_rows.reshape(rows_here, head_count, HEAD),
            ],
            1,
        )
        .reshape(rows_here, 3 * model_width)
        .astype(jnp.bfloat16)
    )
    grad_bias_qkv = jnp.sum(grad_projected.astype(jnp.float32), 0)
    grad_qkv_w = inner(normed_low, grad_projected)
    grad_normed = times_transposed(grad_projected, qkv_back)
    grad_gain_one = jnp.sum(grad_normed * unit_one, 0)
    grad_shift_one = jnp.sum(grad_normed, 0)
    grad_tokens = grad_residual + norm_back(
        grad_normed, unit_one, inverse_one, gain_one_back.astype(jnp.float32)
    )
    gain_one_part, shift_one_part, qkv_part, bias_part, out_part = (
        lax.psum_scatter(
            grad_gain_one.astype(jnp.bfloat16), "fsdp", scatter_dimension=0, tiled=True
        ).astype(jnp.float32),
        lax.psum_scatter(
            grad_shift_one.astype(jnp.bfloat16), "fsdp", scatter_dimension=0, tiled=True
        ).astype(jnp.float32),
        lax.psum_scatter(
            grad_qkv_w.astype(jnp.bfloat16), "fsdp", scatter_dimension=0, tiled=True
        ).astype(jnp.float32),
        lax.psum_scatter(
            grad_bias_qkv.astype(jnp.bfloat16), "fsdp", scatter_dimension=0, tiled=True
        ).astype(jnp.float32),
        lax.psum_scatter(
            grad_out_w.astype(jnp.bfloat16), "fsdp", scatter_dimension=0, tiled=True
        ).astype(jnp.float32),
    )
    finished = (
        lax.psum(gain_one_part.astype(jnp.bfloat16), "ctx").astype(jnp.float32),
        lax.psum(shift_one_part.astype(jnp.bfloat16), "ctx").astype(jnp.float32),
        lax.psum(qkv_part.astype(jnp.bfloat16), "ctx").astype(jnp.float32),
        lax.psum(bias_part.astype(jnp.bfloat16), "ctx").astype(jnp.float32),
        lax.psum(out_part.astype(jnp.bfloat16), "ctx").astype(jnp.float32),
        lax.psum(gain_two_part.astype(jnp.bfloat16), "ctx").astype(jnp.float32),
        lax.psum(shift_two_part.astype(jnp.bfloat16), "ctx").astype(jnp.float32),
        lax.psum(gate_part.astype(jnp.bfloat16), "ctx").astype(jnp.float32),
        lax.psum(up_part.astype(jnp.bfloat16), "ctx").astype(jnp.float32),
        lax.psum(down_part, "ctx").astype(jnp.float32),
    )
    return (
        layer_out.astype(jnp.bfloat16)[None],
        grad_tokens[None],
        finished[0],
        finished[1],
        finished[2],
        finished[3],
        finished[4],
        finished[5],
        finished[6],
        finished[7],
        finished[8],
        finished[9],
    )


def solution(mesh):
    placed = (
        P("fsdp", "ctx", None),
        P("fsdp", None),
        P(),
        P("fsdp"),
        P("fsdp"),
        P("fsdp", None),
        P("fsdp"),
        P("fsdp", None),
        P("fsdp"),
        P("fsdp"),
        P("fsdp", None),
        P("fsdp", None),
        P("fsdp", None),
        P("fsdp", "ctx", None),
    )
    return jax.shard_map(
        body,
        mesh=mesh,
        in_specs=placed,
        out_specs=(
            P("fsdp", "ctx", None),
            P("fsdp", "ctx", None),
            P("fsdp"),
            P("fsdp"),
            P("fsdp", None),
            P("fsdp"),
            P("fsdp", None),
            P("fsdp"),
            P("fsdp"),
            P("fsdp", None),
            P("fsdp", None),
            P("fsdp", None),
        ),
        check_vma=False,
    )
```

profile of v0, /device:TPU:0, one launch (start us, length us, event | category | flops | bytes accessed | tf_op | source)
XLA Modules:
  0.0 4418.8 jit_solution(10883677757403402559)
XLA Ops:
  8.0 14.8 all-gather.2
  34.9 35.9 all-gather
  71.5 366.3 %all-gather.13.cloned.1.call-done = bf16[2048,6144]{1,0:T(8,128)(2,1)} async-done(((bf16[512,6144]{1,0:T(8,128)(2,1)}), bf16[2048,6144]{1,0:T(8,128)(2,1)}) %all-gather.13.cloned.1.call-update) | async-done | bytes 25165840 | tf_op jit(solution)/shard_map/all_gather | solution.py:106
  514.9 14.6 reshape.536
  538.3 35.0 all-gather.17.cloned.1.call-done
  573.3 14.8 reshape.537
  596.9 73.7 %while.39 = (s32[]{:T(128)}, f32[32,256]{1,0:T(8,128)S(1)}, f32[32,256]{1,0:T(8,128)S(1)}, s32[256]{0:T(256)S(1)}, s32[4,512]{1,0:T(4,128)S(1)}, /*index=5*/s32[...) while((s32[]{:T(128)}, f32[32,256]{1,0:T(8,128)S(1)}, ...), condition=%wide.region_6.7_spmd.clone, body=%wide.region_3.6_spmd.clone.sunk | while | flops 570859520 | bytes 37533828 | solution.py:150
  670.7 31.5 while.40
  703.4 21.0 all-gather.19.cloned.1.call-done
  732.6 382.6 %all-gather.21.cloned.1.call-done = bf16[2048,5632]{1,0:T(8,128)(2,1)} async-done(((bf16[512,5632]{1,0:T(8,128)(2,1)}), bf16[2048,5632]{1,0:T(8,128)(2,1)}) %all-gather.21.cloned.1.call-update) | async-done | bytes 23068688 | tf_op jit(solution)/shard_map/all_gather | solution.py:177
  1129.1 377.0 %all-gather.23.cloned.1.call-done = bf16[2048,5632]{1,0:T(8,128)(2,1)} async-done(((bf16[512,5632]{1,0:T(8,128)(2,1)}), bf16[2048,5632]{1,0:T(8,128)(2,1)}) %all-gather.23.cloned.1.call-update) | async-done | bytes 23068688 | tf_op jit(solution)/shard_map/all_gather | solution.py:178
  1520.3 376.8 %all-gather.25.cloned.1.call-done = bf16[5632,2048]{1,0:T(8,128)(2,1)} async-done(((bf16[1408,2048]{1,0:T(8,128)(2,1)}), bf16[5632,2048]{1,0:T(8,128)(2,1)}) %all-gather.25.cloned.1.call-update) | async-done | bytes 23068688 | tf_op jit(solution)/shard_map/all_gather | solution.py:179
  1897.1 18.4 multiply_convert_fusion
  1956.8 237.2 %while.41 = (s32[]{:T(128)}, f32[256,32,64]{0,2,1:T(8,128)}, bf16[4,512,2048]{2,1,0:T(8,128)(2,1)}, bf16[4,512,2048]{2,1,0:T(8,128)(2,1)}, bf16[4,512,32,64]{1,3...) while((s32[]{:T(128)}, f32[256,32,64]{0,2,1:T(8,128)}, ...), condition=%wide.region_15.16_spmd.clone, body=%wide.region_14.15_spmd.clone.sunk | while | flops 2731933696 | bytes 115849432 | solution.py:271
  2246.3 17.4 reduce-scatter.8.cloned.1.call-done
  2266.4 72.5 %reduce-scatter.10.cloned.1.call-done = bf16[256,2048]{1,0:T(8,128)(2,1)} async-done(((bf16[2048,2048]{1,0:T(8,128)(2,1)}), bf16[256,2048]{1,0:T(8,128)(2,1)}) %reduce-scatter.10.cloned.1.call-update) | async-done | bytes 1048592 | tf_op jit(solution)/shard_map/reduce_scatter | solution.py:283
  2346.1 14.3 convolution_convert_fusion.3
  2360.5 125.7 %reduce-scatter.14.cloned.1.call-done = bf16[512,2048]{1,0:T(8,128)(2,1)} async-done(((bf16[2048,2048]{1,0:T(8,128)(2,1)}), bf16[512,2048]{1,0:T(8,128)(2,1)}) %reduce-scatter.14.cloned.1.call-update) | async-done | bytes 2097168 | tf_op jit(solution)/shard_map/reduce_scatter | solution.py:323
  2486.2 383.8 %reduce-scatter.16.cloned.1.call-done = bf16[512,5632]{1,0:T(8,128)(2,1)} async-done(((bf16[2048,5632]{1,0:T(8,128)(2,1)}), bf16[512,5632]{1,0:T(8,128)(2,1)}) %reduce-scatter.16.cloned.1.call-update) | async-done | bytes 5767184 | tf_op jit(solution)/shard_map/reduce_scatter | solution.py:216
  2869.9 384.8 %reduce-scatter.18.cloned.1.call-done = bf16[512,5632]{1,0:T(8,128)(2,1)} async-done(((bf16[2048,5632]{1,0:T(8,128)(2,1)}), bf16[512,5632]{1,0:T(8,128)(2,1)}) %reduce-scatter.18.cloned.1.call-update) | async-done | bytes 5767184 | tf_op jit(solution)/shard_map/reduce_scatter | solution.py:219
  3254.7 384.8 %reduce-scatter.20.cloned.1.call-done = bf16[1408,2048]{1,0:T(8,128)(2,1)} async-done(((bf16[5632,2048]{1,0:T(8,128)(2,1)}), bf16[1408,2048]{1,0:T(8,128)(2,1)}) %reduce-scatter.20.cloned.1.call-update) | async-done | bytes 5767184 | tf_op jit(solution)/shard_map/reduce_scatter | solution.py:212
  3639.5 418.5 %reduce-scatter.12.cloned.1.call-done = bf16[512,6144]{1,0:T(8,128)(2,1)} async-done(((bf16[2048,6144]{1,0:T(8,128)(2,1)}), bf16[512,6144]{1,0:T(8,128)(2,1)}) %reduce-scatter.12.cloned.1.call-update) | async-done | bytes 6291472 | tf_op jit(solution)/shard_map/reduce_scatter | solution.py:317
  4087.3 20.0 all-reduce.7
  4127.8 252.8 %all-reduce.10.cloned.1.call-done = (bf16[512,6144]{1,0:T(8,128)(2,1)}, bf16[512,2048]{1,0:T(8,128)(2,1)}, bf16[512,5632]{1,0:T(8,128)(2,1)}, bf16[512,5632]{1,0:T(8,128)(2,1)}, bf16[1408,2048]{1,0:T(8,128)(2,1)}) async-done(((bf16[512,6144]{1,0:T(8,128)(2,1)}, bf16[512,2048]{1,0:T(8,128)(2,1)}, bf16[512,5632]{1,0:T(8,128)(2,1)}, bf16[512,5632]{1,0:T(8,128)(2,1)}, bf16[1408,2048]{1,0:T(8,128)(2,1)}), ...) | async-done | bytes 25690128 | tf_op jit(solution)/shard_map/psum | solution.py:330
  (307 shorter events, 669.2 us)
Async XLA Ops:
  7.2 462.2 %copy-start = (s32[1,2048]{1,0:T(1,128)S(1)}, s32[1,2048]{1,0:T(1,128)}, u32[]{:S(2)}) copy-start(s32[1,2048]{1,0:T(1,128)} %param.21) | copy-start | bytes 24580
  7.2 63.6 %copy-start.4 = (bf16[1,256,2048]{2,1,0:T(8,128)(2,1)S(1)}, bf16[1,256,2048]{2,1,0:T(8,128)(2,1)}, u32[]{:S(2)}) copy-start(bf16[1,256,2048]{2,1,0:T(8,128)(2,1)} %param.20) | copy-start | bytes 3145732
  7.2 430.5 %all-gather.13.cloned.1.call-start = ((), (), s32[]{:S(2)}) async-start(), calls=%async_computation.7 | async-start | bytes 31457280 | tf_op jit(solution)/shard_map/all_gather | solution.py:106
  8.0 506.9 %all-gather.15.cloned.1.call-start = ((), (), s32[]{:S(2)}) async-start(), calls=%async_computation.8 | async-start | bytes 9437184 | tf_op jit(solution)/shard_map/all_gather | solution.py:125
  34.9 416.3 %copy-start.21 = (f32[4,1,512]{2,1,0:T(1,128)}, f32[4,1,512]{2,1,0:T(1,128)S(1)}, u32[]{:S(2)}) copy-start(f32[4,1,512]{2,1,0:T(1,128)S(1)} %convert_element_type.243) | copy-start | bytes 24580
  70.8 380.4 %copy-start.19 = (f32[4,1,512]{2,1,0:T(1,128)}, f32[4,1,512]{2,1,0:T(1,128)S(1)}, u32[]{:S(2)}) copy-start(f32[4,1,512]{2,1,0:T(1,128)S(1)} %convert_element_type.242) | copy-start | bytes 24580
  71.0 380.2 %copy-start.25 = (f32[256]{0:T(256)}, f32[256]{0:T(256)S(1)}, u32[]{:S(2)}) copy-start(f32[256]{0:T(256)S(1)} %broadcast_multiply_fusion.6) | copy-start | bytes 3076
  71.5 379.8 %copy-start.27 = (f32[256]{0:T(256)}, f32[256]{0:T(256)S(1)}, u32[]{:S(2)}) copy-start(f32[256]{0:T(256)S(1)} %add_rsqrt_fusion.1) | copy-start | bytes 3076
  460.6 112.8 %all-gather.17.cloned.1.call-start = ((), (), s32[]{:S(2)}) async-start(), calls=%async_computation.9 | async-start | bytes 9437184 | tf_op jit(solution)/shard_map/all_gather | solution.py:124
  466.7 257.7 %all-gather.19.cloned.1.call-start = ((), (), s32[]{:S(2)}) async-start(), calls=%async_computation.10 | async-start | bytes 10485760 | tf_op jit(solution)/shard_map/all_gather | solution.py:108
  467.3 647.9 %all-gather.21.cloned.1.call-start = ((), (), s32[]{:S(2)}) async-start(), calls=%async_computation.11 | async-start | bytes 28835840 | tf_op jit(solution)/shard_map/all_gather | solution.py:177
  467.9 1038.2 %all-gather.23.cloned.1.call-start = ((), (), s32[]{:S(2)}) async-start(), calls=%async_computation.12 | async-start | bytes 28835840 | tf_op jit(solution)/shard_map/all_gather | solution.py:178
  468.4 1428.7 %all-gather.25.cloned.1.call-start = ((), (), s32[]{:S(2)}) async-start(), calls=%async_computation.13 | async-start | bytes 28835840 | tf_op jit(solution)/shard_map/all_gather | solution.py:179
  469.2 1794.5 %reduce-scatter.8.cloned.1.call-start = ((), (), s32[]{:S(2)}) async-start(), calls=%async_computation.14 | async-start | bytes 9437184 | tf_op jit(solution)/shard_map/reduce_scatter | solution.py:277
  730.8 1211.1 %copy-start.2 = (f32[256,2048]{1,0:T(8,128)}, f32[256,2048]{1,0:T(8,128)S(1)}, u32[]{:S(2)}) copy-start(f32[256,2048]{1,0:T(8,128)S(1)} %get-tuple-element.547) | copy-start | bytes 6291460
  2194.0 144.9 %reduce-scatter.10.cloned.1.call-start = ((), (), s32[]{:S(2)}) async-start(), calls=%async_computation.15 | async-start | bytes 9437184 | tf_op jit(solution)/shard_map/reduce_scatter | solution.py:283
  2194.8 291.4 %reduce-scatter.14.cloned.1.call-start = ((), (), s32[]{:S(2)}) async-start(), calls=%async_computation.17 | async-start | bytes 10485760 | tf_op jit(solution)/shard_map/reduce_scatter | solution.py:323
  2202.4 667.5 %reduce-scatter.16.cloned.1.call-start = ((), (), s32[]{:S(2)}) async-start(), calls=%async_computation.18 | async-start | bytes 28835840 | tf_op jit(solution)/shard_map/reduce_scatter | solution.py:216
  2217.0 1037.7 %reduce-scatter.18.cloned.1.call-start = ((), (), s32[]{:S(2)}) async-start(), calls=%async_computation.19 | async-start | bytes 28835840 | tf_op jit(solution)/shard_map/reduce_scatter | solution.py:219
  2230.6 1408.9 %reduce-scatter.20.cloned.1.call-start = ((), (), s32[]{:S(2)}) async-start(), calls=%async_computation.20 | async-start | bytes 28835840 | tf_op jit(solution)/shard_map/reduce_scatter | solution.py:212
  2244.7 1813.3 %reduce-scatter.12.cloned.1.call-start = ((), (), s32[]{:S(2)}) async-start(), calls=%async_computation.16 | async-start | bytes 31457280 | tf_op jit(solution)/shard_map/reduce_scatter | solution.py:317
  2246.3 94.9 %copy-start.24 = (f32[256,8]{0,1:T(8,128)S(1)}, f32[256,8]{0,1:T(8,128)}, u32[]{:S(2)}) copy-start(f32[256,8]{0,1:T(8,128)} %copy-done.23) | copy-start | bytes 24580
  2246.3 94.9 %copy-start.29 = (f32[256,8]{0,1:T(8,128)S(1)}, f32[256,8]{0,1:T(8,128)}, u32[]{:S(2)}) copy-start(f32[256,8]{0,1:T(8,128)} %get-tuple-element.543) | copy-start | bytes 24580
  2360.4 2020.2 %all-reduce.10.cloned.1.call-start = ((), (), s32[]{:S(2)}) async-start(), calls=%async_computation.21 | async-start | bytes 51380224 | tf_op jit(solution)/shard_map/psum | solution.py:330
  (37 other events, 309.3 us)
Sparse Core Ops, SparseCore 0:
  9.7 428.0 all-gather.12
  460.7 54.1 all-gather.14
  517.3 55.9 all-gather.16
  574.7 149.6 all-gather.18
  725.8 389.3 all-gather.20
  1116.6 389.3 all-gather.22
  1507.6 389.4 all-gather.24
  2194.1 69.5 reduce-scatter.7
  2267.6 71.2 reduce-scatter.9
  2341.7 144.4 reduce-scatter.13
  2488.5 381.3 reduce-scatter.15
  2872.3 382.3 reduce-scatter.17
  3257.1 382.3 reduce-scatter.19
  3641.9 416.1 reduce-scatter.11
  4062.6 317.9 all-reduce.9
where the time goes:
time: 4430 us; the launch traced here: 4420 us
  waiting for transfers between devices  3610 us (81%)
  matrix products  447 us (10%)
  local copies, waits for them, and re-layouts  136 us (3%)
  blocking collectives  120 us (3%)
  other arithmetic  86.8 us (2%)
    reduce_scatter x1, waiting for transfers between devices, body(): lax.psum_scatter(grad_qkv_w.astype(jnp.bfloat16), 'fsdp', scatter_dimensi...  419 us
    reduce_scatter x1, waiting for transfers between devices, body(): lax.psum_scatter(grad_up_w.astype(jnp.bfloat16), 'fsdp', scatter_dimensio...  385 us
    reduce_scatter x1, waiting for transfers between devices, body(): lax.psum_scatter(grad_down.astype(jnp.bfloat16), 'fsdp', scatter_dimensio...  385 us
    reduce_scatter x1, waiting for transfers between devices, body(): lax.psum_scatter(grad_gate_w.astype(jnp.bfloat16), 'fsdp', scatter_dimens...  384 us
    all_gather x1, waiting for transfers between devices, body(): lax.all_gather(w_gate, 'fsdp', axis=0, tiled=True)  383 us
    all_gather x1, waiting for transfers between devices, body(): lax.all_gather(w_up, 'fsdp', axis=0, tiled=True)  377 us
    all_gather x1, waiting for transfers between devices, body(): lax.all_gather(w_down, 'fsdp', axis=0, tiled=True)  377 us
    all_gather x1, waiting for transfers between devices, body(): lax.all_gather(w_qkv, 'fsdp', axis=0, tiled=True)  366 us
  transfers between devices with their start and end apart: 15, of which 15 were waited for; matrix products, arithmetic and copies ran while one was open for 7% of the time, Pallas kernels for 0%

commit v1 on v0

v1 whole, which is shorter than its diff:
```python
import jax
import jax.numpy as jnp
from jax import lax
from jax.sharding import PartitionSpec as P

HEAD = 64
ROT = 16


NORM_EPSILON = 1e-05
ROTARY_BASE = 10000.0
MASKED_SCORE = -1e30


def norm_rows(values, gain_row, shift_row):
    centered = values - jnp.mean(values, -1, keepdims=True)
    inverse = lax.rsqrt(jnp.mean(centered * centered, -1, keepdims=True) + NORM_EPSILON)
    unit_rows = centered * inverse
    return (unit_rows * gain_row + shift_row, unit_rows, inverse)


def norm_back(grad_rows, unit_rows, inverse, gain_row):
    scaled = grad_rows * gain_row
    return inverse * (
        scaled
        - jnp.mean(scaled, -1, keepdims=True)
        - unit_rows * jnp.mean(scaled * unit_rows, -1, keepdims=True)
    )


def row_places(row_ids, block_pairs, rows_here, axis_size):
    half_rows = rows_here // 2
    owners = row_ids // rows_here
    second = row_ids // half_rows % 2
    matches = owners[:, None] == jnp.arange(axis_size, dtype=jnp.int32)[None, :]
    first_block = jnp.sum(jnp.where(matches, block_pairs[None, :], 0), 1)
    blocks = jnp.where(second == 0, first_block, 2 * axis_size - 1 - first_block)
    return blocks * half_rows + row_ids % half_rows


def rotate(heads_in, angles, turn_sign):
    half_rot = ROT // 2
    cosine = jnp.cos(angles)[:, None, :]
    sine_row = turn_sign * jnp.sin(angles)[:, None, :]
    front_half = heads_in[..., :half_rot]
    behind = heads_in[..., half_rot:ROT]
    return jnp.concatenate(
        [
            front_half * cosine - behind * sine_row,
            behind * cosine + front_half * sine_row,
            heads_in[..., ROT:],
        ],
        -1,
    )


def inner(left_side, right_side):
    return lax.dot_general(
        left_side, right_side, (((0,), (0,)), ((), ())), preferred_element_type=jnp.float32
    )


def times_transposed(left_side, right_side):
    return lax.dot_general(
        left_side, right_side, (((1,), (1,)), ((), ())), preferred_element_type=jnp.float32
    )


def times(left_side, right_side):
    return jnp.dot(left_side, right_side, preferred_element_type=jnp.float32)


def attend(queries, keys, values, allowed):
    score_scale = HEAD ** (-0.5)

    def one_head(args):
        query, key, value = args
        scores = jnp.where(allowed, times_transposed(query, key) * score_scale, MASKED_SCORE)
        row_max = jnp.max(scores, -1, keepdims=True)
        exps = jnp.where(allowed, jnp.exp(scores - row_max), 0.0)
        total = jnp.sum(exps, -1, keepdims=True)
        weights = (exps / total).astype(jnp.bfloat16)
        return times(weights, value), row_max + jnp.log(total)

    return lax.map(one_head, (queries, keys, values))


def attend_back(queries, keys, values, grad_mixed, log_total, delta, allowed):
    score_scale = HEAD ** (-0.5)

    def one_head(args):
        query, key, value, grad, total, row_delta = args
        scores = times_transposed(query, key) * score_scale
        weights = jnp.where(allowed, jnp.exp(scores - total), 0.0)
        grad_value = inner(weights.astype(jnp.bfloat16), grad)
        grad_soft = times_transposed(grad, value)
        grad_raw = (weights * (grad_soft - row_delta) * score_scale).astype(jnp.bfloat16)
        return times(grad_raw, key), inner(grad_raw, query), grad_value

    return lax.map(one_head, (queries, keys, values, grad_mixed, log_total, delta))


def body(
    tokens,
    doc_ids,
    block_pairs,
    ln1_gain,
    ln1_bias,
    w_qkv,
    b_qkv,
    w_out,
    ln2_gain,
    ln2_bias,
    w_gate,
    w_up,
    w_down,
    cotangent,
):
    rows_here = tokens.shape[1]
    width = tokens.shape[2]
    head_count = width // HEAD
    ctx_size = lax.axis_size("ctx")
    fsdp_size = lax.axis_size("fsdp")
    seq_rows = rows_here * ctx_size
    position = lax.axis_index("ctx")
    part = lax.axis_index("fsdp")
    heads_here = head_count // ctx_size
    cols = width // ctx_size
    shard_rows = w_qkv.shape[0]
    hidden_shard = w_down.shape[0]
    strip = hidden_shard // ctx_size

    key_places = row_places(jnp.arange(seq_rows, dtype=jnp.int32), block_pairs, rows_here, ctx_size)
    key_docs = jnp.take(doc_ids[0], key_places)
    allowed = (key_places[:, None] >= key_places[None, :]) & (key_docs[:, None] == key_docs[None, :])
    inverse_freq = ROTARY_BASE ** (-jnp.arange(ROT // 2, dtype=jnp.float32) * 2.0 / ROT)
    angles = key_places.astype(jnp.float32)[:, None] * inverse_freq[None, :]

    small = lax.all_gather(
        jnp.concatenate([ln1_gain, ln1_bias, ln2_gain, ln2_bias, b_qkv]), "fsdp", axis=0
    ).astype(jnp.float32)
    gain_one, shift_one, gain_two, shift_two = (
        small[:, i * shard_rows : (i + 1) * shard_rows].reshape(1, width) for i in range(4)
    )
    bias_full = small[:, 4 * shard_rows :].reshape(3, ctx_size, cols)
    bias_here = lax.dynamic_index_in_dim(bias_full, position, 1, keepdims=False).reshape(3 * cols)

    qkv_strip = lax.dynamic_index_in_dim(
        w_qkv.reshape(shard_rows, 3, ctx_size, cols), position, 2, keepdims=False
    ).reshape(shard_rows, 3 * cols)
    gate_strip, up_strip = (
        lax.dynamic_index_in_dim(
            w.reshape(shard_rows, fsdp_size, ctx_size, strip), position, 2, keepdims=False
        ).reshape(shard_rows, fsdp_size * strip)
        for w in (w_gate, w_up)
    )
    down_strip = lax.dynamic_slice_in_dim(w_down, position * strip, strip, 0)
    out_piece = shard_rows // ctx_size
    out_strip = lax.dynamic_slice_in_dim(w_out, position * out_piece, out_piece, 0)

    tokens_in = tokens[0].astype(jnp.float32)
    normed, unit_one, inverse_one = norm_rows(tokens_in, gain_one, shift_one)
    normed_all = lax.all_gather(normed.astype(jnp.bfloat16), "ctx", axis=0, tiled=True)
    qkv_here = lax.all_gather(qkv_strip, "fsdp", axis=0, tiled=True)
    projected = times(normed_all, qkv_here) + bias_here
    split_heads = projected.reshape(seq_rows, 3, heads_here, HEAD)
    queries, keys, values = (
        jnp.transpose(rows.astype(jnp.bfloat16), (1, 0, 2))
        for rows in (
            rotate(split_heads[:, 0], angles, 1.0),
            rotate(split_heads[:, 1], angles, 1.0),
            split_heads[:, 2],
        )
    )
    attended, log_total = attend(queries, keys, values, allowed)
    mixed_here = (
        jnp.transpose(attended, (1, 0, 2)).reshape(seq_rows, cols).astype(jnp.bfloat16)
    )
    mixed_rows = lax.all_to_all(mixed_here, "ctx", split_axis=0, concat_axis=1, tiled=True)
    out_full = lax.all_gather(out_strip, ("fsdp", "ctx"), axis=0, tiled=True)
    residual = tokens_in + times(mixed_rows, out_full)
    normed_two, unit_two, inverse_two = norm_rows(residual, gain_two, shift_two)
    normed_two_all = lax.all_gather(normed_two.astype(jnp.bfloat16), "ctx", axis=0, tiled=True)
    gate_here = lax.all_gather(gate_strip, "fsdp", axis=0, tiled=True)
    up_here = lax.all_gather(up_strip, "fsdp", axis=0, tiled=True)
    down_here = lax.all_gather(down_strip, "fsdp", axis=0, tiled=True)
    gate_value = times(normed_two_all, gate_here)
    up_value = times(normed_two_all, up_here)
    sigmoid_gate = jax.nn.sigmoid(gate_value)
    silu_gate = gate_value * sigmoid_gate
    hidden = (silu_gate * up_value).astype(jnp.bfloat16)
    layer_out = residual + lax.psum_scatter(
        times(hidden, down_here).astype(jnp.bfloat16), "ctx", scatter_dimension=0, tiled=True
    ).astype(jnp.float32)

    grad_out = cotangent[0]
    grad_out_all = lax.all_gather(grad_out, "ctx", axis=0, tiled=True)
    grad_hidden = times_transposed(grad_out_all, down_here)
    grad_gate = (
        grad_hidden * up_value * sigmoid_gate * (1.0 + gate_value * (1.0 - sigmoid_gate))
    ).astype(jnp.bfloat16)
    grad_up = (grad_hidden * silu_gate).astype(jnp.bfloat16)
    grad_normed_two = lax.psum_scatter(
        (times_transposed(grad_gate, gate_here) + times_transposed(grad_up, up_here)).astype(
            jnp.bfloat16
        ),
        "ctx",
        scatter_dimension=0,
        tiled=True,
    ).astype(jnp.float32)
    grad_residual = grad_out.astype(jnp.float32) + norm_back(
        grad_normed_two, unit_two, inverse_two, gain_two
    )
    grad_branch = grad_residual.astype(jnp.bfloat16)
    grad_mixed_rows = times_transposed(grad_branch, out_full).astype(jnp.bfloat16)
    grad_mixed = lax.all_to_all(grad_mixed_rows, "ctx", split_axis=1, concat_axis=0, tiled=True)
    grad_mixed = jnp.transpose(grad_mixed.reshape(seq_rows, heads_here, HEAD), (1, 0, 2))
    delta = jnp.sum(grad_mixed.astype(jnp.float32) * attended, -1, keepdims=True)
    grad_queries, grad_keys, grad_values = (
        jnp.transpose(grad, (1, 0, 2))
        for grad in attend_back(queries, keys, values, grad_mixed, log_total, delta, allowed)
    )
    grad_projected = (
        jnp.stack(
            [rotate(grad_queries, angles, -1.0), rotate(grad_keys, angles, -1.0), grad_values], 1
        )
        .reshape(seq_rows, 3 * cols)
        .astype(jnp.bfloat16)
    )
    grad_normed = lax.psum_scatter(
        times_transposed(grad_projected, qkv_here).astype(jnp.bfloat16),
        "ctx",
        scatter_dimension=0,
        tiled=True,
    ).astype(jnp.float32)
    grad_tokens = grad_residual + norm_back(grad_normed, unit_one, inverse_one, gain_one)

    def reduced(grad, axes):
        return lax.psum_scatter(
            grad.astype(jnp.bfloat16), axes, scatter_dimension=0, tiled=True
        )

    def spread(piece):
        return lax.all_gather(piece, "ctx", axis=0)

    grad_down_w = spread(reduced(inner(hidden, grad_out_all), "fsdp"))
    grad_gate_w = spread(reduced(inner(normed_two_all, grad_gate), "fsdp"))
    grad_up_w = spread(reduced(inner(normed_two_all, grad_up), "fsdp"))
    grad_out_w = spread(reduced(inner(mixed_rows, grad_branch), ("fsdp", "ctx")))
    grad_qkv_w = spread(reduced(inner(normed_all, grad_projected), "fsdp"))

    grad_bias = jnp.sum(grad_projected.astype(jnp.float32), 0).reshape(3, 1, cols)
    grad_bias = lax.dynamic_update_slice(
        jnp.zeros((3, ctx_size, cols), jnp.float32), grad_bias, (0, position, 0)
    )
    sums = jnp.concatenate(
        [
            jnp.sum(grad_normed * unit_one, 0),
            jnp.sum(grad_normed, 0),
            jnp.sum(grad_normed_two * unit_two, 0),
            jnp.sum(grad_normed_two, 0),
            grad_bias.reshape(3 * width),
        ]
    )
    sums = lax.psum(sums, ("fsdp", "ctx"))
    norm_sums = lax.dynamic_slice_in_dim(
        sums[: 4 * width].reshape(4, width), part * shard_rows, shard_rows, 1
    )
    bias_sums = lax.dynamic_slice_in_dim(
        sums[4 * width :], part * b_qkv.shape[0], b_qkv.shape[0], 0
    )
    float32 = jnp.float32
    return (
        layer_out.astype(jnp.bfloat16)[None],
        grad_tokens[None],
        norm_sums[0],
        norm_sums[1],
        jnp.transpose(grad_qkv_w.reshape(ctx_size, shard_rows, 3, cols), (1, 2, 0, 3))
        .reshape(w_qkv.shape)
        .astype(float32),
        bias_sums,
        grad_out_w.reshape(w_out.shape).astype(float32),
        norm_sums[2],
        norm_sums[3],
        jnp.transpose(grad_gate_w.reshape(ctx_size, shard_rows, fsdp_size, strip), (1, 2, 0, 3))
        .reshape(w_gate.shape)
        .astype(float32),
        jnp.transpose(grad_up_w.reshape(ctx_size, shard_rows, fsdp_size, strip), (1, 2, 0, 3))
        .reshape(w_up.shape)
        .astype(float32),
        grad_down_w.reshape(w_down.shape).astype(float32),
    )


def solution(mesh):
    placed = (
        P("fsdp", "ctx", None),
        P("fsdp", None),
        P(),
        P("fsdp"),
        P("fsdp"),
        P("fsdp", None),
        P("fsdp"),
        P("fsdp", None),
        P("fsdp"),
        P("fsdp"),
        P("fsdp", None),
        P("fsdp", None),
        P("fsdp", None),
        P("fsdp", "ctx", None),
    )
    return jax.shard_map(
        body,
        mesh=mesh,
        in_specs=placed,
        out_specs=(
            P("fsdp", "ctx", None),
            P("fsdp", "ctx", None),
            P("fsdp"),
            P("fsdp"),
            P("fsdp", None),
            P("fsdp"),
            P("fsdp", None),
            P("fsdp"),
            P("fsdp"),
            P("fsdp", None),
            P("fsdp", None),
            P("fsdp", None),
        ),
        check_vma=False,
    )
```

time: 4430 us -> 1450 us (0.33)
  waiting for transfers between devices: 3610 us -> 686 us
  local copies, waits for them, and re-layouts: 136 us -> 240 us
  matrix products: 447 us -> 347 us
  blocking collectives: 120 us -> 55.2 us
    reduce_scatter x7 -> x8, waiting for transfers between devices: 1790 us -> 342 us  [the longest x5 191 us: reduced(): lax.psum_scatter(grad.astype(jnp.bfloat16), axes, scatter_dimension=0, ti...]
    all_gather x7 -> x13, waiting for transfers between devices: 1570 us -> 322 us  [the longest x1 55.6 us: body(): lax.all_gather(normed.astype(jnp.bfloat16), 'ctx', axis=0, tiled=True)]
    psum x1 -> x0, waiting for transfers between devices: 253 us -> none  [body(): lax.psum(qkv_part.astype(jnp.bfloat16), 'ctx').astype(jnp.float32)]
    dot_general x33 -> x13, matrix products: 321 us -> 98.4 us  [times(): return jnp.dot(left_side, right_side, preferred_element_type=jnp.float32)]
    unnamed x97 -> x119, local copies, waits for them, and re-layouts: 27.6 us -> 142 us
    dot_general x5 -> x17, matrix products: 65.8 us -> 155 us  [times_transposed(): lax.dot_general(left_side, right_side, (((1,), (1,)), ((), ())), preferre...]
    all_gather x5 -> x1, blocking collectives: 86.7 us -> 14.8 us  [body(): lax.all_gather(jnp.concatenate([ln1_gain, ln1_bias, ln2_gain, ln2_bias, b...]
    convert_element_type x1 -> x5, local copies, waits for them, and re-layouts: 2.4 us -> 58 us  [the longest x4 56.8 us: body(): return (layer_out.astype(jnp.bfloat16)[None], grad_tokens[None], norm_sum...]
  transfers between devices with their start and end apart: 15 -> 23, of which waited for: 15 -> 15; matrix products, arithmetic and copies ran while one was open for 7% -> 43% of each run, Pallas kernels for 0% -> 0%
where the time goes in v1:
time: 1450 us; the launch traced here: 1440 us
  waiting for transfers between devices  686 us (47%)
  matrix products  347 us (24%)
  local copies, waits for them, and re-layouts  240 us (17%)
  other arithmetic  86.6 us (6%)
  blocking collectives  55.2 us (4%)
  between operations  15.4 us (1%)
    reduce_scatter x5, waiting for transfers between devices, reduced(): lax.psum_scatter(grad.astype(jnp.bfloat16), axes, scatter_dimension=0, ti...  191 us
    dot_general x17, matrix products, times_transposed(): lax.dot_general(left_side, right_side, (((1,), (1,)), ((), ())), preferre...  155 us
    unnamed x119, local copies, waits for them, and re-layouts  142 us
    dot_general x13, matrix products, times(): return jnp.dot(left_side, right_side, preferred_element_type=jnp.float32)  98.4 us
    dot_general x13, matrix products, inner(): lax.dot_general(left_side, right_side, (((0,), (0,)), ((), ())), preferre...  93.6 us
    reduce_scatter x1, waiting for transfers between devices, body(): lax.psum_scatter(times(hidden, down_here).astype(jnp.bfloat16), 'ctx', sc...  72.8 us
    convert_element_type x4, local copies, waits for them, and re-layouts, body(): return (layer_out.astype(jnp.bfloat16)[None], grad_tokens[None], norm_sum...  56.8 us
    all_gather x1, waiting for transfers between devices, body(): lax.all_gather(normed.astype(jnp.bfloat16), 'ctx', axis=0, tiled=True)  55.6 us
  transfers between devices with their start and end apart: 23, of which 15 were waited for; matrix products, arithmetic and copies ran while one was open for 43% of the time, Pallas kernels for 0%

profile of v1, /device:TPU:0, one launch (start us, length us, event | category | flops | bytes accessed | tf_op | source)
XLA Modules:
  0.0 1439.2 jit_solution(14286941995200336807)
XLA Ops:
  19.2 14.8 %all-gather.7 = bf16[4,1,3584]{2,1,0:T(2,128)(2,1)S(1)} all-gather(bf16[1,1,3584]{2,1,0:T(2,128)(2,1)S(1)} %reshape.504), channel_id=2, replica_groups=mesh['ctx'=8,'fsdp'=4] {'fsdp'}, dimensions={0}, use_global_device_ids=true | all-gather | bytes 35840 | tf_op jit(solution)/shard_map/all_gather | solution.py:139
  61.8 22.9 %all-gather.24.cloned.1.call-done = bf16[2048,768]{0,1:T(8,128)(2,1)} async-done(((bf16[512,768]{0,1:T(8,128)(2,1)}), bf16[2048,768]{0,1:T(8,128)(2,1)}) %all-gather.24.cloned.1.call-update) | async-done | bytes 3145744 | tf_op jit(solution)/shard_map/all_gather | solution.py:164
  84.7 55.6 %all-gather.22.cloned.1.call-done = bf16[2048,2048]{1,0:T(8,128)(2,1)} async-done(((bf16[256,2048]{1,0:T(8,128)(2,1)}), bf16[2048,2048]{1,0:T(8,128)(2,1)}) %all-gather.22.cloned.1.call-update) | async-done | bytes 8388624 | tf_op jit(solution)/shard_map/all_gather | solution.py:163
  160.8 82.6 %while.28 = (s32[]{:T(128)}, f32[4,2048,64]{1,2,0:T(8,128)}, f32[4,2048,1]{1,2,0:T(1,128)}, bf16[4,2048,64]{2,1,0:T(8,128)(2,1)S(1)}, bf16[4,2048,64]{2,1,0:T(8,...) while((s32[]{:T(128)}, f32[4,2048,64]{1,2,0:T(8,128)}, ...), condition=%wide.region_6.7_spmd.clone, body=%wide.region_3.6_spmd.clone.sunk | while | flops 1170208768 | bytes 52595292 | solution.py:85
  251.5 14.8 %all-to-all-done = bf16[8,256,256]{1,2,0:T(8,128)(2,1)S(1)} async-done(((bf16[8,256,256]{1,2,0:T(8,128)(2,1)}), bf16[8,256,256]{1,2,0:T(8,128)(2,1)S(1)}, u32[]{:S(2)}, u32[]{:S(2)}) %all-to-all-start) | async-done | bytes 1048608 | tf_op jit(solution)/shard_map/all_to_all | solution.py:179
  288.7 47.5 %all-gather.28.cloned.1.call-done = bf16[2048,2048]{1,0:T(8,128)(2,1)} async-done(((bf16[256,2048]{1,0:T(8,128)(2,1)}), bf16[2048,2048]{1,0:T(8,128)(2,1)}) %all-gather.28.cloned.1.call-update) | async-done | bytes 8388624 | tf_op jit(solution)/shard_map/all_gather | solution.py:183
  347.3 50.1 %all-gather.30.cloned.1.call-done = bf16[2048,704]{0,1:T(8,128)(2,1)} async-done(((bf16[512,704]{0,1:T(8,128)(2,1)}), bf16[2048,704]{0,1:T(8,128)(2,1)}) %all-gather.30.cloned.1.call-update) | async-done | bytes 2883600 | tf_op jit(solution)/shard_map/all_gather | solution.py:184
  408.4 49.1 %all-gather.34.cloned.1.call-done = bf16[704,2048]{1,0:T(8,128)(2,1)} async-done(((bf16[176,2048]{1,0:T(8,128)(2,1)}), bf16[704,2048]{1,0:T(8,128)(2,1)}) %all-gather.34.cloned.1.call-update) | async-done | bytes 2883600 | tf_op jit(solution)/shard_map/all_gather | solution.py:186
  457.5 55.0 %all-gather.36.cloned.1.call-done = bf16[1,2048,2048]{2,1,0:T(8,128)(2,1)} async-done(((bf16[1,256,2048]{2,1,0:T(8,128)(2,1)}), bf16[1,2048,2048]{2,1,0:T(8,128)(2,1)}) %all-gather.36.cloned.1.call-update) | async-done | bytes 8388624 | tf_op jit(solution)/shard_map/all_gather | solution.py:197
  512.5 15.2 %fusion.61 = (bf16[2048,704]{0,1:T(8,128)(2,1)S(1)}, bf16[2048,704]{0,1:T(8,128)(2,1)S(1)}, bf16[2048,704]{0,1:T(8,128)(2,1)}) fusion(f32[2048,704]{0,1:T(8,128)} %fusion.115, f32[2048,704]{0,1:T(8,128)} %fusion.116, bf16[704,2048]{1,0:T(8,128)(2,1)} %all-gather.34.cloned.1.call-done, bf16[1,2048,2048]{2,1,0:T(8,128)(2,1)} %all-gather.36.cloned.1.call-done), kind=kOutput, calls=%fused_computation.75 | convolution fusion | flops 5927206912 | bytes 31457280 | tf_op jit(solution)/shard_map/dot_general | solution.py:64
  586.7 35.4 %reduce-scatter.11.cloned.1.call-done = bf16[256,2048]{1,0:T(8,128)(2,1)} async-done(((bf16[2048,2048]{1,0:T(8,128)(2,1)}), bf16[256,2048]{1,0:T(8,128)(2,1)}) %reduce-scatter.11.cloned.1.call-update) | async-done | bytes 1048592 | tf_op jit(solution)/shard_map/reduce_scatter | solution.py:203
  624.9 72.8 %reduce-scatter.9.cloned.1.call-done = bf16[256,2048]{1,0:T(8,128)(2,1)} async-done(((bf16[2048,2048]{1,0:T(8,128)(2,1)}), bf16[256,2048]{1,0:T(8,128)(2,1)}) %reduce-scatter.9.cloned.1.call-update) | async-done | bytes 1048592 | tf_op jit(solution)/shard_map/reduce_scatter | solution.py:192
  735.9 146.7 %while.29 = (s32[]{:T(128)}, f32[4,2048,64]{1,2,0:T(8,128)}, f32[4,2048,64]{1,2,0:T(8,128)}, bf16[4,2048,64]{1,2,0:T(8,128)(2,1)S(1)}, bf16[4,2048,64]{2,1,0:T(8...) while((s32[]{:T(128)}, f32[4,2048,64]{1,2,0:T(8,128)}, ...), condition=%wide.region_15.16_spmd.clone, body=%wide.region_14.15_spmd.clone.sunk | while | flops 2755657728 | bytes 84538528 | solution.py:100
  919.9 39.0 %reduce-scatter.15.cloned.1.call-done = bf16[512,768]{1,0:T(8,128)(2,1)} async-done(((bf16[2048,768]{1,0:T(8,128)(2,1)}), bf16[512,768]{1,0:T(8,128)(2,1)}) %reduce-scatter.15.cloned.1.call-update) | async-done | bytes 786448 | tf_op jit(solution)/shard_map/reduce_scatter | solution.py:239
  959.0 151.6 %reduce-scatter.17.cloned.1.call-done = bf16[64,2048]{1,0:T(8,128)(2,1)} async-done(((bf16[2048,2048]{1,0:T(8,128)(2,1)}), bf16[64,2048]{1,0:T(8,128)(2,1)}) %reduce-scatter.17.cloned.1.call-update) | async-done | bytes 262160 | tf_op jit(solution)/shard_map/reduce_scatter | solution.py:239
  1111.0 41.6 %all-gather.42.cloned.1.call-done = bf16[4096,704]{0,1:T(8,128)(2,1)} async-done(((bf16[512,704]{0,1:T(8,128)(2,1)}), bf16[4096,704]{0,1:T(8,128)(2,1)}) %all-gather.42.cloned.1.call-update) | async-done | bytes 5767184 | tf_op jit(solution)/shard_map/all_gather | solution.py:244
  1161.2 20.9 %copy.120 = f32[88,8,8,512]{3,2,1,0:T(8,128)} copy(f32[88,8,8,512]{3,1,2,0:T(8,128)} %bitcast.277) | data formatting | bytes 23068672
  1182.1 15.4 %copy.105 = f32[8,512,4,176]{1,3,0,2:T(8,128)} copy(f32[8,512,4,176]{1,0,3,2:T(8,128)} %bitcast.278) | data formatting | bytes 23068672 | tf_op jit(solution)/shard_map/convert_element_type | solution.py:287
  1218.4 20.4 %copy.121 = f32[88,8,8,512]{3,2,1,0:T(8,128)} copy(f32[88,8,8,512]{3,1,2,0:T(8,128)} %bitcast.280) | data formatting | bytes 23068672
  1238.9 15.5 %copy.106 = f32[8,512,4,176]{1,3,0,2:T(8,128)} copy(f32[8,512,4,176]{1,0,3,2:T(8,128)} %bitcast.281) | data formatting | bytes 23068672 | tf_op jit(solution)/shard_map/convert_element_type | solution.py:290
  1276.0 43.1 %reduce-scatter.13.cloned.1.call-done = bf16[256,2048]{1,0:T(8,128)(2,1)} async-done(((bf16[2048,2048]{1,0:T(8,128)(2,1)}), bf16[256,2048]{1,0:T(8,128)(2,1)}) %reduce-scatter.13.cloned.1.call-update) | async-done | bytes 1048592 | tf_op jit(solution)/shard_map/reduce_scatter | solution.py:230
  1321.6 40.3 %psum.7 = f32[14336]{0:T(1024)S(1)} all-reduce(f32[14336]{0:T(1024)S(1)} %constant_dynamic-update-slice_fusion.3), channel_id=1, replica_groups=mesh['ctx'=8,'fsdp'=4] {'fsdp','ctx'}, use_global_device_ids=true, to_apply=%region_24.25 | all-reduce | flops 14336 | bytes 114688 | tf_op jit(solution)/shard_map/psum | solution.py:265
  1377.0 21.8 %copy.119 = f32[96,8,8,512]{3,2,1,0:T(8,128)} copy(f32[96,8,8,512]{3,1,2,0:T(8,128)} %bitcast.274) | data formatting | bytes 25165824
  1398.8 16.4 %copy.104 = f32[512,3,8,256]{0,3,2,1:T(8,128)} copy(f32[512,3,8,256]{0,2,3,1:T(8,128)} %bitcast.275) | data formatting | bytes 25165824 | tf_op jit(solution)/shard_map/convert_element_type | solution.py:280
  (312 shorter events, 564.0 us)
Async XLA Ops:
  7.2 77.5 %all-gather.24.cloned.1.call-start = ((), (), s32[]{:S(2)}) async-start(), calls=%async_computation.11 | async-start | bytes 3932160 | tf_op jit(solution)/shard_map/all_gather | solution.py:164
  18.2 122.0 %all-gather.22.cloned.1.call-start = ((), (), s32[]{:S(2)}) async-start(), calls=%async_computation.10 | async-start | bytes 9437184 | tf_op jit(solution)/shard_map/all_gather | solution.py:163
  37.4 229.0 %all-gather.26.cloned.1.call-start = ((), (), s32[]{:S(2)}) async-start(), calls=%async_computation.12 | async-start | bytes 8650752 | tf_op jit(solution)/shard_map/all_gather | solution.py:180
  38.3 250.5 %all-gather.32.cloned.1.call-start = ((), (), s32[]{:S(2)}) async-start(), calls=%async_computation.15 | async-start | bytes 3604480 | tf_op jit(solution)/shard_map/all_gather | solution.py:185
  247.5 18.9 %all-to-all-start = ((bf16[8,256,256]{1,2,0:T(8,128)(2,1)}), bf16[8,256,256]{1,2,0:T(8,128)(2,1)S(1)}, u32[]{:S(2)}, u32[]{:S(2)}) async-start(bf16[8,256,256]{1,2,0:T(8,128)(2,1)} %copy.94), calls=%async_computation | async-start | bytes 2097152 | tf_op jit(solution)/shard_map/all_to_all | solution.py:179
  251.0 85.2 %all-gather.28.cloned.1.call-start = ((), (), s32[]{:S(2)}) async-start(), calls=%async_computation.13 | async-start | bytes 9437184 | tf_op jit(solution)/shard_map/all_gather | solution.py:183
  275.4 122.0 %all-gather.30.cloned.1.call-start = ((), (), s32[]{:S(2)}) async-start(), calls=%async_computation.14 | async-start | bytes 3604480 | tf_op jit(solution)/shard_map/all_gather | solution.py:184
  285.8 171.7 %all-gather.34.cloned.1.call-start = ((), (), s32[]{:S(2)}) async-start(), calls=%async_computation.16 | async-start | bytes 3604480 | tf_op jit(solution)/shard_map/all_gather | solution.py:186
  287.9 224.6 %all-gather.36.cloned.1.call-start = ((), (), s32[]{:S(2)}) async-start(), calls=%async_computation.25 | async-start | bytes 9437184 | tf_op jit(solution)/shard_map/all_gather | solution.py:197
  288.7 333.4 %reduce-scatter.11.cloned.1.call-start = ((), (), s32[]{:S(2)}) async-start(), calls=%async_computation.18 | async-start | bytes 9437184 | tf_op jit(solution)/shard_map/reduce_scatter | solution.py:203
  550.7 147.0 %reduce-scatter.9.cloned.1.call-start = ((), (), s32[]{:S(2)}) async-start(), calls=%async_computation.17 | async-start | bytes 9437184 | tf_op jit(solution)/shard_map/reduce_scatter | solution.py:192
  562.2 344.5 %reduce-scatter.19.cloned.1.call-start = ((), (), s32[]{:S(2)}) async-start(), calls=%async_computation.22 | async-start | bytes 3604480 | tf_op jit(solution)/shard_map/reduce_scatter | solution.py:239
  574.3 333.1 %reduce-scatter.21.cloned.1.call-start = ((), (), s32[]{:S(2)}) async-start(), calls=%async_computation.23 | async-start | bytes 3604480 | tf_op jit(solution)/shard_map/reduce_scatter | solution.py:239
  585.5 112.1 %copy-start.12 = (bf16[1,256,2048]{2,1,0:T(8,128)(2,1)S(1)}, bf16[1,256,2048]{2,1,0:T(8,128)(2,1)}, u32[]{:S(2)}) copy-start(bf16[1,256,2048]{2,1,0:T(8,128)(2,1)} %param.31) | copy-start | bytes 3145732
  709.6 18.9 %all-to-all-start.1 = ((bf16[256,8,256]{0,2,1:T(8,128)(2,1)}), bf16[256,8,256]{0,2,1:T(8,128)(2,1)S(1)}, u32[]{:S(2)}, u32[]{:S(2)}) async-start(bf16[256,8,256]{0,2,1:T(8,128)(2,1)} %bitcast.24), calls=%async_computation.3 | async-start | bytes 2097152 | tf_op jit(solution)/shard_map/all_to_all | solution.py:216
  713.1 194.8 %reduce-scatter.23.cloned.1.call-start = ((), (), s32[]{:S(2)}) async-start(), calls=%async_computation.24 | async-start | bytes 3604480 | tf_op jit(solution)/shard_map/reduce_scatter | solution.py:239
  723.9 235.1 %reduce-scatter.15.cloned.1.call-start = ((), (), s32[]{:S(2)}) async-start(), calls=%async_computation.20 | async-start | bytes 3932160 | tf_op jit(solution)/shard_map/reduce_scatter | solution.py:239
  899.1 211.5 %reduce-scatter.17.cloned.1.call-start = ((), (), s32[]{:S(2)}) async-start(), calls=%async_computation.21 | async-start | bytes 8650752 | tf_op jit(solution)/shard_map/reduce_scatter | solution.py:239
  906.7 245.9 %all-gather.42.cloned.1.call-start = ((), (), s32[]{:S(2)}) async-start(), calls=%async_computation.28 | async-start | bytes 6488064 | tf_op jit(solution)/shard_map/all_gather | solution.py:244
  907.3 302.5 %all-gather.44.cloned.1.call-start = ((), (), s32[]{:S(2)}) async-start(), calls=%async_computation.29 | async-start | bytes 6488064 | tf_op jit(solution)/shard_map/all_gather | solution.py:244
  907.9 359.3 %all-gather.46.cloned.1.call-start = ((), (), s32[]{:S(2)}) async-start(), calls=%async_computation.30 | async-start | bytes 6488064 | tf_op jit(solution)/shard_map/all_gather | solution.py:244
  908.4 410.7 %reduce-scatter.13.cloned.1.call-start = ((), (), s32[]{:S(2)}) async-start(), calls=%async_computation.19 | async-start | bytes 9437184 | tf_op jit(solution)/shard_map/reduce_scatter | solution.py:230
  919.9 447.5 %all-gather.38.cloned.1.call-start = ((), (), s32[]{:S(2)}) async-start(), calls=%async_computation.26 | async-start | bytes 7077888 | tf_op jit(solution)/shard_map/all_gather | solution.py:244
  959.0 469.0 %all-gather.40.cloned.1.call-start = ((), (), s32[]{:S(2)}) async-start(), calls=%async_computation.27 | async-start | bytes 2359296 | tf_op jit(solution)/shard_map/all_gather | solution.py:244
  (48 other events, 766.6 us)
Sparse Core Ops, SparseCore 0:
  18.4 66.3 all-gather.23
  87.2 53.0 all-gather.21
  143.7 77.2 all-gather.25
  223.0 57.7 all-gather.31
  283.1 53.1 all-gather.27
  338.2 59.1 all-gather.29
  399.5 57.8 all-gather.33
  459.4 53.0 all-gather.35
  550.8 71.2 reduce-scatter.10
  626.3 71.2 reduce-scatter.8
  700.5 56.1 reduce-scatter.18
  759.5 56.0 reduce-scatter.20
  817.8 56.0 reduce-scatter.22
  899.2 59.6 reduce-scatter.14
  961.6 148.8 reduce-scatter.16
  1112.3 40.2 all-gather.41
  1154.3 44.3 all-gather.43
  1200.4 43.3 all-gather.45
  1247.8 71.2 reduce-scatter.12
  1321.0 46.3 all-gather.37
  1369.5 27.8 all-gather.39

commit v2 on v1

v2 whole, which is shorter than its diff:
```python
import functools

import jax
import jax.numpy as jnp
from jax import lax
from jax.experimental import pallas as pl
from jax.experimental.pallas import tpu as pltpu
from jax.sharding import PartitionSpec as P

HEAD = 64
ROT = 16


NORM_EPSILON = 1e-05
ROTARY_BASE = 10000.0
MASKED_SCORE = -1e30


MESH_IDS = pl.DeviceIdType.MESH


def bit_of(index, bit):
    return index // (1 << bit) % 2


def flipped(index, mask, bits):
    result = index
    for bit in range(bits):
        if mask >> bit & 1:
            result = result + (1 - 2 * bit_of(index, bit)) * (1 << bit)
    return result


def greet(partners):
    barrier = pltpu.get_barrier_semaphore()
    for partner in partners:
        pl.semaphore_signal(barrier, inc=1, device_id={"ctx": partner}, device_id_type=MESH_IDS)
    pl.semaphore_wait(barrier, len(partners))


def half_orders(bits):
    chip_bits = list(range(1, bits))
    return [chip_bits, chip_bits[1:] + chip_bits[:1]]


def gather_plan(bits):
    steps = []
    for order in half_orders(bits):
        held = [0]
        plan = []
        for bit in order:
            plan.append((bit, list(held)))
            held = held + [mask | 1 << bit for mask in held]
        steps.append((plan, held))
    return steps


def column_half(ref, half):
    width = ref.shape[-1] // 2
    return ref.at[..., pl.ds(half * width, width)]


def row_half(ref, half):
    rows = ref.shape[-2] // 2
    if len(ref.shape) == 2:
        return ref.at[pl.ds(half * rows, rows)]
    return ref.at[..., pl.ds(half * rows, rows), :]


def stacked_rows(ref, block, half):
    return row_half(ref.at[block], half)


def stacked_columns(ref, block, half):
    return column_half(ref.at[block], half)


def middle_columns(ref, block, half):
    return column_half(ref.at[:, block], half)


def block_view(ref, block):
    return ref.at[block]


def column_view(ref, block, width):
    return ref.at[:, pl.ds(pl.multiple_of(block * width, width), width)]


def gather_run(bits, take, put, source, out, send_sem, recv_sem, core_send, core_recv, local_sem):
    me = lax.axis_index("ctx")
    steps = gather_plan(bits)
    finals = []
    for half in range(2):
        copy = pltpu.make_async_copy(take(source, half), put(out, me, half), local_sem.at[half])
        copy.start()
        finals.append(copy.wait)

    def push(half, mask, bit, send, recv, index):
        block = flipped(me, mask, bits)
        copy = pltpu.make_async_remote_copy(
            src_ref=take(source, half) if mask == 0 else put(out, block, half),
            dst_ref=put(out, block, half),
            send_sem=send.at[half, index],
            recv_sem=recv.at[half, index],
            device_id={"ctx": flipped(me, 1 << bit, bits)},
            device_id_type=MESH_IDS,
        )
        copy.start()
        return copy

    arriving = {}
    for phase in range(bits):
        for half in range(2):
            plan, held = steps[half]
            if phase > 0:
                for copy in arriving[half]:
                    copy.wait_recv()
            if phase < bits - 1:
                bit, masks = plan[phase]
                arriving[half] = [
                    push(half, mask, bit, send_sem, recv_sem, (1 << phase) - 1 + number)
                    for number, mask in enumerate(masks)
                ]
                finals += [copy.wait_send for copy in arriving[half]]
            fresh = held[:1] if phase == 0 else held[1 << (phase - 1) : 1 << phase]
            for mask in fresh:
                copy = push(half, mask, 0, core_send, core_recv, held.index(mask))
                finals.append(copy.wait)
            yield
    for wait in finals:
        wait()


def gather_op(x, size, take=row_half, put=stacked_rows, out_shape=None):
    bits = size.bit_length() - 1
    steps = size // 2 - 1
    dma = pltpu.SemaphoreType.DMA
    return dict(
        run=functools.partial(gather_run, bits, take, put),
        inputs=[x],
        in_space=pl.ANY,
        outs=[jax.ShapeDtypeStruct(out_shape or (size,) + x.shape, x.dtype)],
        out_space=pl.ANY,
        scratch=[dma((2, steps)), dma((2, steps)), dma((2, steps + 1)), dma((2, steps + 1)), dma((2,))],
        far=False,
        moved=2 * size * x.size * 2,
    )


def add_into(target, first, second, rows, step):
    @pl.loop(0, rows // step)
    def _(i):
        at = pl.ds(pl.multiple_of(i * step, step), step)
        target[at] = (first[at].astype(jnp.float32) + second[at].astype(jnp.float32)).astype(
            target.dtype
        )


def scatter_plan(bits):
    plans = []
    for order in half_orders(bits):
        kept = [mask << 1 for mask in range(1 << (bits - 1))]
        plan = []
        for bit in order:
            plan.append((bit, [mask for mask in kept if mask >> bit & 1]))
            kept = [mask for mask in kept if not mask >> bit & 1]
        plans.append(plan)
    return plans


def farthest_first(masks):
    return sorted(masks, key=lambda mask: -bin(mask).count("1"))


def scatter_run(bits, step, part_ref, out_ref, core_buf, chip_buf, core_send, core_recv, send_sem, recv_sem):
    me = lax.axis_index("ctx")
    rows = part_ref.shape[1]
    width = part_ref.shape[2] // 2
    plans = scatter_plan(bits)
    chip_masks = farthest_first([mask << 1 for mask in range(1 << (bits - 1))])
    finals = []
    core_copies = {}
    for mask in chip_masks:
        copy = pltpu.make_async_remote_copy(
            src_ref=part_ref.at[flipped(me, mask | 1, bits)],
            dst_ref=core_buf.at[mask >> 1],
            send_sem=core_send.at[mask >> 1],
            recv_sem=core_recv.at[mask >> 1],
            device_id={"ctx": flipped(me, 1, bits)},
            device_id_type=MESH_IDS,
        )
        copy.start()
        core_copies[mask] = copy
        finals.append(copy.wait_send)
    arriving = {}

    def columns(half):
        return pl.ds(half * width, width)

    def send(half, phase, bit, mask):
        slot = plans[half][phase][1].index(mask)
        copy = pltpu.make_async_remote_copy(
            src_ref=part_ref.at[flipped(me, mask, bits), :, columns(half)],
            dst_ref=chip_buf.at[half, phase, slot],
            send_sem=send_sem.at[half, phase, slot],
            recv_sem=recv_sem.at[half, phase, slot],
            device_id={"ctx": flipped(me, 1 << bit, bits)},
            device_id_type=MESH_IDS,
        )
        copy.start()
        finals.append(copy.wait_send)
        arriving[half, phase, mask & ~(1 << bit)] = (copy, slot)

    yield
    for mask in chip_masks:
        core_copies[mask].wait_recv()
        here = part_ref.at[flipped(me, mask, bits)]
        add_into(here, here, core_buf.at[mask >> 1], rows, step)
        for half in range(2):
            bit, masks = plans[half][0]
            if mask in masks:
                send(half, 0, bit, mask)
    yield
    phases = bits - 1
    for phase in range(1, phases + 1):
        for half in range(2):
            last_bit, last_masks = plans[half][phase - 1]
            kept = farthest_first([mask & ~(1 << last_bit) for mask in last_masks])
            for mask in kept:
                copy, slot = arriving[half, phase - 1, mask]
                copy.wait_recv()
                here = part_ref.at[flipped(me, mask, bits), :, columns(half)]
                buf = chip_buf.at[half, phase - 1, slot]
                if phase < phases:
                    add_into(here, here, buf, rows, step)
                    bit, masks = plans[half][phase]
                    if mask in masks:
                        send(half, phase, bit, mask)
                else:
                    add_into(out_ref.at[:, columns(half)], here, buf, rows, step)
        yield
    for wait in finals:
        wait()


def scatter_op(part, size):
    bits = size.bit_length() - 1
    chips = size // 2
    rows, width = part.shape[1:]
    dma = pltpu.SemaphoreType.DMA
    return dict(
        run=functools.partial(scatter_run, bits, 32),
        inputs=[part],
        in_space=pltpu.VMEM,
        outs=[jax.ShapeDtypeStruct((rows, width), jnp.float32)],
        out_space=pltpu.VMEM,
        scratch=[
            pltpu.VMEM((chips, rows, width), part.dtype),
            pltpu.VMEM((2, bits - 1, chips // 2, rows, width // 2), part.dtype),
            dma((chips,)),
            dma((chips,)),
            dma((2, bits - 1, chips // 2)),
            dma((2, bits - 1, chips // 2)),
        ],
        far=False,
        moved=4 * part.size,
    )


def exchange_run(size, take, put, source, out, send_sem, recv_sem, local_sem):
    me = lax.axis_index("ctx")
    local = pltpu.make_async_copy(take(source, me), put(out, me), local_sem)
    local.start()
    copies = []
    for step in range(1, size):
        other = lax.rem(me + step, size)
        copy = pltpu.make_async_remote_copy(
            src_ref=take(source, other),
            dst_ref=put(out, me),
            send_sem=send_sem.at[step - 1],
            recv_sem=recv_sem.at[step - 1],
            device_id={"ctx": other},
            device_id_type=MESH_IDS,
        )
        copy.start()
        copies.append(copy)
    yield
    local.wait()
    for copy in copies:
        copy.wait()


def exchange_op(x, size, out_shape, take, put):
    dma = pltpu.SemaphoreType.DMA
    return dict(
        run=functools.partial(exchange_run, size, take, put),
        inputs=[x],
        in_space=pl.ANY,
        outs=[jax.ShapeDtypeStruct(out_shape, x.dtype)],
        out_space=pl.ANY,
        scratch=[dma((size - 1,)), dma((size - 1,)), dma],
        far=True,
        moved=4 * x.size,
    )


def plane_kernel(size, parts, *refs):
    bits = size.bit_length() - 1
    me = lax.axis_index("ctx")
    if any(far for _, _, _, _, far in parts):
        greet([lax.rem(me + step, size) for step in range(1, size)])
    else:
        greet([flipped(me, 1 << bit, bits) for bit in range(bits)])
    ins = sum(part[1] for part in parts)
    outs = sum(part[2] for part in parts)
    groups = [list(refs[:ins]), list(refs[ins : ins + outs]), list(refs[ins + outs :])]
    running = []
    for run, *counts, far in parts:
        own = []
        for group, count in zip(groups, counts):
            own += group[:count]
            del group[:count]
        running.append(run(*own))
    while running:
        running = [turn_of for turn_of in running if next(turn_of, 1) is None]


def plane(size, collective_id, *ops):
    parts = [
        (op["run"], len(op["inputs"]), len(op["outs"]), len(op["scratch"]), op["far"]) for op in ops
    ]
    results = pl.pallas_call(
        functools.partial(plane_kernel, size, parts),
        out_shape=[out for op in ops for out in op["outs"]],
        in_specs=[pl.BlockSpec(memory_space=op["in_space"]) for op in ops for _ in op["inputs"]],
        out_specs=[pl.BlockSpec(memory_space=op["out_space"]) for op in ops for _ in op["outs"]],
        scratch_shapes=[scratch for op in ops for scratch in op["scratch"]],
        compiler_params=pltpu.CompilerParams(
            collective_id=collective_id, has_side_effects=True, vmem_limit_bytes=60 << 20
        ),
        cost_estimate=pl.CostEstimate(
            flops=0, bytes_accessed=sum(op["moved"] for op in ops), transcendentals=0
        ),
    )(*[x for op in ops for x in op["inputs"]])
    return results if len(results) > 1 else results[0]


def plane_groups(size, collective_id, *ops):
    groups = []
    room = 0
    for op in ops:
        need = 0 if op["in_space"] == pl.ANY else op["moved"] * 5 // 4
        if not groups or need > room:
            groups.append([])
            room = 52 << 20
        groups[-1].append(op)
        room -= need
    results = []
    for i, group in enumerate(groups):
        got = plane(size, collective_id + i, *group)
        results += got if isinstance(got, (list, tuple)) else [got]
    return results


def unpack_kernel(segments, count, source, out):
    strip = source.shape[2] // segments
    pieces = []
    for segment in range(segments):
        for owner in range(count):
            pieces.append(source[owner, :, segment * strip : (segment + 1) * strip])
    out[...] = jnp.concatenate(pieces, 1).astype(jnp.float32)


def unpack_columns(gathered, segments):
    count, rows, width = gathered.shape
    step = 64
    return pl.pallas_call(
        functools.partial(unpack_kernel, segments, count),
        grid=(rows // step,),
        in_specs=[pl.BlockSpec((count, step, width), lambda i: (0, i, 0))],
        out_specs=pl.BlockSpec((step, count * width), lambda i: (i, 0)),
        out_shape=jax.ShapeDtypeStruct((rows, count * width), jnp.float32),
        compiler_params=pltpu.CompilerParams(vmem_limit_bytes=32 << 20),
        cost_estimate=pl.CostEstimate(
            flops=0, bytes_accessed=6 * gathered.size, transcendentals=0
        ),
    )(gathered)


def norm_rows(values, gain_row, shift_row):
    centered = values - jnp.mean(values, -1, keepdims=True)
    inverse = lax.rsqrt(jnp.mean(centered * centered, -1, keepdims=True) + NORM_EPSILON)
    unit_rows = centered * inverse
    return (unit_rows * gain_row + shift_row, unit_rows, inverse)


def norm_back(grad_rows, unit_rows, inverse, gain_row):
    scaled = grad_rows * gain_row
    return inverse * (
        scaled
        - jnp.mean(scaled, -1, keepdims=True)
        - unit_rows * jnp.mean(scaled * unit_rows, -1, keepdims=True)
    )


def turn(rows, cosine, sine_low, sine_high, width):
    repeat = width // 128
    wide = [jnp.concatenate([table] * repeat, 1) for table in (cosine, sine_low, sine_high)]
    return (
        rows * wide[0]
        + pltpu.roll(rows, width - ROT // 2, 1) * wide[1]
        + pltpu.roll(rows, ROT // 2, 1) * wide[2]
    )


def head_stack(features_first, heads):
    owner = lax.broadcasted_iota(jnp.int32, features_first.shape, 0) // HEAD
    zero = jnp.zeros_like(features_first)
    return jnp.concatenate([jnp.where(owner == h, features_first, zero) for h in range(heads)], 1)


def row_stack(rows, heads):
    owner = lax.broadcasted_iota(jnp.int32, rows.shape, 1) // HEAD
    zero = jnp.zeros_like(rows)
    return jnp.concatenate([jnp.where(owner == h, rows, zero) for h in range(heads)], 0)


def allowed_pairs(query_tile, key_tile, tile, heads, starts):
    query_place = query_tile * tile + lax.broadcasted_iota(jnp.int32, (1, tile), 1)
    query_place = jnp.concatenate([query_place] * heads, 1)
    first_key = jnp.concatenate([starts] * heads, 1)
    key_place = key_tile * tile + lax.broadcasted_iota(jnp.int32, (tile, 1), 0)
    return (key_place <= query_place) & (key_place >= first_key)


def transposed(rows):
    return jnp.transpose(rows.astype(jnp.float32)).astype(rows.dtype)


def attend_kernel(
    block,
    heads,
    order,
    lowest,
    projected,
    starts,
    cosine,
    sine_low,
    sine_high,
    qkv,
    attended,
    mixed,
    log_total,
    value_t,
    summed,
    top,
    total,
):
    cols = heads * HEAD
    seq = projected.shape[0]
    tile = 2 * block

    @pl.loop(0, seq // block)
    def _(p):
        at = pl.ds(pl.multiple_of(p * block, block), block)
        rows = projected[pl.ds(pl.multiple_of(order[p] * block, block), block)]
        tables = (cosine[at], sine_low[at], sine_high[at])
        query = turn(rows[:, :cols], *tables, cols) * HEAD ** (-0.5)
        key = turn(rows[:, cols : 2 * cols], *tables, cols)
        value = rows[:, 2 * cols :]
        qkv[at, :cols] = query.astype(jnp.bfloat16)
        qkv[at, cols : 2 * cols] = key.astype(jnp.bfloat16)
        qkv[at, 2 * cols :] = value.astype(jnp.bfloat16)
        value_t[:, at] = jnp.transpose(value).astype(jnp.bfloat16)

    @pl.loop(0, seq // tile)
    def _(i):
        at = pl.ds(pl.multiple_of(i * tile, tile), tile)
        query_t = head_stack(transposed(qkv[at, :cols]), heads)
        first_keys = starts[:, at]
        top[...] = jnp.full(top.shape, MASKED_SCORE, jnp.float32)
        total[...] = jnp.zeros_like(total)
        summed[...] = jnp.zeros_like(summed)

        @pl.loop(lowest[i], i + 1)
        def _(j):
            keys_at = pl.ds(pl.multiple_of(j * tile, tile), tile)
            scores = jnp.dot(
                qkv[keys_at, cols : 2 * cols], query_t, preferred_element_type=jnp.float32
            )
            scores = jnp.where(
                allowed_pairs(i, j, tile, heads, first_keys), scores, MASKED_SCORE
            )
            old_top = top[...]
            new_top = jnp.maximum(old_top, jnp.max(scores, 0, keepdims=True))
            exps = jnp.exp(scores - new_top)
            fade = jnp.exp(old_top - new_top)
            total[...] = total[...] * fade + jnp.sum(exps, 0, keepdims=True)
            top[...] = new_top
            low = exps.astype(jnp.bfloat16)
            for h in range(heads):
                own = slice(h * tile, (h + 1) * tile)
                features = slice(h * HEAD, (h + 1) * HEAD)
                summed[features] = summed[features] * fade[:, own] + jnp.dot(
                    value_t[features, keys_at], low[:, own], preferred_element_type=jnp.float32
                )

        log_total[i] = top[...] + jnp.log(total[...])
        scale = 1.0 / total[...]
        for h in range(heads):
            features = slice(h * HEAD, (h + 1) * HEAD)
            summed[features] = summed[features] * scale[:, h * tile : (h + 1) * tile]
        rows = jnp.transpose(summed[...])
        attended[at] = rows
        for part in range(2):
            place = pl.ds(pl.multiple_of(order[2 * i + part] * block, block), block)
            mixed[place] = rows[part * block : (part + 1) * block].astype(jnp.bfloat16)


def attend(projected, order, lowest, starts, tables, heads):
    seq, wide = projected.shape
    cols = wide // 3
    block = seq // order.shape[0]
    tile = 2 * block
    vmem = pl.BlockSpec(memory_space=pltpu.VMEM)
    smem = pl.BlockSpec(memory_space=pltpu.SMEM)
    return pl.pallas_call(
        functools.partial(attend_kernel, block, heads),
        in_specs=[smem, smem] + [vmem] * 5,
        out_specs=[vmem] * 4,
        out_shape=[
            jax.ShapeDtypeStruct((seq, wide), jnp.bfloat16),
            jax.ShapeDtypeStruct((seq, cols), jnp.float32),
            jax.ShapeDtypeStruct((seq, cols), jnp.bfloat16),
            jax.ShapeDtypeStruct((seq // tile, 1, heads * tile), jnp.float32),
        ],
        scratch_shapes=[
            pltpu.VMEM((cols, seq), jnp.bfloat16),
            pltpu.VMEM((cols, tile), jnp.float32),
            pltpu.VMEM((1, heads * tile), jnp.float32),
            pltpu.VMEM((1, heads * tile), jnp.float32),
        ],
        compiler_params=pltpu.CompilerParams(vmem_limit_bytes=48 << 20),
        cost_estimate=pl.CostEstimate(
            flops=4 * seq * seq * cols, bytes_accessed=12 * seq * cols, transcendentals=0
        ),
    )(order, lowest, projected, starts, *tables)


def attend_back_kernel(
    block,
    heads,
    order,
    lowest,
    qkv,
    grad_mixed,
    attended,
    log_total,
    starts,
    cosine,
    sine_low,
    sine_high,
    out,
    sums,
    key_t,
    grad_rows,
    grad_key,
    grad_value,
    grad_query,
):
    cols = heads * HEAD
    seq = qkv.shape[0]
    tile = 2 * block

    @pl.loop(0, seq // block)
    def _(p):
        at = pl.ds(pl.multiple_of(p * block, block), block)
        key_t[:, at] = transposed(qkv[at, cols : 2 * cols])
        grad_rows[at] = grad_mixed[pl.ds(pl.multiple_of(order[p] * block, block), block)]
        grad_key[at] = jnp.zeros((block, cols), jnp.float32)
        grad_value[at] = jnp.zeros((block, cols), jnp.float32)

    sums[...] = jnp.zeros_like(sums)

    def finish(p, columns, rows):
        low = rows.astype(jnp.bfloat16)
        out[pl.ds(pl.multiple_of(order[p] * block, block), block), columns] = low
        sums[:, columns] += jnp.sum(low.astype(jnp.float32), 0, keepdims=True)

    def turned_back(p, rows):
        at = pl.ds(pl.multiple_of(p * block, block), block)
        return turn(rows, cosine[at], -sine_low[at], -sine_high[at], cols)

    @pl.loop(0, seq // tile)
    def _(i):
        at = pl.ds(pl.multiple_of(i * tile, tile), tile)
        query = qkv[at, :cols]
        grad = grad_rows[at]
        query_t = head_stack(transposed(query), heads)
        query_rows = row_stack(query, heads)
        grad_t = head_stack(transposed(grad), heads)
        grads = row_stack(grad, heads)
        products = jnp.transpose(grad.astype(jnp.float32) * attended[at])
        delta = jnp.concatenate(
            [
                jnp.sum(products[h * HEAD : (h + 1) * HEAD], 0, keepdims=True)
                for h in range(heads)
            ],
            1,
        )
        logs = log_total[i]
        first_keys = starts[:, at]
        grad_query[...] = jnp.zeros_like(grad_query)

        @pl.loop(lowest[i], i + 1)
        def _(j):
            keys_at = pl.ds(pl.multiple_of(j * tile, tile), tile)
            scores = jnp.dot(
                qkv[keys_at, cols : 2 * cols], query_t, preferred_element_type=jnp.float32
            )
            weights = jnp.where(
                allowed_pairs(i, j, tile, heads, first_keys), jnp.exp(scores - logs), 0.0
            )
            grad_soft = jnp.dot(
                qkv[keys_at, 2 * cols :], grad_t, preferred_element_type=jnp.float32
            )
            grad_value[keys_at] += jnp.dot(
                weights.astype(jnp.bfloat16), grads, preferred_element_type=jnp.float32
            )
            grad_scores = (weights * (grad_soft - delta)).astype(jnp.bfloat16)
            grad_key[keys_at] += jnp.dot(
                grad_scores, query_rows, preferred_element_type=jnp.float32
            )
            for h in range(heads):
                features = slice(h * HEAD, (h + 1) * HEAD)
                grad_query[features] += jnp.dot(
                    key_t[features, keys_at],
                    grad_scores[:, h * tile : (h + 1) * tile],
                    preferred_element_type=jnp.float32,
                )

        rows = jnp.transpose(grad_query[...]) * HEAD ** (-0.5)
        for part in range(2):
            p = 2 * i + part
            finish(p, slice(0, cols), turned_back(p, rows[part * block : (part + 1) * block]))

    @pl.loop(0, seq // block)
    def _(p):
        at = pl.ds(pl.multiple_of(p * block, block), block)
        finish(p, slice(cols, 2 * cols), turned_back(p, grad_key[at]))
        finish(p, slice(2 * cols, 3 * cols), grad_value[at])


def attend_back(qkv, grad_mixed, attended, log_total, order, lowest, starts, tables, heads):
    seq, wide = qkv.shape
    cols = wide // 3
    block = seq // order.shape[0]
    tile = 2 * block
    vmem = pl.BlockSpec(memory_space=pltpu.VMEM)
    smem = pl.BlockSpec(memory_space=pltpu.SMEM)
    return pl.pallas_call(
        functools.partial(attend_back_kernel, block, heads),
        in_specs=[smem, smem] + [vmem] * 8,
        out_specs=[vmem] * 2,
        out_shape=[
            jax.ShapeDtypeStruct((seq, wide), jnp.bfloat16),
            jax.ShapeDtypeStruct((1, wide), jnp.float32),
        ],
        scratch_shapes=[
            pltpu.VMEM((cols, seq), jnp.bfloat16),
            pltpu.VMEM((seq, cols), jnp.bfloat16),
            pltpu.VMEM((seq, cols), jnp.float32),
            pltpu.VMEM((seq, cols), jnp.float32),
            pltpu.VMEM((cols, tile), jnp.float32),
        ],
        compiler_params=pltpu.CompilerParams(vmem_limit_bytes=48 << 20),
        cost_estimate=pl.CostEstimate(
            flops=10 * seq * seq * cols, bytes_accessed=20 * seq * cols, transcendentals=0
        ),
    )(order, lowest, qkv, grad_mixed, attended, log_total, starts, *tables)


def rotary_tables(seq):
    lane = jnp.arange(128, dtype=jnp.int32)[None, :] % HEAD
    half_rot = ROT // 2
    freq = ROTARY_BASE ** (-(lane % half_rot).astype(jnp.float32) * 2.0 / ROT)
    angles = jnp.arange(seq, dtype=jnp.int32).astype(jnp.float32)[:, None] * freq
    sine = jnp.sin(angles)
    return (
        jnp.where(lane < ROT, jnp.cos(angles), 1.0),
        jnp.where(lane < half_rot, -sine, 0.0),
        jnp.where((lane >= half_rot) & (lane < ROT), sine, 0.0),
    )


def place_order(block_pairs, axis_size):
    device_blocks = jnp.stack([block_pairs, 2 * axis_size - 1 - block_pairs], 1).reshape(-1)
    places = jnp.arange(2 * axis_size, dtype=jnp.int32)
    return jnp.sum(
        jnp.where(device_blocks[None, :] == places[:, None], places[None, :], 0), 1
    ).astype(jnp.int32)


def document_starts(docs):
    first = jnp.sum((docs < 1).astype(jnp.int32))
    second = jnp.sum((docs < 2).astype(jnp.int32))
    return jnp.where(docs == 0, 0, jnp.where(docs == 1, first, second))


def inner(left_side, right_side):
    return lax.dot_general(
        left_side, right_side, (((0,), (0,)), ((), ())), preferred_element_type=jnp.float32
    )


def times_transposed(left_side, right_side):
    return lax.dot_general(
        left_side, right_side, (((1,), (1,)), ((), ())), preferred_element_type=jnp.float32
    )


def times(left_side, right_side):
    return jnp.dot(left_side, right_side, preferred_element_type=jnp.float32)


def after(value, *earlier):
    return lax.optimization_barrier((value,) + earlier)[0]


def body(
    tokens,
    doc_ids,
    block_pairs,
    ln1_gain,
    ln1_bias,
    w_qkv,
    b_qkv,
    w_out,
    ln2_gain,
    ln2_bias,
    w_gate,
    w_up,
    w_down,
    cotangent,
):
    rows_here = tokens.shape[1]
    width = tokens.shape[2]
    head_count = width // HEAD
    ctx_size = lax.axis_size("ctx")
    fsdp_size = lax.axis_size("fsdp")
    seq_rows = rows_here * ctx_size
    position = lax.axis_index("ctx")
    heads_here = head_count // ctx_size
    cols = width // ctx_size
    shard_rows = w_qkv.shape[0]
    hidden_shard = w_down.shape[0]
    strip = hidden_shard // ctx_size

    tile = 2 * (rows_here // 2)
    order = place_order(block_pairs, ctx_size)
    starts = document_starts(doc_ids[0])
    lowest = starts[::tile] // tile
    starts = starts[None]
    tables = rotary_tables(seq_rows)

    small = lax.all_gather(
        jnp.concatenate([ln1_gain, ln1_bias, ln2_gain, ln2_bias, b_qkv]), "fsdp", axis=0
    ).astype(jnp.float32)
    gain_one, shift_one, gain_two, shift_two = (
        small[:, i * shard_rows : (i + 1) * shard_rows].reshape(1, width) for i in range(4)
    )
    bias_full = small[:, 4 * shard_rows :].reshape(3, ctx_size, cols)
    bias_here = lax.dynamic_index_in_dim(bias_full, position, 1, keepdims=False).reshape(3 * cols)

    def strips(w, count, size):
        stride = w.shape[1] // count
        return [
            lax.dynamic_slice_in_dim(w, i * stride + position * size, size, 1)
            for i in range(count)
        ]

    qkv_strip = jnp.concatenate(strips(w_qkv, 3, cols), 1)
    both_strip = jnp.concatenate(
        strips(w_gate, fsdp_size, strip) + strips(w_up, fsdp_size, strip), 1
    )
    down_strip = lax.dynamic_slice_in_dim(w_down, position * strip, strip, 0)
    out_piece = shard_rows // ctx_size
    out_strip = lax.dynamic_slice_in_dim(w_out, position * out_piece, out_piece, 0)
    hidden_here = fsdp_size * strip

    out_here = lax.all_gather(out_strip, "fsdp", axis=0)
    qkv_here = lax.all_gather(qkv_strip, "fsdp", axis=0, tiled=True)
    both_here = lax.all_gather(both_strip, "fsdp", axis=0, tiled=True)
    down_here = lax.all_gather(down_strip, "fsdp", axis=0, tiled=True)

    grad_out = cotangent[0]
    tokens_all, grad_out_all = plane(
        ctx_size, 1, gather_op(tokens[0], ctx_size), gather_op(grad_out, ctx_size)
    )
    tokens_all = tokens_all.reshape(seq_rows, width)
    grad_out_all = grad_out_all.reshape(seq_rows, width)
    tokens_in = tokens[0].astype(jnp.float32)
    normed, unit_one, inverse_one = norm_rows(tokens_in, gain_one, shift_one)
    normed_all = norm_rows(tokens_all.astype(jnp.float32), gain_one, shift_one)[0].astype(
        jnp.bfloat16
    )
    projected = times(normed_all, qkv_here) + bias_here
    qkv_rows, attended, mixed_here, log_total = attend(
        projected, order, lowest, starts, tables, heads_here
    )
    mixed_here = mixed_here.reshape(ctx_size, rows_here, cols)
    to_columns = functools.partial(column_view, width=cols)
    mixed_rows, out_full = plane(
        ctx_size,
        2,
        exchange_op(mixed_here, ctx_size, (rows_here, width), block_view, to_columns),
        gather_op(
            out_here,
            ctx_size,
            column_half,
            middle_columns,
            (fsdp_size, ctx_size, out_piece, width),
        ),
    )
    out_full = out_full.reshape(width, width)
    residual = tokens_in + times(mixed_rows, out_full)
    normed_two, unit_two, inverse_two = norm_rows(residual, gain_two, shift_two)
    normed_two_all = plane(ctx_size, 3, gather_op(normed_two.astype(jnp.bfloat16), ctx_size))
    normed_two_all = normed_two_all.reshape(seq_rows, width)
    both_value = times(normed_two_all, both_here)
    gate_value = both_value[:, :hidden_here]
    up_value = both_value[:, hidden_here:]
    sigmoid_gate = jax.nn.sigmoid(gate_value)
    silu_gate = gate_value * sigmoid_gate
    hidden = (silu_gate * up_value).astype(jnp.bfloat16)

    def blocks(rows):
        return rows.astype(jnp.bfloat16).reshape(ctx_size, rows_here, width)

    grad_down_w = inner(hidden, grad_out_all).astype(jnp.bfloat16)
    grad_hidden = times_transposed(after(grad_out_all, grad_down_w), down_here)
    grad_gate = grad_hidden * up_value * sigmoid_gate * (1.0 + gate_value * (1.0 - sigmoid_gate))
    grad_up = grad_hidden * silu_gate
    grad_both = jnp.concatenate([grad_gate, grad_up], 1).astype(jnp.bfloat16)
    grad_both_w = inner(normed_two_all, grad_both).astype(jnp.bfloat16)
    grad_normed_two = plane(
        ctx_size,
        4,
        scatter_op(blocks(times_transposed(after(grad_both, grad_both_w), both_here)), ctx_size),
    )
    grad_residual = grad_out.astype(jnp.float32) + norm_back(
        grad_normed_two, unit_two, inverse_two, gain_two
    )
    grad_branch = grad_residual.astype(jnp.bfloat16)
    grad_mixed_rows = times_transposed(grad_branch, out_full).astype(jnp.bfloat16)
    grad_mixed = plane(
        ctx_size,
        5,
        exchange_op(
            grad_mixed_rows, ctx_size, (ctx_size, rows_here, cols), to_columns, block_view
        ),
    )
    grad_projected, grad_bias = attend_back(
        qkv_rows,
        grad_mixed.reshape(seq_rows, cols),
        attended,
        log_total,
        order,
        lowest,
        starts,
        tables,
        heads_here,
    )
    grad_qkv_w = inner(normed_all, grad_projected).astype(jnp.bfloat16)
    mixed_blocks = jnp.transpose(
        mixed_rows.reshape(rows_here, fsdp_size, ctx_size, out_piece), (0, 2, 1, 3)
    ).reshape(rows_here, width)
    grad_normed, grad_out_w = plane_groups(
        ctx_size,
        6,
        scatter_op(
            blocks(times_transposed(after(grad_projected, grad_qkv_w), qkv_here)), ctx_size
        ),
        scatter_op(
            inner(mixed_blocks, after(grad_branch, grad_qkv_w))
            .astype(jnp.bfloat16)
            .reshape(ctx_size, fsdp_size * out_piece, width),
            ctx_size,
        ),
    )
    grad_tokens = grad_residual + norm_back(grad_normed, unit_one, inverse_one, gain_one)

    def reduced(grad):
        return lax.psum_scatter(
            grad.astype(jnp.bfloat16), "fsdp", scatter_dimension=0, tiled=True
        )

    grad_down_w = reduced(grad_down_w)
    grad_both_w = reduced(grad_both_w)
    grad_qkv_w = reduced(grad_qkv_w)
    norm_sums = jnp.stack(
        [
            jnp.sum(grad_normed * unit_one, 0),
            jnp.sum(grad_normed, 0),
            jnp.sum(grad_normed_two * unit_two, 0),
            jnp.sum(grad_normed_two, 0),
        ]
    )
    norm_sums = jnp.transpose(norm_sums.reshape(4, fsdp_size, shard_rows), (1, 0, 2)).reshape(
        fsdp_size, 1, 4 * shard_rows
    )
    bias_sums = lax.dynamic_update_slice(
        jnp.zeros((3, ctx_size, cols), jnp.float32),
        grad_bias.reshape(3, 1, cols),
        (0, position, 0),
    ).reshape(fsdp_size, 1, 3 * width // fsdp_size)
    padded = [
        jnp.pad(rows, ((0, 0), (0, extra), (0, width - rows.shape[2])))
        for rows, extra in ((norm_sums, 0), (bias_sums, 14))
    ]
    grad_out_w = jnp.concatenate(
        [grad_out_w.reshape(fsdp_size, out_piece, width)] + padded, 1
    )
    grad_out_w = reduced(grad_out_w.reshape(fsdp_size * (out_piece + 16), width))
    layer_part, grad_down_w, grad_both_w = plane_groups(
        ctx_size,
        8,
        scatter_op(blocks(times(after(hidden, grad_normed), down_here)), ctx_size),
        gather_op(grad_down_w, ctx_size, column_half, stacked_columns),
        gather_op(grad_both_w, ctx_size),
    )
    layer_out = residual + layer_part
    grad_out_w, grad_qkv_w = plane(
        ctx_size,
        10,
        gather_op(after(grad_out_w, grad_down_w), ctx_size, column_half, stacked_columns),
        gather_op(grad_qkv_w, ctx_size),
    )
    sums = jnp.sum(grad_out_w[:, out_piece : out_piece + 2].astype(jnp.float32), 0)
    norm_sums = sums[0, : 4 * shard_rows].reshape(4, shard_rows)
    bias_sums = sums[1, : b_qkv.shape[0]]
    grad_out_w = grad_out_w[:, :out_piece]
    float32 = jnp.float32
    return (
        layer_out.astype(jnp.bfloat16)[None],
        grad_tokens[None],
        norm_sums[0],
        norm_sums[1],
        unpack_columns(grad_qkv_w, 3),
        bias_sums,
        grad_out_w.reshape(w_out.shape).astype(float32),
        norm_sums[2],
        norm_sums[3],
        unpack_columns(grad_both_w[:, :, :hidden_here], fsdp_size),
        unpack_columns(grad_both_w[:, :, hidden_here:], fsdp_size),
        grad_down_w.reshape(w_down.shape).astype(float32),
    )


def solution(mesh):
    placed = (
        P("fsdp", "ctx", None),
        P("fsdp", None),
        P(),
        P("fsdp"),
        P("fsdp"),
        P("fsdp", None),
        P("fsdp"),
        P("fsdp", None),
        P("fsdp"),
        P("fsdp"),
        P("fsdp", None),
        P("fsdp", None),
        P("fsdp", None),
        P("fsdp", "ctx", None),
    )
    return jax.shard_map(
        body,
        mesh=mesh,
        in_specs=placed,
        out_specs=(
            P("fsdp", "ctx", None),
            P("fsdp", "ctx", None),
            P("fsdp"),
            P("fsdp"),
            P("fsdp", None),
            P("fsdp"),
            P("fsdp", None),
            P("fsdp"),
            P("fsdp"),
            P("fsdp", None),
            P("fsdp", None),
            P("fsdp", None),
        ),
        check_vma=False,
    )
```

time: 1450 us -> 861 us (0.59)
  waiting for transfers between devices: 686 us -> 0.9 us
  Pallas kernels: 0 us -> 571 us
  matrix products: 347 us -> 140 us
  local copies, waits for them, and re-layouts: 240 us -> 47.3 us
  blocking collectives: 55.2 us -> 15.3 us
  other arithmetic: 86.6 us -> 66.3 us
    pallas_call x0 -> x13, Pallas kernels: none -> 571 us  [the longest x8 486 us: plane(): pl.pallas_call(functools.partial(plane_kernel, size, parts), out_shape=[o...]
    reduce_scatter x8 -> x4, waiting for transfers between devices: 342 us -> 0.04 us  [reduced(): lax.psum_scatter(grad.astype(jnp.bfloat16), 'fsdp', scatter_dimension=0,...]
    all_gather x11 -> x2, waiting for transfers between devices: 250 us -> 0.02 us  [the longest x1 0.02 us: body(): both_here = lax.all_gather(both_strip, 'fsdp', axis=0, tiled=True)]
    unnamed x119 -> x93, local copies, waits for them, and re-layouts: 142 us -> 14.9 us
    dot_general x17 -> x4, matrix products: 155 us -> 48.5 us  [times_transposed(): lax.dot_general(left_side, right_side, (((1,), (1,)), ((), ())), preferre...]
    convert_element_type x5 -> x0, local copies, waits for them, and re-layouts: 58 us -> none  [the longest x4 56.8 us: body(): return (layer_out.astype(jnp.bfloat16)[None], grad_tokens[None], norm_sum...]
    dot_general x13 -> x4, matrix products: 98.4 us -> 46.4 us  [times(): return jnp.dot(left_side, right_side, preferred_element_type=jnp.float32)]
    all_gather x1, waiting for transfers between devices: 49.1 us -> 0.01 us  [body(): down_here = lax.all_gather(down_strip, 'fsdp', axis=0, tiled=True)]
  transfers between devices with their start and end apart: 23 -> 8, of which waited for: 15 -> 0; matrix products, arithmetic and copies ran while one was open for 43% -> 24% of each run, Pallas kernels for 0% -> 59%
where the time goes in v2:
time: 861 us; the launch traced here: 857 us
  Pallas kernels  571 us (66%)
  matrix products  140 us (16%)
  other arithmetic  66.3 us (8%)
  local copies, waits for them, and re-layouts  47.3 us (5%)
  blocking collectives  15.3 us (2%)
  between operations  15 us (2%)
    pallas_call x8, Pallas kernels, plane(): pl.pallas_call(functools.partial(plane_kernel, size, parts), out_shape=[o...  486 us
    dot_general x4, matrix products, times_transposed(): lax.dot_general(left_side, right_side, (((1,), (1,)), ((), ())), preferre...  48.5 us
    dot_general x4, matrix products, times(): return jnp.dot(left_side, right_side, preferred_element_type=jnp.float32)  46.4 us
    dot_general x4, matrix products, inner(): lax.dot_general(left_side, right_side, (((0,), (0,)), ((), ())), preferre...  45.3 us
    pallas_call x1, Pallas kernels, attend_back(): pl.pallas_call(functools.partial(attend_back_kernel, block, heads), in_sp...  35.8 us
    pallas_call x1, Pallas kernels, attend(): pl.pallas_call(functools.partial(attend_kernel, block, heads), in_specs=[...  30.4 us
    pallas_call x3, Pallas kernels, unpack_columns(): pl.pallas_call(functools.partial(unpack_kernel, segments, count), grid=(r...  18.6 us
  transfers between devices with their start and end apart: 8, of which 0 were waited for; matrix products, arithmetic and copies ran while one was open for 24% of the time, Pallas kernels for 59%

profile of v2, /device:TPU:0, one launch (start us, length us, event | category | flops | bytes accessed | tf_op | source)
XLA Modules:
  0.0 856.6 jit_solution(7273203977459842612)
XLA Ops:
  18.9 15.3 %all-gather.2 = bf16[4,1,3584]{2,1,0:T(2,128)(2,1)S(1)} all-gather(bf16[1,1,3584]{2,1,0:T(2,128)(2,1)S(1)} %reshape.283), channel_id=2, replica_groups=mesh['ctx'=8,'fsdp'=4] {'fsdp'}, dimensions={0}, use_global_device_ids=true | all-gather | bytes 35840 | tf_op jit(solution)/shard_map/all_gather | solution.py:767
  34.5 76.8 %shard_map.229 = (bf16[8,256,2048]{2,1,0:T(8,128)(2,1)}, bf16[8,256,2048]{2,1,0:T(8,128)(2,1)}) custom-call(bf16[256,2048]{1,0:T(8,128)(2,1)} %bitcast.109, bf16[256,2048]{1,0:T(8,128)(2,1)} %bitcast.118), custom_call_target="tpu_custom_call" | custom-call | bytes 33554432 | tf_op jit(solution)/shard_map/pallas_call | solution.py:333
  123.0 8.7 %fusion.3 = bf16[2048,2048]{1,0:T(8,128)(2,1)} fusion(bf16[8,256,2048]{2,1,0:T(8,128)(2,1)} %get-tuple-element.35, f32[2048]{0:T(1024)S(1)} %bitcast.133, f32[2048]{0:T(1024)S(1)} %bitcast.126, f32[2048]{0:T(1024)S(1)} %bitcast.131, f32[2048]{0:T(1024)S(1)} %bitcast.132), kind=kLoop, calls=%fused_computation.4 | loop fusion | flops 25165824 | bytes 16809984 | tf_op jit(solution)/shard_map/convert_element_type | solution.py:805
  135.6 11.7 %broadcast_add_fusion.projected = f32[2048,768]{1,0:T(8,128)} fusion(f32[768]{0:T(1024)S(1)} %add.201, bf16[2048,2048]{1,0:T(8,128)(2,1)} %fusion.3, bf16[2048,768]{1,0:T(8,128)(2,1)} %all-gather.8.cloned.1.call-done), kind=kOutput, calls=%fused_computation.21 | convolution fusion | flops 6444023808 | bytes 17828864 | tf_op jit(solution)/shard_map/dot_general | solution.py:724
  147.3 30.4 %shard_map.230 = (bf16[2048,768]{1,0:T(8,128)(2,1)}, f32[2048,256]{1,0:T(8,128)}, bf16[2048,256]{1,0:T(8,128)(2,1)S(1)}, f32[8,1,1024]{2,1,0:T(1,128)S(1)}) custom-call(s32[16]{0:T(128)S(1)} %select_reduce_fusion.order, s32[8]{0:T(128)S(1)} %and_select_fusion.2.lowest, f32[2048,768]{1,0:T(8,128)} %broadcast_add_fusion.projected, ...), custom_call_target="tpu_custom_call" | custom-call | flops 4294967296 | bytes 6291456 | tf_op jit(solution)/shard_map/pallas_call | solution.py:528
  178.7 55.6 %shard_map.231 = (bf16[256,2048]{1,0:T(8,128)(2,1)}, bf16[4,8,64,2048]{3,2,1,0:T(8,128)(2,1)}) custom-call(bf16[8,256,256]{2,1,0:T(8,128)(2,1)} %bitcast.105, bf16[4,64,2048]{2,1,0:T(8,128)(2,1)} %bitcast.120), custom_call_target="tpu_custom_call" | custom-call | bytes 18874368 | tf_op jit(solution)/shard_map/pallas_call | solution.py:333
  243.5 43.9 %shard_map.232 = bf16[8,256,2048]{2,1,0:T(8,128)(2,1)} custom-call(bf16[256,2048]{1,0:T(8,128)(2,1)} %add_convert_fusion.1.refs_0_), custom_call_target="tpu_custom_call" | custom-call | bytes 16777216 | tf_op jit(solution)/shard_map/pallas_call | solution.py:333
  287.4 19.0 %fusion.37 = f32[2048,1408]{0,1:T(8,128)} fusion(bf16[2048,2048]{1,0:T(8,128)(2,1)} %bitcast.112, bf16[2048,1408]{1,0:T(8,128)(2,1)} %all-gather.10.cloned.1.call-done), kind=kOutput, calls=%fused_computation.125 | convolution fusion | flops 11811160064 | bytes 25690112 | tf_op jit(solution)/shard_map/dot_general | solution.py:724
  313.3 10.8 %convolution_convert_fusion.6 = bf16[704,2048]{1,0:T(8,128)(2,1)} fusion(bf16[2048,704]{0,1:T(8,128)(2,1)S(1)} %multiply_convert_fusion.2, bf16[2048,2048]{1,0:T(8,128)(2,1)} %bitcast.139), kind=kOutput, calls=%fused_computation.20 | convolution fusion | flops 5907021824 | bytes 14155776 | tf_op jit(solution)/shard_map/dot_general | solution.py:712
  330.8 14.8 %multiply_convert_fusion.1 = (bf16[2048,704]{0,1:T(8,128)(2,1)S(1)}, bf16[2048,704]{0,1:T(8,128)(2,1)S(1)}) fusion(f32[2048,1408]{0,1:T(8,128)} %fusion.37, bf16[2048,2048]{1,0:T(8,128)(2,1)} %bitcast.140, bf16[704,2048]{1,0:T(8,128)(2,1)} %all-gather.12.cloned.1.call-done), kind=kOutput, calls=%fused_computation.15 | convolution fusion | flops 5924323328 | bytes 28573696 | tf_op jit(solution)/shard_map/dot_general | solution.py:718
  348.1 17.3 %convolution_convert_fusion.4 = bf16[2048,1408]{1,0:T(8,128)(2,1)} fusion(bf16[2048,2048]{1,0:T(8,128)(2,1)} %bitcast.113, bf16[2048,704]{0,1:T(8,128)(2,1)S(1)} %get-tuple-element.71, bf16[2048,704]{0,1:T(8,128)(2,1)S(1)} %get-tuple-element.70), kind=kOutput, calls=%fused_computation.11 | convolution fusion | flops 11825577984 | bytes 19922944 | tf_op jit(solution)/shard_map/dot_general | solution.py:712
  369.0 18.0 %convolution_convert_fusion.3 = bf16[2048,2048]{1,0:T(8,128)(2,1)} fusion(bf16[2048,1408]{0,1:T(8,128)(2,1)S(1)} %pad_maximum_fusion, bf16[2048,1408]{1,0:T(8,128)(2,1)} %all-gather.10.cloned.1.call-done), kind=kOutput, calls=%fused_computation.10 | convolution fusion | flops 11815354368 | bytes 19922944 | tf_op jit(solution)/shard_map/dot_general | solution.py:718
  387.0 47.6 %shard_map.233 = f32[256,2048]{1,0:T(8,128)} custom-call(bf16[8,256,2048]{2,1,0:T(8,128)(2,1)} %bitcast.111), custom_call_target="tpu_custom_call" | custom-call | bytes 16777216 | tf_op jit(solution)/shard_map/pallas_call | solution.py:333
  442.5 6.7 convolution_convert_fusion.7.refs_0_
  449.3 13.9 %shard_map.234 = bf16[8,256,256]{2,1,0:T(8,128)(2,1)} custom-call(bf16[256,2048]{1,0:T(8,128)(2,1)} %convolution_convert_fusion.7.refs_0_), custom_call_target="tpu_custom_call" | custom-call | bytes 2097152 | tf_op jit(solution)/shard_map/pallas_call | solution.py:333
  464.4 35.8 %shard_map.235 = (bf16[2048,768]{1,0:T(8,128)(2,1)}, f32[1,768]{1,0:T(1,128)S(1)}) custom-call(s32[16]{0:T(128)S(1)} %select_reduce_fusion.order, s32[8]{0:T(128)S(1)} %copy-done.7, bf16[2048,768]{1,0:T(8,128)(2,1)} %get-tuple-element.39.qkv, bf16[2048,256]{1,0:T(8,128)(2,1)S(1)} %bitcast.104, f32[2048,256]{1,0:T(8,128)} %get-tuple-element.43.attended, ...), custom_call_target="tpu_custom_call" | custom-call | flops 10737418240 | bytes 10485760 | tf_op jit(solution)/shard_map/pallas_call | solution.py:662
  500.2 11.5 %convolution_convert_fusion.5 = bf16[2048,768]{1,0:T(8,128)(2,1)} fusion(bf16[2048,2048]{1,0:T(8,128)(2,1)} %fusion.3, bf16[2048,768]{1,0:T(8,128)(2,1)} %get-tuple-element.46), kind=kOutput, calls=%fused_computation.19 | convolution fusion | flops 6444023808 | bytes 14680064 | tf_op jit(solution)/shard_map/dot_general | solution.py:712
  517.4 9.0 %convolution_convert_fusion.2 = bf16[2048,2048]{1,0:T(8,128)(2,1)} fusion(bf16[2048,768]{1,0:T(8,128)(2,1)S(1)} %copy-done.37, bf16[2048,768]{1,0:T(8,128)(2,1)S(1)} %copy-done.35), kind=kOutput, calls=%fused_computation.9 | convolution fusion | flops 6446645248 | bytes 14680064 | tf_op jit(solution)/shard_map/dot_general | solution.py:718
  526.5 83.0 %shard_map.236 = (f32[256,2048]{1,0:T(8,128)}, f32[256,2048]{1,0:T(8,128)}) custom-call(bf16[8,256,2048]{2,1,0:T(8,128)(2,1)} %bitcast.114, bf16[8,256,2048]{2,1,0:T(8,128)(2,1)} %bitcast.108), custom_call_target="tpu_custom_call" | custom-call | bytes 33554432 | tf_op jit(solution)/shard_map/pallas_call | solution.py:333
  620.8 9.2 %convolution_convert_fusion = bf16[2048,2048]{1,0:T(8,128)(2,1)} fusion(bf16[2048,704]{0,1:T(8,128)(2,1)S(1)} %copy-done.21, bf16[704,2048]{1,0:T(8,128)(2,1)S(1)} %copy-done.36), kind=kOutput, calls=%fused_computation.7 | convolution fusion | flops 5909774336 | bytes 14155776 | tf_op jit(solution)/shard_map/dot_general | solution.py:724
  630.1 121.9 %shard_map.237 = (f32[256,2048]{1,0:T(8,128)}, bf16[8,176,2048]{2,1,0:T(8,128)(2,1)}, bf16[8,512,1408]{2,1,0:T(8,128)(2,1)}) custom-call(bf16[8,256,2048]{2,1,0:T(8,128)(2,1)} %bitcast.110, bf16[176,2048]{1,0:T(8,128)(2,1)} %reduce-scatter.5.cloned.1.call-done.refs_1_, bf16[512,1408]{1,0:T(8,128)(2,1)} %reduce-scatter.7.cloned.1.call-done.refs_2_), custom_call_target="tpu_custom_call" | custom-call | bytes 51380224 | tf_op jit(solution)/shard_map/pallas_call | solution.py:333
  752.0 43.8 %shard_map.238 = (bf16[8,80,2048]{2,1,0:T(8,128)(2,1)}, bf16[8,512,768]{2,1,0:T(8,128)(2,1)}) custom-call(bf16[80,2048]{1,0:T(8,128)(2,1)} %reduce-scatter.9.cloned.1.call-done.refs_0_, bf16[512,768]{1,0:T(8,128)(2,1)} %reduce-scatter.11.cloned.1.call-done.refs_1_), custom_call_target="tpu_custom_call" | custom-call | bytes 17825792 | tf_op jit(solution)/shard_map/pallas_call | solution.py:333
  801.4 8.8 %bitcast_convert_fusion = f32[1408,2048]{1,0:T(8,128)} fusion(bf16[8,176,2048]{2,1,0:T(8,128)(2,1)} %get-tuple-element.53), kind=kLoop, calls=%fused_computation.13 | loop fusion | flops 2883584 | bytes 17301504 | tf_op jit(solution)/shard_map/convert_element_type | solution.py:957
  815.9 13.1 %fusion.34 = (bf16[8,512,704]{2,1,0:T(8,128)(2,1)}, bf16[8,512,704]{2,1,0:T(8,128)(2,1)}) fusion(bf16[8,512,1408]{2,1,0:T(8,128)(2,1)} %get-tuple-element.57), kind=kLoop, calls=%fused_computation.122 | loop fusion | bytes 23068672 | tf_op jit(solution)/shard_map/slice | solution.py:956
  (190 shorter events, 115.0 us)
Async XLA Ops:
  7.2 128.4 %all-gather.8.cloned.1.call-start = ((), (), s32[]{:S(2)}) async-start(), calls=%async_computation.4 | async-start | bytes 3932160 | tf_op jit(solution)/shard_map/all_gather | solution.py:793
  9.5 169.2 %all-gather.14.cloned.1.call-start = ((), (), s32[]{:S(2)}) async-start(), calls=%async_computation.11 | async-start | bytes 1310720 | tf_op jit(solution)/shard_map/all_gather | solution.py:792
  10.3 277.1 %all-gather.10.cloned.1.call-start = ((), (), s32[]{:S(2)}) async-start(), calls=%async_computation.5 | async-start | bytes 7208960 | tf_op jit(solution)/shard_map/all_gather | solution.py:794
  13.3 5.5 copy-start.29
  13.4 20.9 %copy-start.12 = (bf16[1,256,2048]{2,1,0:T(8,128)(2,1)S(1)}, bf16[1,256,2048]{2,1,0:T(8,128)(2,1)}, u32[]{:S(2)}) copy-start(bf16[1,256,2048]{2,1,0:T(8,128)(2,1)} %param.14) | copy-start | bytes 3145732
  15.8 315.0 %all-gather.12.cloned.1.call-start = ((), (), s32[]{:S(2)}) async-start(), calls=%async_computation.6 | async-start | bytes 3604480 | tf_op jit(solution)/shard_map/all_gather | solution.py:795
  17.9 612.2 %reduce-scatter.5.cloned.1.call-start = ((), (), s32[]{:S(2)}) async-start(), calls=%async_computation.7 | async-start | bytes 3604480 | tf_op jit(solution)/shard_map/reduce_scatter | solution.py:895
  111.3 6.8 copy-start.8
  120.5 11.3 %copy-start.26 = (f32[1,4,4,128]{3,1,2,0:T(4,128)}, f32[1,4,4,128]{3,1,2,0:T(4,128)S(1)}, u32[]{:S(2)}) copy-start(f32[1,4,4,128]{3,1,2,0:T(4,128)S(1)} %copy.50) | copy-start | bytes 24580
  122.7 24.7 %copy-start.6 = (s32[8]{0:T(128)}, s32[8]{0:T(128)S(1)}, u32[]{:S(2)}) copy-start(s32[8]{0:T(128)S(1)} %and_select_fusion.2.lowest) | copy-start | bytes 100
  324.1 306.0 %reduce-scatter.7.cloned.1.call-start = ((), (), s32[]{:S(2)}) async-start(), calls=%async_computation.8 | async-start | bytes 7208960 | tf_op jit(solution)/shard_map/reduce_scatter | solution.py:895
  365.4 386.5 %reduce-scatter.9.cloned.1.call-start = ((), (), s32[]{:S(2)}) async-start(), calls=%async_computation.9 | async-start | bytes 1638400 | tf_op jit(solution)/shard_map/reduce_scatter | solution.py:895
  442.5 20.6 %copy-start.7 = (s32[8]{0:T(128)S(1)}, s32[8]{0:T(128)}, u32[]{:S(2)}) copy-start(s32[8]{0:T(128)} %copy-done.6) | copy-start | bytes 100
  500.1 11.5 %copy-start.17 = (bf16[256,8,4,64]{0,3,2,1:T(8,128)(2,1)S(1)}, bf16[256,8,4,64]{0,3,2,1:T(8,128)(2,1)}, u32[]{:S(2)}) copy-start(bf16[256,8,4,64]{0,3,2,1:T(8,128)(2,1)} %copy.42) | copy-start | bytes 3145732
  500.1 11.5 %copy-start.19 = (bf16[256,2048]{1,0:T(8,128)(2,1)S(1)}, bf16[256,2048]{1,0:T(8,128)(2,1)}, u32[]{:S(2)}) copy-start(bf16[256,2048]{1,0:T(8,128)(2,1)} %copy-done.18) | copy-start | bytes 3145732
  511.7 5.8 copy-start.35
  511.7 5.8 copy-start.37
  526.5 83.0 %copy-start.13 = (bf16[1,256,2048]{2,1,0:T(8,128)(2,1)S(1)}, bf16[1,256,2048]{2,1,0:T(8,128)(2,1)}, u32[]{:S(2)}) copy-start(bf16[1,256,2048]{2,1,0:T(8,128)(2,1)} %param.14) | copy-start | bytes 3145732
  526.5 83.0 %copy-start.27 = (f32[1,4,4,128]{3,1,2,0:T(4,128)S(1)}, f32[1,4,4,128]{3,1,2,0:T(4,128)}, u32[]{:S(2)}) copy-start(f32[1,4,4,128]{3,1,2,0:T(4,128)} %copy-done.26) | copy-start | bytes 24580
  616.2 135.8 %reduce-scatter.11.cloned.1.call-start = ((), (), s32[]{:S(2)}) async-start(), calls=%async_computation.10 | async-start | bytes 3932160 | tf_op jit(solution)/shard_map/reduce_scatter | solution.py:895
  795.8 14.4 %slice-start = ((s8[6291456]{0:T(1024)(128)(4,1)}), s8[4194304]{0:T(1024)(128)(4,1)S(1)}, s32[]{:S(2)}) async-start(s8[6291456]{0:T(1024)(128)(4,1)} %bitcast.102), calls=%async_computation.12 | async-start | bytes 8388608
  801.4 8.8 %slice-start.1 = ((s8[6291456]{0:T(1024)(128)(4,1)}), s8[2097152]{0:T(1024)(128)(4,1)S(1)}, s32[]{:S(2)}) async-start(s8[6291456]{0:T(1024)(128)(4,1)} %bitcast.102), calls=%async_computation.13 | async-start | bytes 4194304
  831.8 6.4 copy-start.2
  838.2 6.4 copy-start.15
  (24 other events, 74.7 us)
Sparse Core Ops, SparseCore 0:
  10.2 67.0 all-gather.7
  79.5 26.4 all-gather.13
  108.1 106.1 all-gather.9
  215.8 57.4 all-gather.11
  324.2 53.8 reduce-scatter.4
  380.8 102.0 reduce-scatter.6
  616.3 28.5 reduce-scatter.8
  647.8 59.0 reduce-scatter.10

commit v3 on v2

--- a/solution.py
+++ b/solution.py
@@ -31,11 +31,12 @@
     return result
 
 
-def greet(partners):
+def greet(partners, along_z=()):
     barrier = pltpu.get_barrier_semaphore()
-    for partner in partners:
-        pl.semaphore_signal(barrier, inc=1, device_id={"ctx": partner}, device_id_type=MESH_IDS)
-    pl.semaphore_wait(barrier, len(partners))
+    for axis, others in (("ctx", partners), ("fsdp", along_z)):
+        for other in others:
+            pl.semaphore_signal(barrier, inc=1, device_id={axis: other}, device_id_type=MESH_IDS)
+    pl.semaphore_wait(barrier, len(partners) + len(along_z))
 
 
 def half_orders(bits):
@@ -87,20 +88,24 @@
     return ref.at[:, pl.ds(pl.multiple_of(block * width, width), width)]
 
 
-def gather_run(bits, take, put, source, out, send_sem, recv_sem, core_send, core_recv, local_sem):
+def gather_run(
+    bits, take, put, relative, source, out, send_sem, recv_sem, core_send, core_recv, local_sem
+):
     me = lax.axis_index("ctx")
     steps = gather_plan(bits)
     finals = []
     for half in range(2):
-        copy = pltpu.make_async_copy(take(source, half), put(out, me, half), local_sem.at[half])
+        own = put(out, 0 if relative else me, half)
+        copy = pltpu.make_async_copy(take(source, half), own, local_sem.at[half])
         copy.start()
         finals.append(copy.wait)
 
     def push(half, mask, bit, send, recv, index):
-        block = flipped(me, mask, bits)
+        block = mask if relative else flipped(me, mask, bits)
+        there = mask | 1 << bit if relative else block
         copy = pltpu.make_async_remote_copy(
             src_ref=take(source, half) if mask == 0 else put(out, block, half),
-            dst_ref=put(out, block, half),
+            dst_ref=put(out, there, half),
             send_sem=send.at[half, index],
             recv_sem=recv.at[half, index],
             device_id={"ctx": flipped(me, 1 << bit, bits)},
@@ -132,18 +137,17 @@
         wait()
 
 
-def gather_op(x, size, take=row_half, put=stacked_rows, out_shape=None):
+def gather_op(x, size, take=row_half, put=stacked_rows, out_shape=None, relative=False):
     bits = size.bit_length() - 1
     steps = size // 2 - 1
     dma = pltpu.SemaphoreType.DMA
     return dict(
-        run=functools.partial(gather_run, bits, take, put),
+        run=functools.partial(gather_run, bits, take, put, relative),
         inputs=[x],
         in_space=pl.ANY,
         outs=[jax.ShapeDtypeStruct(out_shape or (size,) + x.shape, x.dtype)],
         out_space=pl.ANY,
         scratch=[dma((2, steps)), dma((2, steps)), dma((2, steps + 1)), dma((2, steps + 1)), dma((2,))],
-        far=False,
         moved=2 * size * x.size * 2,
     )
 
@@ -263,7 +267,6 @@
             dma((2, bits - 1, chips // 2)),
             dma((2, bits - 1, chips // 2)),
         ],
-        far=False,
         moved=4 * part.size,
     )
 
@@ -305,18 +308,206 @@
     )
 
 
-def plane_kernel(size, parts, *refs):
+def z_gather_run(size, source, out, send_sem, recv_sem, local_sem):
+    me = lax.axis_index("fsdp")
+    local = pltpu.make_async_copy(source, out.at[me], local_sem)
+    local.start()
+    copies = []
+    for step in range(1, size):
+        copy = pltpu.make_async_remote_copy(
+            src_ref=source,
+            dst_ref=out.at[me],
+            send_sem=send_sem.at[step - 1],
+            recv_sem=recv_sem.at[step - 1],
+            device_id={"fsdp": lax.rem(me + step, size)},
+            device_id_type=MESH_IDS,
+        )
+        copy.start()
+        copies.append(copy)
+    for _ in range(4):
+        yield
+    local.wait()
+    for copy in copies:
+        copy.wait()
+
+
+def z_gather_op(x, size):
+    dma = pltpu.SemaphoreType.DMA
+    return dict(
+        run=functools.partial(z_gather_run, size),
+        inputs=[x],
+        in_space=pl.ANY,
+        outs=[jax.ShapeDtypeStruct((size,) + x.shape, x.dtype)],
+        out_space=pl.ANY,
+        scratch=[dma((size - 1,)), dma((size - 1,)), dma],
+        z=size,
+        moved=2 * size * x.size,
+    )
+
+
+def z_scatter_run(size, source, out, buf, send_sem, recv_sem):
+    me = lax.axis_index("fsdp")
+    copies = []
+    for step in range(1, size):
+        other = lax.rem(me + step, size)
+        copy = pltpu.make_async_remote_copy(
+            src_ref=source.at[other],
+            dst_ref=buf.at[step - 1],
+            send_sem=send_sem.at[step - 1],
+            recv_sem=recv_sem.at[step - 1],
+            device_id={"fsdp": other},
+            device_id_type=MESH_IDS,
+        )
+        copy.start()
+        copies.append(copy)
+    for _ in range(4):
+        yield
+    total = source[me].astype(jnp.float32)
+    for step, copy in enumerate(copies):
+        copy.wait()
+        total += buf[step].astype(jnp.float32)
+    out[...] = total.astype(out.dtype)
+
+
+def z_scatter_op(x, size):
+    dma = pltpu.SemaphoreType.DMA
+    return dict(
+        run=functools.partial(z_scatter_run, size),
+        inputs=[x],
+        in_space=pltpu.VMEM,
+        outs=[jax.ShapeDtypeStruct(x.shape[1:], x.dtype)],
+        out_space=pltpu.VMEM,
+        scratch=[
+            pltpu.VMEM((size - 1,) + x.shape[1:], x.dtype),
+            dma((size - 1,)),
+            dma((size - 1,)),
+        ],
+        z=size,
+        moved=4 * x.size,
+    )
+
+
+def z_sum_gather_run(bits, size, source, out, low, buf, send_sem, recv_sem, *sems):
+    yield from z_scatter_run(size, source, low, buf, send_sem, recv_sem)
+    yield from gather_run(bits, column_half, stacked_columns, False, low, out, *sems)
+
+
+def z_sum_gather_op(x, z_size, size):
+    summed = z_scatter_op(x, z_size)
+    (shape,) = summed["outs"]
+    gather = gather_op(shape, size)
+    return dict(
+        run=functools.partial(z_sum_gather_run, size.bit_length() - 1, z_size),
+        inputs=[x],
+        in_space=pltpu.VMEM,
+        outs=gather["outs"],
+        out_space=pl.ANY,
+        scratch=[pltpu.VMEM(shape.shape, shape.dtype)] + summed["scratch"] + gather["scratch"],
+        z=z_size,
+        moved=summed["moved"] + gather["moved"],
+    )
+
+
+def project_run(
+    cols,
+    tokens,
+    weights,
+    gain,
+    shift,
+    bias,
+    cosine,
+    sine_low,
+    sine_high,
+    qkv,
+    normed,
+    tokens_buf,
+    normed_buf,
+    weights_buf,
+    load_sem,
+    store_sem,
+    weights_sem,
+):
+    size, rows = tokens.shape[:2]
+
+    def load(block):
+        slot = block % 2
+        return pltpu.make_async_copy(tokens.at[block], tokens_buf.at[slot], load_sem.at[slot])
+
+    def store(block):
+        slot = block % 2
+        return pltpu.make_async_copy(normed_buf.at[slot], normed.at[block], store_sem.at[slot])
+
+    load_weights = pltpu.make_async_copy(weights, weights_buf, weights_sem)
+    load(0).start()
+    load_weights.start()
+    yield
+    for block in range(size):
+        if block + 1 < size:
+            load(block + 1).start()
+        load(block).wait()
+        at = pl.ds(block * rows, rows)
+        values = tokens_buf[block % 2].astype(jnp.float32)
+        centered = values - jnp.mean(values, -1, keepdims=True)
+        inverse = lax.rsqrt(jnp.mean(centered * centered, -1, keepdims=True) + NORM_EPSILON)
+        low = (centered * inverse * gain[...] + shift[...]).astype(jnp.bfloat16)
+        if block >= 2:
+            store(block - 2).wait()
+        normed_buf[block % 2] = low
+        store(block).start()
+        if block == 0:
+            load_weights.wait()
+        projected = jnp.dot(low, weights_buf[...], preferred_element_type=jnp.float32)
+        projected += bias[...]
+        tables = (cosine[at], sine_low[at], sine_high[at])
+        query = turn(projected[:, :cols], *tables, cols) * HEAD ** (-0.5)
+        qkv[block, :, :cols] = query.astype(jnp.bfloat16)
+        key = turn(projected[:, cols : 2 * cols], *tables, cols)
+        qkv[block, :, cols : 2 * cols] = key.astype(jnp.bfloat16)
+        qkv[block, :, 2 * cols :] = projected[:, 2 * cols :].astype(jnp.bfloat16)
+        yield
+    store(size - 2).wait()
+    store(size - 1).wait()
+
+
+def project_op(tokens, weights, gain, shift, bias, tables):
+    size, rows, width = tokens.shape
+    wide = weights.shape[1]
+    low = jnp.bfloat16
+    dma = pltpu.SemaphoreType.DMA
+    return dict(
+        run=functools.partial(project_run, wide // 3),
+        inputs=[tokens, weights, gain, shift, bias, *tables],
+        in_spaces=[pl.ANY] * 2 + [pltpu.VMEM] * 6,
+        outs=[
+            jax.ShapeDtypeStruct((size, rows, wide), low),
+            jax.ShapeDtypeStruct((size, rows, width), low),
+        ],
+        out_spaces=[pltpu.VMEM, pl.ANY],
+        scratch=[
+            pltpu.VMEM((2, rows, width), low),
+            pltpu.VMEM((2, rows, width), low),
+            pltpu.VMEM(weights.shape, low),
+            dma((2,)),
+            dma((2,)),
+            dma,
+        ],
+        moved=4 * tokens.size,
+    )
+
+
+def plane_kernel(size, parts, far, z_size, *refs):
     bits = size.bit_length() - 1
     me = lax.axis_index("ctx")
-    if any(far for _, _, _, _, far in parts):
-        greet([lax.rem(me + step, size) for step in range(1, size)])
-    else:
-        greet([flipped(me, 1 << bit, bits) for bit in range(bits)])
+    my_z = lax.axis_index("fsdp")
+    partners = [flipped(me, 1 << bit, bits) for bit in range(bits)]
+    if far:
+        partners = [lax.rem(me + step, size) for step in range(1, size)]
+    greet(partners, [lax.rem(my_z + step, z_size) for step in range(1, z_size)])
     ins = sum(part[1] for part in parts)
     outs = sum(part[2] for part in parts)
     groups = [list(refs[:ins]), list(refs[ins : ins + outs]), list(refs[ins + outs :])]
     running = []
-    for run, *counts, far in parts:
+    for run, *counts in parts:
         own = []
         for group, count in zip(groups, counts):
             own += group[:count]
@@ -326,15 +517,20 @@
         running = [turn_of for turn_of in running if next(turn_of, 1) is None]
 
 
+def spaces(op, side):
+    arrays = op["inputs"] if side == "in" else op["outs"]
+    return op.get(side + "_spaces") or [op[side + "_space"]] * len(arrays)
+
+
 def plane(size, collective_id, *ops):
-    parts = [
-        (op["run"], len(op["inputs"]), len(op["outs"]), len(op["scratch"]), op["far"]) for op in ops
-    ]
+    parts = [(op["run"], len(op["inputs"]), len(op["outs"]), len(op["scratch"])) for op in ops]
+    far = any(op.get("far") for op in ops)
+    z_size = max(op.get("z", 1) for op in ops)
     results = pl.pallas_call(
-        functools.partial(plane_kernel, size, parts),
+        functools.partial(plane_kernel, size, parts, far, z_size),
         out_shape=[out for op in ops for out in op["outs"]],
-        in_specs=[pl.BlockSpec(memory_space=op["in_space"]) for op in ops for _ in op["inputs"]],
-        out_specs=[pl.BlockSpec(memory_space=op["out_space"]) for op in ops for _ in op["outs"]],
+        in_specs=[pl.BlockSpec(memory_space=space) for op in ops for space in spaces(op, "in")],
+        out_specs=[pl.BlockSpec(memory_space=space) for op in ops for space in spaces(op, "out")],
         scratch_shapes=[scratch for op in ops for scratch in op["scratch"]],
         compiler_params=pltpu.CompilerParams(
             collective_id=collective_id, has_side_effects=True, vmem_limit_bytes=60 << 20
@@ -350,7 +546,7 @@
     groups = []
     room = 0
     for op in ops:
-        need = 0 if op["in_space"] == pl.ANY else op["moved"] * 5 // 4
+        need = 0 if op.get("in_space") == pl.ANY else op["moved"] * 5 // 4
         if not groups or need > room:
             groups.append([])
             room = 52 << 20
@@ -361,6 +557,560 @@
         got = plane(size, collective_id + i, *group)
         results += got if isinstance(got, (list, tuple)) else [got]
     return results
+
+
+def swapped(tile):
+    return tile % 2 + 2 * (tile // 4 % 2) + 4 * (tile // 2 % 2)
+
+
+def tile_put(ref, mask, half):
+    return row_half(ref.at[mask if half == 0 else swapped(mask)], half)
+
+
+def tile_partner(me, bit):
+    return {"ctx": flipped(me, 1 << bit, 3)}
+
+
+def tile_copy(source, target, half, bit, me, send_sem, recv_sem):
+    rows = source.shape[0] // 2
+    at = pl.ds(half * rows, rows)
+    return pltpu.make_async_remote_copy(
+        src_ref=source.at[at],
+        dst_ref=target.at[at],
+        send_sem=send_sem.at[half],
+        recv_sem=recv_sem.at[half],
+        device_id=tile_partner(me, bit),
+        device_id_type=MESH_IDS,
+    )
+
+
+def core_copy(source, target, me, send_sem, recv_sem):
+    return pltpu.make_async_remote_copy(
+        src_ref=source,
+        dst_ref=target,
+        send_sem=send_sem,
+        recv_sem=recv_sem,
+        device_id=tile_partner(me, 0),
+        device_id_type=MESH_IDS,
+    )
+
+
+class TileGather:
+    def __init__(self, tiles, send_sem, recv_sem, core_send, core_recv):
+        me = lax.axis_index("ctx")
+        self.hops = {
+            target: [
+                tile_copy(
+                    tiles.at[source],
+                    tiles.at[target],
+                    half,
+                    (first, 3 - first)[half],
+                    me,
+                    send_sem.at[target // 2 - 1],
+                    recv_sem.at[target // 2 - 1],
+                )
+                for half in range(2)
+            ]
+            for source, target, first in ((0, 2, 1), (0, 4, 2), (2, 6, 2))
+        }
+        self.cores = [
+            core_copy(tiles.at[2 * i], tiles.at[2 * i + 1], me, core_send.at[i], core_recv.at[i])
+            for i in range(4)
+        ]
+
+    def before(self, tile):
+        if tile == 0:
+            for copy in self.hops[2]:
+                copy.start()
+            self.cores[0].start()
+        elif tile % 2 == 1:
+            self.cores[tile // 2].wait_recv()
+            if tile == 1:
+                for copy in self.hops[4]:
+                    copy.start()
+        else:
+            for copy in self.hops[tile]:
+                copy.wait_recv()
+            if tile == 2:
+                for copy in self.hops[6]:
+                    copy.start()
+            self.cores[tile // 2].start()
+
+    def finish(self):
+        for copies in self.hops.values():
+            for copy in copies:
+                copy.wait_send()
+        for copy in self.cores:
+            copy.wait_send()
+
+
+def gather_sems():
+    dma = pltpu.SemaphoreType.DMA
+    return [dma((3, 2)), dma((3, 2)), dma((4,)), dma((4,))]
+
+
+class TileScatter:
+    def __init__(self, parts, core_buf, chip_buf, send_sem, recv_sem, core_send, core_recv):
+        me = lax.axis_index("ctx")
+        self.parts, self.core_buf, self.chip_buf = parts, core_buf, chip_buf
+        self.hops = {
+            source: [
+                tile_copy(
+                    parts.at[source],
+                    chip_buf.at[source // 2 - 1],
+                    half,
+                    (first, 3 - first)[half],
+                    me,
+                    send_sem.at[source // 2 - 1],
+                    recv_sem.at[source // 2 - 1],
+                )
+                for half in range(2)
+            ]
+            for source, first in ((6, 1), (4, 2), (2, 1))
+        }
+        self.cores = [
+            core_copy(parts.at[2 * i + 1], core_buf.at[i], me, core_send.at[i], core_recv.at[i])
+            for i in range(4)
+        ]
+
+    def add(self, tile, buf):
+        here = self.parts.at[tile]
+        add_into(here, here, buf, here.shape[0], 32)
+
+    def after(self, tile):
+        if tile % 2 == 1:
+            self.cores[tile // 2].start()
+            return
+        self.cores[tile // 2].wait_recv()
+        self.add(tile, self.core_buf.at[tile // 2])
+        if tile == 6 or tile == 2:
+            for copy in self.hops[tile]:
+                copy.start()
+        if tile == 2:
+            self.pass_on()
+
+    def pass_on(self):
+        for copy in self.hops[6]:
+            copy.wait_recv()
+        self.add(4, self.chip_buf.at[2])
+        for copy in self.hops[4]:
+            copy.start()
+
+    def finish(self, out):
+        for tile in (2, 4):
+            for copy in self.hops[tile]:
+                copy.wait_recv()
+        rows = out.shape[0]
+
+        @pl.loop(0, rows // 32)
+        def _(i):
+            at = pl.ds(pl.multiple_of(i * 32, 32), 32)
+            out[at] = (
+                self.parts[0, at].astype(jnp.float32)
+                + self.chip_buf[0, at].astype(jnp.float32)
+                + self.chip_buf[1, at].astype(jnp.float32)
+            )
+
+        for copies in self.hops.values():
+            for copy in copies:
+                copy.wait_send()
+        for copy in self.cores:
+            copy.wait_send()
+
+
+def scatter_scratch(rows, width):
+    return [
+        pltpu.VMEM((8, rows, width), jnp.bfloat16),
+        pltpu.VMEM((4, rows, width), jnp.bfloat16),
+        pltpu.VMEM((3, rows, width), jnp.bfloat16),
+    ] + gather_sems()
+
+
+def produce_run(produce, count, *refs):
+    inputs, (out, *scratch) = refs[:count], refs[count:]
+    me = lax.axis_index("ctx")
+    scatter = TileScatter(*scratch)
+    for tile in range(7, -1, -1):
+        scatter.parts[tile] = produce(inputs, tile, me).astype(jnp.bfloat16)
+        scatter.after(tile)
+        yield
+    scatter.finish(out)
+
+
+def produce_op(produce, rows, width, *inputs):
+    return dict(
+        run=functools.partial(produce_run, produce, len(inputs)),
+        inputs=list(inputs),
+        in_space=pltpu.VMEM,
+        outs=[jax.ShapeDtypeStruct((rows, width), jnp.float32)],
+        out_space=pltpu.VMEM,
+        scratch=scatter_scratch(rows, width),
+        moved=32 * rows * width,
+    )
+
+
+def tile_rows(ref, tile, me):
+    half = ref.shape[1] // 2
+    return jnp.concatenate(
+        [ref[flipped(me, tile, 3), :half], ref[flipped(me, swapped(tile), 3), half:]], 0
+    )
+
+
+def product_of_rows(refs, tile, me):
+    return times_transposed(tile_rows(refs[0], tile, me), refs[1][...])
+
+
+def product_of_tiles(refs, tile, me):
+    return jnp.dot(refs[0][tile], refs[1][...], preferred_element_type=jnp.float32)
+
+
+def product_of_columns(refs, tile, me):
+    return jnp.dot(
+        tile_rows(refs[0], tile, me), refs[1][...], preferred_element_type=jnp.float32
+    )
+
+
+def unpack_both_kernel(segments, count, source, gate, up):
+    hidden_size = source.shape[2] // 2
+    main = hidden_size // 128 * 128
+    strip = hidden_size // segments
+    for out, first, last in ((gate, 0, 2 * main), (up, main, main + hidden_size)):
+        owners = [
+            jnp.concatenate(
+                [
+                    source[owner, :, first : first + main],
+                    source[owner, :, last : last + hidden_size - main],
+                ],
+                1,
+            )
+            for owner in range(count)
+        ]
+        out[...] = jnp.concatenate(
+            [
+                rows[:, segment * strip : (segment + 1) * strip]
+                for segment in range(segments)
+                for rows in owners
+            ],
+            1,
+        ).astype(jnp.float32)
+
+
+def unpack_both(gathered, segments):
+    count, rows, width = gathered.shape
+    step = 64
+    block = pl.BlockSpec((step, count * width // 2), lambda i: (i, 0))
+    return pl.pallas_call(
+        functools.partial(unpack_both_kernel, segments, count),
+        grid=(rows // step,),
+        in_specs=[pl.BlockSpec((count, step, width), lambda i: (0, i, 0))],
+        out_specs=[block, block],
+        out_shape=[jax.ShapeDtypeStruct((rows, count * width // 2), jnp.float32)] * 2,
+        compiler_params=pltpu.CompilerParams(vmem_limit_bytes=32 << 20),
+        cost_estimate=pl.CostEstimate(
+            flops=0, bytes_accessed=6 * gathered.size, transcendentals=0
+        ),
+    )(gathered)
+
+
+def greet_near(size):
+    me = lax.axis_index("ctx")
+    bits = size.bit_length() - 1
+    greet([flipped(me, 1 << bit, bits) for bit in range(bits)])
+
+
+def forward_kernel(
+    hidden_size,
+    normed,
+    weights,
+    grads,
+    normed_t,
+    values,
+    hidden,
+    grad_down,
+    tiles,
+    weights_buf,
+    grads_buf,
+    turned,
+    values_buf,
+    hidden_t,
+    load_sem,
+    out_sem,
+    *sems,
+):
+    greet_near(8)
+    own = pltpu.make_async_copy(normed, tiles.at[0], load_sem.at[0])
+    load = pltpu.make_async_copy(weights, weights_buf, load_sem.at[1])
+    own.start()
+    load.start()
+    pltpu.make_async_copy(grads, grads_buf, load_sem.at[2]).start()
+    own.wait()
+    gather = TileGather(tiles, *sems)
+    rows = tiles.shape[1]
+    main = hidden_size // 128 * 128
+
+    def write_out(tile, slot):
+        at = pl.ds(pl.multiple_of(tile * rows, rows), rows)
+        return [
+            pltpu.make_async_copy(values_buf.at[slot], values.at[tile], out_sem.at[0, slot]),
+            pltpu.make_async_copy(turned.at[slot], normed_t.at[:, at], out_sem.at[1, slot]),
+        ]
+
+    @pl.loop(0, 8)
+    def _(t):
+        for tile in range(8):
+
+            @pl.when(t == tile)
+            def _():
+                gather.before(tile)
+                if tile == 0:
+                    load.wait()
+
+        slot = t % 2
+
+        @pl.when(t >= 2)
+        def _():
+            for copy in write_out(t - 2, slot):
+                copy.wait()
+
+        here = tiles[t]
+        value = jnp.dot(here, weights_buf[...], preferred_element_type=jnp.float32)
+        values_buf[slot] = value
+        gate, up = value[:, :main], value[:, main : 2 * main]
+        front = gate * jax.nn.sigmoid(gate) * up
+        last = value[:, 2 * main :]
+        behind = last * jax.nn.sigmoid(last) * pltpu.roll(last, 64, 1)
+        both = jnp.concatenate([front, behind], 1)
+        hidden[t] = both[:, :hidden_size].astype(jnp.bfloat16)
+        at = pl.ds(pl.multiple_of(t * rows, rows), rows)
+        hidden_t[:, at] = jnp.transpose(both)[:hidden_size].astype(jnp.bfloat16)
+        turned[slot] = jnp.transpose(here)
+        for copy in write_out(t, slot):
+            copy.start()
+
+    pltpu.make_async_copy(grads, grads_buf, load_sem.at[2]).wait()
+    width = grads_buf.shape[2]
+    step = 256
+
+    @pl.loop(0, width // step)
+    def _(i):
+        at = pl.ds(pl.multiple_of(i * step, step), step)
+        grad_down[:, at] = jnp.dot(
+            hidden_t[...],
+            grads_buf[:, :, at].reshape(8 * rows, step),
+            preferred_element_type=jnp.float32,
+        ).astype(jnp.bfloat16)
+
+    for tile in (6, 7):
+        for copy in write_out(tile, tile % 2):
+            copy.wait()
+    gather.finish()
+
+
+def forward_mlp(normed, weights, grads, hidden_size, collective_id):
+    rows, width = normed.shape
+    wide = weights.shape[1]
+    any_space = pl.BlockSpec(memory_space=pl.ANY)
+    vmem = pl.BlockSpec(memory_space=pltpu.VMEM)
+    low = jnp.bfloat16
+    dma = pltpu.SemaphoreType.DMA
+    return pl.pallas_call(
+        functools.partial(forward_kernel, hidden_size),
+        in_specs=[any_space] * 3,
+        out_specs=[any_space, any_space, vmem, vmem],
+        out_shape=[
+            jax.ShapeDtypeStruct((width, 8 * rows), low),
+            jax.ShapeDtypeStruct((8, rows, wide), jnp.float32),
+            jax.ShapeDtypeStruct((8, rows, hidden_size), low),
+            jax.ShapeDtypeStruct((hidden_size, width), low),
+        ],
+        scratch_shapes=[
+            pltpu.VMEM((8, rows, width), low),
+            pltpu.VMEM(weights.shape, low),
+            pltpu.VMEM((8, rows, width), low),
+            pltpu.VMEM((2, width, rows), low),
+            pltpu.VMEM((2, rows, wide), jnp.float32),
+            pltpu.VMEM((hidden_size, 8 * rows), low),
+            dma((3,)),
+            dma((2, 2)),
+        ]
+        + gather_sems(),
+        compiler_params=pltpu.CompilerParams(
+            collective_id=collective_id, has_side_effects=True, vmem_limit_bytes=60 << 20
+        ),
+        cost_estimate=pl.CostEstimate(
+            flops=16 * rows * width * (wide + hidden_size),
+            bytes_accessed=64 * rows * width,
+            transcendentals=0,
+        ),
+    )(normed, weights, grads)
+
+
+def backward_kernel(
+    hidden_size,
+    grads,
+    values,
+    weights,
+    down,
+    normed_t,
+    grad_normed,
+    grad_both_w,
+    grads_buf,
+    values_buf,
+    weights_buf,
+    down_buf,
+    normed_buf,
+    grad_both,
+    out_buf,
+    load_sem,
+    tile_sem,
+    out_sem,
+    *scatter_refs,
+):
+    greet_near(8)
+    scatter = TileScatter(*scatter_refs)
+    rows = grads_buf.shape[1]
+    main = hidden_size // 128 * 128
+    load_weights = pltpu.make_async_copy(weights, weights_buf, load_sem.at[0])
+    load_down = pltpu.make_async_copy(down, down_buf, load_sem.at[1])
+
+    def load_tile(tile, slot):
+        return [
+            pltpu.make_async_copy(grads.at[tile], grads_buf.at[slot], tile_sem.at[0, slot]),
+            pltpu.make_async_copy(values.at[tile], values_buf.at[slot], tile_sem.at[1, slot]),
+        ]
+
+    def load_chunk(i):
+        at = pl.ds(pl.multiple_of(i * rows, rows), rows)
+        return pltpu.make_async_copy(normed_t.at[at], normed_buf.at[i % 2], tile_sem.at[2, i % 2])
+
+    load_down.start()
+    for copy in load_tile(7, 1):
+        copy.start()
+    load_weights.start()
+    load_chunk(0).start()
+
+    @pl.loop(0, 8)
+    def _(u):
+        t = 7 - u
+        slot = t % 2
+
+        @pl.when(u < 7)
+        def _():
+            for copy in load_tile(t - 1, 1 - slot):
+                copy.start()
+
+        @pl.when(u == 0)
+        def _():
+            load_down.wait()
+
+        for copy in load_tile(t, slot):
+            copy.wait()
+        grad_hidden = lax.dot_general(
+            grads_buf[slot],
+            down_buf[...],
+            (((1,), (1,)), ((), ())),
+            preferred_element_type=jnp.float32,
+        )
+        value = values_buf[slot]
+        gate, up, above = value[:, :main], value[:, main : 2 * main], grad_hidden[:, :main]
+        sigmoid = jax.nn.sigmoid(gate)
+        grad_both[t, :, :main] = (
+            above * up * sigmoid * (1.0 + gate * (1.0 - sigmoid))
+        ).astype(jnp.bfloat16)
+        grad_both[t, :, main : 2 * main] = (above * (gate * sigmoid)).astype(jnp.bfloat16)
+        last = value[:, 2 * main :]
+        above = grad_hidden[:, main:]
+        above = jnp.concatenate([above, jnp.zeros_like(above)], 1)
+        sigmoid = jax.nn.sigmoid(last)
+        to_gate = above * pltpu.roll(last, 64, 1) * sigmoid * (1.0 + last * (1.0 - sigmoid))
+        to_up = pltpu.roll(above * (last * sigmoid), 64, 1)
+        lane = lax.broadcasted_iota(jnp.int32, last.shape, 1)
+        grad_both[t, :, 2 * main :] = jnp.where(lane < 64, to_gate, to_up).astype(jnp.bfloat16)
+
+        @pl.when(u == 0)
+        def _():
+            load_weights.wait()
+
+        scatter.parts[t] = lax.dot_general(
+            grad_both[t],
+            weights_buf[...],
+            (((1,), (1,)), ((), ())),
+            preferred_element_type=jnp.float32,
+        ).astype(jnp.bfloat16)
+        for tile in range(8):
+
+            @pl.when(t == tile)
+            def _():
+                scatter.after(tile)
+
+    chunks = normed_t.shape[0] // rows
+
+    def store_chunk(i):
+        at = pl.ds(pl.multiple_of(i * rows, rows), rows)
+        return pltpu.make_async_copy(out_buf.at[i % 2], grad_both_w.at[at], out_sem.at[i % 2])
+
+    @pl.loop(0, chunks)
+    def _(i):
+        @pl.when(i < chunks - 1)
+        def _():
+            load_chunk(i + 1).start()
+
+        load_chunk(i).wait()
+
+        @pl.when(i >= 2)
+        def _():
+            store_chunk(i - 2).wait()
+
+        out_buf[i % 2] = jnp.dot(
+            normed_buf[i % 2],
+            grad_both[...].reshape(8 * rows, grad_both.shape[2]),
+            preferred_element_type=jnp.float32,
+        ).astype(jnp.bfloat16)
+        store_chunk(i).start()
+
+    store_chunk(chunks - 2).wait()
+    store_chunk(chunks - 1).wait()
+    scatter.finish(grad_normed)
+
+
+def backward_mlp(grads, values, weights, down, normed_t, collective_id):
+    size, rows, width = grads.shape
+    hidden_size = down.shape[0]
+    wide = weights.shape[1]
+    any_space = pl.BlockSpec(memory_space=pl.ANY)
+    vmem = pl.BlockSpec(memory_space=pltpu.VMEM)
+    low = jnp.bfloat16
+    dma = pltpu.SemaphoreType.DMA
+    return pl.pallas_call(
+        functools.partial(backward_kernel, hidden_size),
+        in_specs=[any_space] * 5,
+        out_specs=[vmem, any_space],
+        out_shape=[
+            jax.ShapeDtypeStruct((rows, width), jnp.float32),
+            jax.ShapeDtypeStruct((width, wide), low),
+        ],
+        scratch_shapes=[
+            pltpu.VMEM((2, rows, width), low),
+            pltpu.VMEM((2, rows, wide), jnp.float32),
+            pltpu.VMEM(weights.shape, low),
+            pltpu.VMEM(down.shape, low),
+            pltpu.VMEM((2, rows, 8 * rows), low),
+            pltpu.VMEM((8, rows, wide), low),
+            pltpu.VMEM((2, rows, wide), low),
+            dma((2,)),
+            dma((3, 2)),
+            dma((2,)),
+        ]
+        + scatter_scratch(rows, width),
+        compiler_params=pltpu.CompilerParams(
+            collective_id=collective_id, has_side_effects=True, vmem_limit_bytes=60 << 20
+        ),
+        cost_estimate=pl.CostEstimate(
+            flops=16 * rows * width * (2 * wide + hidden_size),
+            bytes_accessed=64 * rows * width,
+            transcendentals=0,
+        ),
+    )(grads, values, weights, down, normed_t)
 
 
 def unpack_kernel(segments, count, source, out):
@@ -445,9 +1195,6 @@
     lowest,
     projected,
     starts,
-    cosine,
-    sine_low,
-    sine_high,
     qkv,
     attended,
     mixed,
@@ -465,14 +1212,8 @@
     def _(p):
         at = pl.ds(pl.multiple_of(p * block, block), block)
         rows = projected[pl.ds(pl.multiple_of(order[p] * block, block), block)]
-        tables = (cosine[at], sine_low[at], sine_high[at])
-        query = turn(rows[:, :cols], *tables, cols) * HEAD ** (-0.5)
-        key = turn(rows[:, cols : 2 * cols], *tables, cols)
-        value = rows[:, 2 * cols :]
-        qkv[at, :cols] = query.astype(jnp.bfloat16)
-        qkv[at, cols : 2 * cols] = key.astype(jnp.bfloat16)
-        qkv[at, 2 * cols :] = value.astype(jnp.bfloat16)
-        value_t[:, at] = jnp.transpose(value).astype(jnp.bfloat16)
+        qkv[at] = rows
+        value_t[:, at] = transposed(rows[:, 2 * cols :])
 
     @pl.loop(0, seq // tile)
     def _(i):
@@ -518,7 +1259,7 @@
             mixed[place] = rows[part * block : (part + 1) * block].astype(jnp.bfloat16)
 
 
-def attend(projected, order, lowest, starts, tables, heads):
+def attend(projected, order, lowest, starts, heads):
     seq, wide = projected.shape
     cols = wide // 3
     block = seq // order.shape[0]
@@ -527,7 +1268,7 @@
     smem = pl.BlockSpec(memory_space=pltpu.SMEM)
     return pl.pallas_call(
         functools.partial(attend_kernel, block, heads),
-        in_specs=[smem, smem] + [vmem] * 5,
+        in_specs=[smem, smem] + [vmem] * 2,
         out_specs=[vmem] * 4,
         out_shape=[
             jax.ShapeDtypeStruct((seq, wide), jnp.bfloat16),
@@ -545,7 +1286,7 @@
         cost_estimate=pl.CostEstimate(
             flops=4 * seq * seq * cols, bytes_accessed=12 * seq * cols, transcendentals=0
         ),
-    )(order, lowest, projected, starts, *tables)
+    )(order, lowest, projected, starts)
 
 
 def attend_back_kernel(
@@ -589,7 +1330,7 @@
         sums[:, columns] += jnp.sum(low.astype(jnp.float32), 0, keepdims=True)
 
     def turned_back(p, rows):
-        at = pl.ds(pl.multiple_of(p * block, block), block)
+        at = pl.ds(pl.multiple_of(order[p] * block, block), block)
         return turn(rows, cosine[at], -sine_low[at], -sine_high[at], cols)
 
     @pl.loop(0, seq // tile)
@@ -681,11 +1422,11 @@
     )(order, lowest, qkv, grad_mixed, attended, log_total, starts, *tables)
 
 
-def rotary_tables(seq):
+def rotary_tables(places):
     lane = jnp.arange(128, dtype=jnp.int32)[None, :] % HEAD
     half_rot = ROT // 2
     freq = ROTARY_BASE ** (-(lane % half_rot).astype(jnp.float32) * 2.0 / ROT)
-    angles = jnp.arange(seq, dtype=jnp.int32).astype(jnp.float32)[:, None] * freq
+    angles = places.astype(jnp.float32)[:, None] * freq
     sine = jnp.sin(angles)
     return (
         jnp.where(lane < ROT, jnp.cos(angles), 1.0),
@@ -762,16 +1503,10 @@
     starts = document_starts(doc_ids[0])
     lowest = starts[::tile] // tile
     starts = starts[None]
-    tables = rotary_tables(seq_rows)
-
-    small = lax.all_gather(
-        jnp.concatenate([ln1_gain, ln1_bias, ln2_gain, ln2_bias, b_qkv]), "fsdp", axis=0
-    ).astype(jnp.float32)
-    gain_one, shift_one, gain_two, shift_two = (
-        small[:, i * shard_rows : (i + 1) * shard_rows].reshape(1, width) for i in range(4)
-    )
-    bias_full = small[:, 4 * shard_rows :].reshape(3, ctx_size, cols)
-    bias_here = lax.dynamic_index_in_dim(bias_full, position, 1, keepdims=False).reshape(3 * cols)
+    device_blocks = jnp.stack([block_pairs, 2 * ctx_size - 1 - block_pairs], 1).reshape(-1, 1)
+    half_rows = rows_here // 2
+    places = device_blocks * half_rows + jnp.arange(half_rows, dtype=jnp.int32)[None, :]
+    tables = rotary_tables(places.reshape(-1))
 
     def strips(w, count, size):
         stride = w.shape[1] // count
@@ -781,40 +1516,47 @@
         ]
 
     qkv_strip = jnp.concatenate(strips(w_qkv, 3, cols), 1)
+    hidden_here = fsdp_size * strip
+    main = hidden_here // 128 * 128
+    fused = ctx_size == 8 and hidden_here - main == 64 and rows_here == 256
+    gate_strip = jnp.concatenate(strips(w_gate, fsdp_size, strip), 1)
+    up_strip = jnp.concatenate(strips(w_up, fsdp_size, strip), 1)
     both_strip = jnp.concatenate(
-        strips(w_gate, fsdp_size, strip) + strips(w_up, fsdp_size, strip), 1
+        [gate_strip[:, :main], up_strip[:, :main], gate_strip[:, main:], up_strip[:, main:]], 1
     )
     down_strip = lax.dynamic_slice_in_dim(w_down, position * strip, strip, 0)
     out_piece = shard_rows // ctx_size
     out_strip = lax.dynamic_slice_in_dim(w_out, position * out_piece, out_piece, 0)
-    hidden_here = fsdp_size * strip
-
-    out_here = lax.all_gather(out_strip, "fsdp", axis=0)
     qkv_here = lax.all_gather(qkv_strip, "fsdp", axis=0, tiled=True)
     both_here = lax.all_gather(both_strip, "fsdp", axis=0, tiled=True)
     down_here = lax.all_gather(down_strip, "fsdp", axis=0, tiled=True)
 
+    small = jnp.concatenate([ln1_gain, ln1_bias, ln2_gain, ln2_bias, b_qkv])
+    small_rows = -(-small.size // 2048) * 16
+    small = jnp.pad(small, (0, small_rows * 128 - small.size)).reshape(small_rows, 128)
     grad_out = cotangent[0]
-    tokens_all, grad_out_all = plane(
-        ctx_size, 1, gather_op(tokens[0], ctx_size), gather_op(grad_out, ctx_size)
-    )
-    tokens_all = tokens_all.reshape(seq_rows, width)
-    grad_out_all = grad_out_all.reshape(seq_rows, width)
-    tokens_in = tokens[0].astype(jnp.float32)
-    normed, unit_one, inverse_one = norm_rows(tokens_in, gain_one, shift_one)
-    normed_all = norm_rows(tokens_all.astype(jnp.float32), gain_one, shift_one)[0].astype(
-        jnp.bfloat16
-    )
-    projected = times(normed_all, qkv_here) + bias_here
-    qkv_rows, attended, mixed_here, log_total = attend(
-        projected, order, lowest, starts, tables, heads_here
-    )
-    mixed_here = mixed_here.reshape(ctx_size, rows_here, cols)
-    to_columns = functools.partial(column_view, width=cols)
-    mixed_rows, out_full = plane(
+    gather_grads = gather_op(grad_out, ctx_size)
+    if fused:
+        gather_grads = gather_op(grad_out, ctx_size, row_half, tile_put, relative=True)
+    small, out_here, tokens_all, grad_out_all = plane(
+        ctx_size,
+        1,
+        z_gather_op(small, fsdp_size),
+        z_gather_op(out_strip, fsdp_size),
+        gather_op(tokens[0], ctx_size),
+        gather_grads,
+    )
+    small = small.reshape(fsdp_size, small_rows * 128).astype(jnp.float32)
+    gain_one, shift_one, gain_two, shift_two = (
+        small[:, i * shard_rows : (i + 1) * shard_rows].reshape(1, width) for i in range(4)
+    )
+    bias_full = small[:, 4 * shard_rows : 4 * shard_rows + b_qkv.size]
+    bias_full = bias_full.reshape(3, ctx_size, cols)
+    bias_here = lax.dynamic_index_in_dim(bias_full, position, 1, keepdims=False)
+    bias_here = bias_here.reshape(1, 3 * cols)
+    out_full, projected, normed_all = plane(
         ctx_size,
         2,
-        exchange_op(mixed_here, ctx_size, (rows_here, width), block_view, to_columns),
         gather_op(
             out_here,
             ctx_size,
@@ -822,33 +1564,63 @@
             middle_columns,
             (fsdp_size, ctx_size, out_piece, width),
         ),
+        project_op(tokens_all, qkv_here, gain_one, shift_one, bias_here, tables),
     )
     out_full = out_full.reshape(width, width)
+    normed_all = normed_all.reshape(seq_rows, width)
+    tokens_in = tokens[0].astype(jnp.float32)
+    unit_one, inverse_one = norm_rows(tokens_in, gain_one, shift_one)[1:]
+    qkv_rows, attended, mixed_here, log_total = attend(
+        projected.reshape(seq_rows, 3 * cols), order, lowest, starts, heads_here
+    )
+    mixed_here = mixed_here.reshape(ctx_size, rows_here, cols)
+    to_columns = functools.partial(column_view, width=cols)
+    mixed_rows = plane(
+        ctx_size,
+        12,
+        exchange_op(mixed_here, ctx_size, (rows_here, width), block_view, to_columns),
+    )
     residual = tokens_in + times(mixed_rows, out_full)
     normed_two, unit_two, inverse_two = norm_rows(residual, gain_two, shift_two)
-    normed_two_all = plane(ctx_size, 3, gather_op(normed_two.astype(jnp.bfloat16), ctx_size))
-    normed_two_all = normed_two_all.reshape(seq_rows, width)
-    both_value = times(normed_two_all, both_here)
-    gate_value = both_value[:, :hidden_here]
-    up_value = both_value[:, hidden_here:]
-    sigmoid_gate = jax.nn.sigmoid(gate_value)
-    silu_gate = gate_value * sigmoid_gate
-    hidden = (silu_gate * up_value).astype(jnp.bfloat16)
-
     def blocks(rows):
         return rows.astype(jnp.bfloat16).reshape(ctx_size, rows_here, width)
 
-    grad_down_w = inner(hidden, grad_out_all).astype(jnp.bfloat16)
-    grad_hidden = times_transposed(after(grad_out_all, grad_down_w), down_here)
-    grad_gate = grad_hidden * up_value * sigmoid_gate * (1.0 + gate_value * (1.0 - sigmoid_gate))
-    grad_up = grad_hidden * silu_gate
-    grad_both = jnp.concatenate([grad_gate, grad_up], 1).astype(jnp.bfloat16)
-    grad_both_w = inner(normed_two_all, grad_both).astype(jnp.bfloat16)
-    grad_normed_two = plane(
-        ctx_size,
-        4,
-        scatter_op(blocks(times_transposed(after(grad_both, grad_both_w), both_here)), ctx_size),
-    )
+    normed_two_low = normed_two.astype(jnp.bfloat16)
+    if fused:
+        normed_two_t, both_value, hidden, grad_down_w = forward_mlp(
+            normed_two_low, both_here, grad_out_all, hidden_here, 3
+        )
+        grad_normed_two, grad_both_w = backward_mlp(
+            grad_out_all, both_value, both_here, down_here, normed_two_t, 4
+        )
+    else:
+        grad_out_all = grad_out_all.reshape(seq_rows, width)
+        normed_two_all = plane(ctx_size, 3, gather_op(normed_two_low, ctx_size))
+        normed_two_all = normed_two_all.reshape(seq_rows, width)
+        both_value = times(normed_two_all, both_here)
+        gate_value = jnp.concatenate(
+            [both_value[:, :main], both_value[:, 2 * main : main + hidden_here]], 1
+        )
+        up_value = jnp.concatenate(
+            [both_value[:, main : 2 * main], both_value[:, main + hidden_here :]], 1
+        )
+        sigmoid_gate = jax.nn.sigmoid(gate_value)
+        silu_gate = gate_value * sigmoid_gate
+        hidden = (silu_gate * up_value).astype(jnp.bfloat16)
+
+        grad_down_w = inner(hidden, grad_out_all).astype(jnp.bfloat16)
+        grad_hidden = times_transposed(after(grad_out_all, grad_down_w), down_here)
+        grad_gate = grad_hidden * up_value * sigmoid_gate * (1.0 + gate_value * (1.0 - sigmoid_gate))
+        grad_up = grad_hidden * silu_gate
+        grad_both = jnp.concatenate(
+            [grad_gate[:, :main], grad_up[:, :main], grad_gate[:, main:], grad_up[:, main:]], 1
+        ).astype(jnp.bfloat16)
+        grad_both_w = inner(normed_two_all, grad_both).astype(jnp.bfloat16)
+        grad_normed_two = plane(
+            ctx_size,
+            4,
+            scatter_op(blocks(times_transposed(after(grad_both, grad_both_w), both_here)), ctx_size),
+        )
     grad_residual = grad_out.astype(jnp.float32) + norm_back(
         grad_normed_two, unit_two, inverse_two, gain_two
     )
@@ -873,32 +1645,56 @@
         heads_here,
     )
     grad_qkv_w = inner(normed_all, grad_projected).astype(jnp.bfloat16)
-    mixed_blocks = jnp.transpose(
-        mixed_rows.reshape(rows_here, fsdp_size, ctx_size, out_piece), (0, 2, 1, 3)
-    ).reshape(rows_here, width)
-    grad_normed, grad_out_w = plane_groups(
-        ctx_size,
-        6,
-        scatter_op(
-            blocks(times_transposed(after(grad_projected, grad_qkv_w), qkv_here)), ctx_size
-        ),
-        scatter_op(
+
+    def reduced(grad):
+        return lax.psum_scatter(
+            grad.astype(jnp.bfloat16), "fsdp", scatter_dimension=0, tiled=True
+        )
+
+    hidden = after(hidden, grad_qkv_w)
+    grad_down_w, grad_both_w = reduced(grad_down_w), reduced(grad_both_w)
+    if fused:
+        mixed_t = jnp.transpose(
+            mixed_rows.reshape(rows_here, fsdp_size, ctx_size, out_piece), (2, 1, 3, 0)
+        ).reshape(ctx_size, fsdp_size * out_piece, rows_here)
+        layer_op = produce_op(product_of_tiles, rows_here, width, hidden, down_here)
+        out_op = produce_op(product_of_columns, rows_here, width, mixed_t, grad_branch)
+    else:
+        mixed_blocks = jnp.transpose(
+            mixed_rows.reshape(rows_here, fsdp_size, ctx_size, out_piece), (0, 2, 1, 3)
+        ).reshape(rows_here, width)
+        layer_op = scatter_op(blocks(times(hidden, down_here)), ctx_size)
+        out_op = scatter_op(
             inner(mixed_blocks, after(grad_branch, grad_qkv_w))
             .astype(jnp.bfloat16)
             .reshape(ctx_size, fsdp_size * out_piece, width),
             ctx_size,
-        ),
+        )
+    grad_down_w, layer_part, grad_out_w = plane_groups(
+        ctx_size,
+        6,
+        gather_op(grad_down_w, ctx_size, column_half, stacked_columns),
+        layer_op,
+        out_op,
+    )
+    layer_out = residual + layer_part
+    grad_qkv_w = reduced(after(grad_qkv_w, layer_part, grad_both_w))
+    grad_projected = after(grad_projected, layer_part)
+    if fused:
+        normed_op = produce_op(
+            product_of_rows,
+            rows_here,
+            width,
+            grad_projected.reshape(ctx_size, rows_here, 3 * cols),
+            qkv_here,
+        )
+    else:
+        normed_op = scatter_op(blocks(times_transposed(grad_projected, qkv_here)), ctx_size)
+    grad_both_w, grad_normed = plane_groups(
+        ctx_size, 9, gather_op(grad_both_w, ctx_size), normed_op
     )
     grad_tokens = grad_residual + norm_back(grad_normed, unit_one, inverse_one, gain_one)
 
-    def reduced(grad):
-        return lax.psum_scatter(
-            grad.astype(jnp.bfloat16), "fsdp", scatter_dimension=0, tiled=True
-        )
-
-    grad_down_w = reduced(grad_down_w)
-    grad_both_w = reduced(grad_both_w)
-    grad_qkv_w = reduced(grad_qkv_w)
     norm_sums = jnp.stack(
         [
             jnp.sum(grad_normed * unit_one, 0),
@@ -922,25 +1718,18 @@
     grad_out_w = jnp.concatenate(
         [grad_out_w.reshape(fsdp_size, out_piece, width)] + padded, 1
     )
-    grad_out_w = reduced(grad_out_w.reshape(fsdp_size * (out_piece + 16), width))
-    layer_part, grad_down_w, grad_both_w = plane_groups(
-        ctx_size,
-        8,
-        scatter_op(blocks(times(after(hidden, grad_normed), down_here)), ctx_size),
-        gather_op(grad_down_w, ctx_size, column_half, stacked_columns),
-        gather_op(grad_both_w, ctx_size),
-    )
-    layer_out = residual + layer_part
+    grad_out_w = grad_out_w.astype(jnp.bfloat16)
     grad_out_w, grad_qkv_w = plane(
         ctx_size,
-        10,
-        gather_op(after(grad_out_w, grad_down_w), ctx_size, column_half, stacked_columns),
+        13,
+        z_sum_gather_op(grad_out_w, fsdp_size, ctx_size),
         gather_op(grad_qkv_w, ctx_size),
     )
     sums = jnp.sum(grad_out_w[:, out_piece : out_piece + 2].astype(jnp.float32), 0)
     norm_sums = sums[0, : 4 * shard_rows].reshape(4, shard_rows)
     bias_sums = sums[1, : b_qkv.shape[0]]
     grad_out_w = grad_out_w[:, :out_piece]
+    grad_gate_w, grad_up_w = unpack_both(grad_both_w, fsdp_size)
     float32 = jnp.float32
     return (
         layer_out.astype(jnp.bfloat16)[None],
@@ -952,8 +1741,8 @@
         grad_out_w.reshape(w_out.shape).astype(float32),
         norm_sums[2],
         norm_sums[3],
-        unpack_columns(grad_both_w[:, :, :hidden_here], fsdp_size),
-        unpack_columns(grad_both_w[:, :, hidden_here:], fsdp_size),
+        grad_gate_w,
+        grad_up_w,
         grad_down_w.reshape(w_down.shape).astype(float32),
     )
 

time: 861 us -> 721 us (0.84)
  matrix products: 140 us -> 25.2 us
  other arithmetic: 66.3 us -> 39 us
  Pallas kernels: 571 us -> 598 us
  blocking collectives: 15.3 us -> 0 us
  local copies, waits for them, and re-layouts: 47.3 us -> 37.8 us
    pallas_call x8 -> x10, Pallas kernels: 486 us -> 532 us  [the longest x7 416 us: plane(): pl.pallas_call(functools.partial(plane_kernel, size, parts, far, z_size),...]
    dot_general x4 -> x1, matrix products: 48.5 us -> 6.81 us  [times_transposed(): lax.dot_general(left_side, right_side, (((1,), (1,)), ((), ())), preferre...]
    dot_general x4 -> x1, matrix products: 46.4 us -> 7.04 us  [times(): return jnp.dot(left_side, right_side, preferred_element_type=jnp.float32)]
    dot_general x4 -> x1, matrix products: 45.3 us -> 11.4 us  [inner(): lax.dot_general(left_side, right_side, (((0,), (0,)), ((), ())), preferre...]
    all_gather x1 -> x0, blocking collectives: 15.3 us -> none  [body(): lax.all_gather(jnp.concatenate([ln1_gain, ln1_bias, ln2_gain, ln2_bias, b...]
    convert_element_type x4 -> x2, other arithmetic: 15.4 us -> 1.5 us  [the longest x1 1.42 us: body(): normed_two_low = normed_two.astype(jnp.bfloat16)]
    pallas_call x3 -> x1, Pallas kernels: 18.6 us -> 5.72 us  [unpack_columns(): pl.pallas_call(functools.partial(unpack_kernel, segments, count), grid=(r...]
    slice x2, local copies, waits for them, and re-layouts: 13.1 us -> 1.83 us  [the longest x1 1.83 us: body(): gate_strip[:, main:]]
  transfers between devices with their start and end apart: 8 -> 6, of which waited for: 0 -> 0; matrix products, arithmetic and copies ran while one was open for 24% -> 11% of each run, Pallas kernels for 59% -> 76%
where the time goes in v3:
time: 721 us; the launch traced here: 715 us
  Pallas kernels  598 us (83%)
  other arithmetic  39 us (5%)
  local copies, waits for them, and re-layouts  37.8 us (5%)
  matrix products  25.2 us (3%)
  between operations  15 us (2%)
    pallas_call x7, Pallas kernels, plane(): pl.pallas_call(functools.partial(plane_kernel, size, parts, far, z_size),...  416 us
    pallas_call x1, Pallas kernels, backward_mlp(): pl.pallas_call(functools.partial(backward_kernel, hidden_size), in_specs=...  53.6 us
    pallas_call x1, Pallas kernels, forward_mlp(): pl.pallas_call(functools.partial(forward_kernel, hidden_size), in_specs=[...  53.5 us
    pallas_call x1, Pallas kernels, attend_back(): pl.pallas_call(functools.partial(attend_back_kernel, block, heads), in_sp...  34.5 us
    pallas_call x1, Pallas kernels, attend(): pl.pallas_call(functools.partial(attend_kernel, block, heads), in_specs=[...  25.7 us
    unnamed x65, local copies, waits for them, and re-layouts  16.1 us
  transfers between devices with their start and end apart: 6, of which 0 were waited for; matrix products, arithmetic and copies ran while one was open for 11% of the time, Pallas kernels for 76%

profile of v3, /device:TPU:0, one launch (start us, length us, event | category | flops | bytes accessed | tf_op | source)
XLA Modules:
  0.0 715.2 jit_solution(4677208285143175414)
XLA Ops:
  11.4 2.9 constant_dynamic-slice_fusion.5
  15.0 3.3 concatenate.25
  22.9 81.0 %shard_map.229 = (bf16[4,32,128]{2,1,0:T(8,128)(2,1)}, bf16[4,64,2048]{2,1,0:T(8,128)(2,1)}, bf16[8,256,2048]{2,1,0:T(8,128)(2,1)}, bf16[8,256,2048]{2,1,0:T(8,128)(2,1)}) custom-call(bf16[32,128]{1,0:T(8,128)(2,1)} %pad_bitcast_fusion.refs_0_, bf16[64,2048]{1,0:T(8,128)(2,1)} %constant_dynamic-slice_fusion.14.refs_1_, bf16[256,2048]{1,0:T(8,128)(2,1)} %bitcast.80, ...), custom_call_target="tpu_custom_call" | custom-call | bytes 34635776 | tf_op jit(solution)/shard_map/pallas_call | solution.py:529
  108.5 6.0 fusion.13
  115.1 55.2 %shard_map.230 = (bf16[4,8,64,2048]{3,2,1,0:T(8,128)(2,1)}, bf16[8,256,768]{2,1,0:T(8,128)(2,1)}, bf16[8,256,2048]{2,1,0:T(8,128)(2,1)}) custom-call(bf16[4,64,2048]{2,1,0:T(8,128)(2,1)} %get-tuple-element.43.refs_0_, bf16[8,256,2048]{2,1,0:T(8,128)(2,1)} %get-tuple-element.44.refs_1_, bf16[2048,768]{1,0:T(8,128)(2,1)} %all-gather.4.cloned.1.call-done.refs_2_, ...), custom_call_target="tpu_custom_call" | custom-call | bytes 33554432 | tf_op jit(solution)/shard_map/pallas_call | solution.py:529
  170.3 25.7 %shard_map.231 = (bf16[2048,768]{1,0:T(8,128)(2,1)}, f32[2048,256]{1,0:T(8,128)S(1)}, bf16[2048,256]{1,0:T(8,128)(2,1)S(1)}, f32[8,1,1024]{2,1,0:T(1,128)S(1)}) custom-call(s32[16]{0:T(128)S(1)} %select_reduce_fusion.order, s32[8]{0:T(128)S(1)} %and_select_fusion.2.lowest, bf16[2048,768]{1,0:T(8,128)(2,1)} %bitcast.106, ...), custom_call_target="tpu_custom_call" | custom-call | flops 4294967296 | bytes 6291456 | tf_op jit(solution)/shard_map/pallas_call | solution.py:1269
  198.3 13.7 %shard_map.232 = bf16[256,2048]{1,0:T(8,128)(2,1)} custom-call(bf16[8,256,256]{2,1,0:T(8,128)(2,1)} %bitcast.77), custom_call_target="tpu_custom_call" | custom-call | bytes 2097152 | tf_op jit(solution)/shard_map/pallas_call | solution.py:529
  212.0 7.0 fusion.28
  220.9 53.5 %shard_map.233 = (bf16[2048,2048]{1,0:T(8,128)(2,1)}, f32[8,256,1408]{2,1,0:T(8,128)}, bf16[8,256,704]{2,1,0:T(8,128)(2,1)}, bf16[704,2048]{1,0:T(8,128)(2,1)}) custom-call(bf16[256,2048]{1,0:T(8,128)(2,1)} %add_convert_fusion.1.normed, bf16[2048,1408]{1,0:T(8,128)(2,1)} %all-gather.6.cloned.1.call-done.weights, bf16[8,256,2048]{2,1,0:T(8,128)(2,1)} %get-tuple-element.49.grads), custom_call_target="tpu_custom_call" | custom-call | flops 17716740096 | bytes 33554432 | tf_op jit(solution)/shard_map/pallas_call | solution.py:916
  274.5 53.6 %shard_map.234 = (f32[256,2048]{1,0:T(8,128)}, bf16[2048,1408]{1,0:T(8,128)(2,1)}) custom-call(bf16[8,256,2048]{2,1,0:T(8,128)(2,1)} %get-tuple-element.49.grads, f32[8,256,1408]{2,1,0:T(8,128)} %get-tuple-element.54.values, bf16[2048,1408]{1,0:T(8,128)(2,1)} %all-gather.6.cloned.1.call-done.weights, ...), custom_call_target="tpu_custom_call" | custom-call | flops 29527900160 | bytes 33554432 | tf_op jit(solution)/shard_map/pallas_call | solution.py:1084
  337.6 6.8 convolution_convert_fusion.1.refs_0_
  344.4 14.1 %shard_map.235 = bf16[8,256,256]{2,1,0:T(8,128)(2,1)} custom-call(bf16[256,2048]{1,0:T(8,128)(2,1)} %convolution_convert_fusion.1.refs_0_), custom_call_target="tpu_custom_call" | custom-call | bytes 2097152 | tf_op jit(solution)/shard_map/pallas_call | solution.py:529
  359.8 34.5 %shard_map.236 = (bf16[2048,768]{1,0:T(8,128)(2,1)}, f32[1,768]{1,0:T(1,128)S(1)}) custom-call(s32[16]{0:T(128)S(1)} %select_reduce_fusion.order, s32[8]{0:T(128)S(1)} %and_select_fusion.2.lowest, bf16[2048,768]{1,0:T(8,128)(2,1)} %get-tuple-element.53.qkv, bf16[2048,256]{1,0:T(8,128)(2,1)S(1)} %bitcast.76, f32[2048,256]{1,0:T(8,128)} %copy-done.9, ...), custom_call_target="tpu_custom_call" | custom-call | flops 10737418240 | bytes 10485760 | tf_op jit(solution)/shard_map/pallas_call | solution.py:1403
  394.3 11.4 %convolution_convert_fusion = bf16[2048,768]{1,0:T(8,128)(2,1)} fusion(bf16[2048,2048]{1,0:T(8,128)(2,1)} %bitcast.103, bf16[2048,768]{1,0:T(8,128)(2,1)} %get-tuple-element.63), kind=kOutput, calls=%fused_computation.1 | convolution fusion | flops 6444023808 | bytes 14680064 | tf_op jit(solution)/shard_map/dot_general | solution.py:1453
  405.6 109.1 %shard_map.237 = (bf16[8,176,2048]{2,1,0:T(8,128)(2,1)}, f32[256,2048]{1,0:T(8,128)}, f32[256,2048]{1,0:T(8,128)}) custom-call(bf16[176,2048]{1,0:T(8,128)(2,1)} %reduce-scatter.4.cloned.1.call-done.refs_0_, bf16[8,256,704]{2,1,0:T(8,128)(2,1)} %get-tuple-element.60.refs_1_, bf16[704,2048]{1,0:T(8,128)(2,1)} %all-gather.8.cloned.1.call-done.down.refs_2_, ...), custom_call_target="tpu_custom_call" | custom-call | bytes 45088768 | tf_op jit(solution)/shard_map/pallas_call | solution.py:529
  520.3 3.2 fusion.18
  523.5 6.4 bitcast_convert_fusion
  529.9 95.4 %shard_map.238 = (bf16[8,512,1408]{2,1,0:T(8,128)(2,1)}, f32[256,2048]{1,0:T(8,128)}) custom-call(bf16[512,1408]{1,0:T(8,128)(2,1)} %reduce-scatter.6.cloned.1.call-done.refs_0_, bf16[8,256,768]{2,1,0:T(8,128)(2,1)} %bitcast.85, bf16[2048,768]{1,0:T(8,128)(2,1)} %all-gather.4.cloned.1.call-done.refs_2_), custom_call_target="tpu_custom_call" | custom-call | bytes 39845888 | tf_op jit(solution)/shard_map/pallas_call | solution.py:529
  628.0 4.3 copy-done.2
  632.3 8.9 %shard_map.241 = (f32[512,5632]{1,0:T(8,128)}, f32[512,5632]{1,0:T(8,128)}) custom-call(bf16[8,512,1408]{2,1,0:T(8,128)(2,1)S(1)} %copy-done.2), custom_call_target="tpu_custom_call" | custom-call | bytes 34603008 | tf_op jit(solution)/shard_map/pallas_call | solution.py:802
  645.4 47.2 %shard_map.239 = (bf16[8,80,2048]{2,1,0:T(8,128)(2,1)}, bf16[8,512,768]{2,1,0:T(8,128)(2,1)}) custom-call(bf16[4,80,2048]{2,1,0:T(8,128)(2,1)} %fusion.15.refs_0_, bf16[512,768]{1,0:T(8,128)(2,1)} %reduce-scatter.8.cloned.1.call-done.refs_1_), custom_call_target="tpu_custom_call" | custom-call | bytes 20447232 | tf_op jit(solution)/shard_map/pallas_call | solution.py:529
  696.7 2.8 copy-done.3
  699.5 5.7 shard_map.240
  705.2 2.7 bitcast_convert_fusion.1
  (142 shorter events, 45.7 us)
Async XLA Ops:
  7.2 15.0 %copy-start = (bf16[512,2048]{1,0:T(8,128)(2,1)S(1)}, bf16[512,2048]{1,0:T(8,128)(2,1)}, u32[]{:S(2)}) copy-start(bf16[512,2048]{1,0:T(8,128)(2,1)} %param.21) | copy-start | bytes 6291460
  7.2 107.9 %all-gather.4.cloned.1.call-start = ((), (), s32[]{:S(2)}) async-start(), calls=%async_computation.3 | async-start | bytes 3932160 | tf_op jit(solution)/shard_map/all_gather | solution.py:1530
  9.5 211.3 %all-gather.6.cloned.1.call-start = ((), (), s32[]{:S(2)}) async-start(), calls=%async_computation.4 | async-start | bytes 7208960 | tf_op jit(solution)/shard_map/all_gather | solution.py:1531
  18.3 2.6 copy-start.23
  18.3 2.8 copy-start.24
  18.3 3.0 copy-start.25
  18.3 3.2 copy-start.21
  18.3 256.2 %all-gather.8.cloned.1.call-start = ((), (), s32[]{:S(2)}) async-start(), calls=%async_computation.6 | async-start | bytes 3604480 | tf_op jit(solution)/shard_map/all_gather | solution.py:1532
  20.5 84.2 %copy-start.26 = (s32[8]{0:T(128)S(1)}, s32[8]{0:T(128)}, u32[]{:S(2)}) copy-start(s32[8]{0:T(128)} %param.16) | copy-start | bytes 100
  20.5 84.6 %copy-start.20 = (s32[1,2048]{1,0:T(1,128)S(1)}, s32[1,2048]{1,0:T(1,128)}, u32[]{:S(2)}) copy-start(s32[1,2048]{1,0:T(1,128)} %param.15) | copy-start | bytes 24580
  20.5 385.1 %reduce-scatter.4.cloned.1.call-start = ((), (), s32[]{:S(2)}) async-start(), calls=%async_computation.5 | async-start | bytes 3604480 | tf_op jit(solution)/shard_map/reduce_scatter | solution.py:1650
  219.0 115.0 %copy-start.10 = (f32[256,2048]{1,0:T(8,128)}, f32[256,2048]{1,0:T(8,128)S(1)}, u32[]{:S(2)}) copy-start(f32[256,2048]{1,0:T(8,128)S(1)} %get-tuple-element.110) | copy-start | bytes 6291460
  274.4 240.3 %reduce-scatter.6.cloned.1.call-start = ((), (), s32[]{:S(2)}) async-start(), calls=%async_computation.7 | async-start | bytes 7208960 | tf_op jit(solution)/shard_map/reduce_scatter | solution.py:1650
  328.2 317.2 %reduce-scatter.8.cloned.1.call-start = ((), (), s32[]{:S(2)}) async-start(), calls=%async_computation.8 | async-start | bytes 3932160 | tf_op jit(solution)/shard_map/reduce_scatter | solution.py:1650
  337.6 21.0 %copy-start.6 = (f32[2048,128]{1,0:T(8,128)S(1)}, f32[2048,128]{1,0:T(8,128)}, u32[]{:S(2)}) copy-start(f32[2048,128]{1,0:T(8,128)} %get-tuple-element.108.refs_6_.cosine) | copy-start | bytes 3145732
  344.4 14.1 %copy-start.4 = (f32[2048,128]{1,0:T(8,128)S(1)}, f32[2048,128]{1,0:T(8,128)}, u32[]{:S(2)}) copy-start(f32[2048,128]{1,0:T(8,128)} %get-tuple-element.106.refs_8_.sine_high) | copy-start | bytes 3145732
  344.4 14.2 %copy-start.5 = (f32[2048,128]{1,0:T(8,128)S(1)}, f32[2048,128]{1,0:T(8,128)}, u32[]{:S(2)}) copy-start(f32[2048,128]{1,0:T(8,128)} %get-tuple-element.107.refs_7_.sine_low) | copy-start | bytes 3145732
  516.2 4.1 copy-start.11
  518.1 5.4 copy-start.17
  529.9 95.4 %copy-start.13 = (bf16[1,256,2048]{2,1,0:T(8,128)(2,1)S(1)}, bf16[1,256,2048]{2,1,0:T(8,128)(2,1)}, u32[]{:S(2)}) copy-start(bf16[1,256,2048]{2,1,0:T(8,128)(2,1)} %param.14) | copy-start | bytes 3145732
  628.0 4.3 copy-start.2
  632.3 10.2 %copy-start.16 = (f32[256,2048]{1,0:T(8,128)S(1)}, f32[256,2048]{1,0:T(8,128)}, u32[]{:S(2)}) copy-start(f32[256,2048]{1,0:T(8,128)} %get-tuple-element.64) | copy-start | bytes 6291460
  696.7 2.8 copy-start.3
  699.5 8.4 %copy-start.1 = (bf16[512,2048]{1,0:T(8,128)(2,1)S(1)}, bf16[512,2048]{1,0:T(8,128)(2,1)}, u32[]{:S(2)}) copy-start(bf16[512,2048]{1,0:T(8,128)(2,1)} %param.21) | copy-start | bytes 6291460
  (9 other events, 13.8 us)
Sparse Core Ops, SparseCore 0:
  10.2 88.9 all-gather.3
  101.3 105.3 all-gather.5
  208.3 57.5 all-gather.7
  274.6 53.6 reduce-scatter.3
  330.4 102.0 reduce-scatter.5
  514.9 57.8 reduce-scatter.7

commit v4 on v3

--- a/solution.py
+++ b/solution.py
@@ -114,25 +114,35 @@
         copy.start()
         return copy
 
+    def hop(half, phase, mask):
+        bit, masks = steps[half][0][phase]
+        index = (1 << phase) - 1 + masks.index(mask)
+        copy = push(half, mask, bit, send_sem, recv_sem, index)
+        finals.append(copy.wait_send)
+        arriving[half, mask | 1 << bit] = copy
+
+    def to_core(half, mask):
+        copy = push(half, mask, 0, core_send, core_recv, steps[half][1].index(mask))
+        finals.append(copy.wait)
+
     arriving = {}
-    for phase in range(bits):
+    phases = bits - 1
+    for phase in range(phases):
         for half in range(2):
-            plan, held = steps[half]
-            if phase > 0:
-                for copy in arriving[half]:
-                    copy.wait_recv()
-            if phase < bits - 1:
-                bit, masks = plan[phase]
-                arriving[half] = [
-                    push(half, mask, bit, send_sem, recv_sem, (1 << phase) - 1 + number)
-                    for number, mask in enumerate(masks)
-                ]
-                finals += [copy.wait_send for copy in arriving[half]]
-            fresh = held[:1] if phase == 0 else held[1 << (phase - 1) : 1 << phase]
-            for mask in fresh:
-                copy = push(half, mask, 0, core_send, core_recv, held.index(mask))
-                finals.append(copy.wait)
-            yield
+            hop(half, phase, 0)
+    for half in range(2):
+        to_core(half, 0)
+    yield
+    for phase in range(phases):
+        for half in range(2):
+            bit, masks = steps[half][0][phase]
+            for mask in masks:
+                arrived = mask | 1 << bit
+                arriving[half, arrived].wait_recv()
+                for later in range(phase + 1, phases):
+                    hop(half, later, arrived)
+                to_core(half, arrived)
+        yield
     for wait in finals:
         wait()
 
@@ -156,9 +166,7 @@
     @pl.loop(0, rows // step)
     def _(i):
         at = pl.ds(pl.multiple_of(i * step, step), step)
-        target[at] = (first[at].astype(jnp.float32) + second[at].astype(jnp.float32)).astype(
-            target.dtype
-        )
+        target[at] = first[at].astype(target.dtype) + second[at].astype(target.dtype)
 
 
 def scatter_plan(bits):
@@ -649,6 +657,14 @@
     return [dma((3, 2)), dma((3, 2)), dma((4,)), dma((4,))]
 
 
+def part_slot(tile):
+    odd = tile % 2
+    return (1 - odd) * (tile // 2) + odd * (5 - tile // 4)
+
+
+SCATTER_ORDER = (7, 6, 3, 2, 5, 4, 1, 0)
+
+
 class TileScatter:
     def __init__(self, parts, core_buf, chip_buf, send_sem, recv_sem, core_send, core_recv):
         me = lax.axis_index("ctx")
@@ -656,7 +672,7 @@
         self.hops = {
             source: [
                 tile_copy(
-                    parts.at[source],
+                    parts.at[part_slot(source)],
                     chip_buf.at[source // 2 - 1],
                     half,
                     (first, 3 - first)[half],
@@ -669,32 +685,42 @@
             for source, first in ((6, 1), (4, 2), (2, 1))
         }
         self.cores = [
-            core_copy(parts.at[2 * i + 1], core_buf.at[i], me, core_send.at[i], core_recv.at[i])
+            core_copy(
+                parts.at[part_slot(2 * i + 1)],
+                core_buf.at[i],
+                me,
+                core_send.at[i],
+                core_recv.at[i],
+            )
             for i in range(4)
         ]
 
     def add(self, tile, buf):
-        here = self.parts.at[tile]
+        here = self.parts.at[part_slot(tile)]
         add_into(here, here, buf, here.shape[0], 32)
+
+    def before(self, tile):
+        if tile in (5, 1):
+            self.cores[tile // 2 + 1].wait_send()
 
     def after(self, tile):
         if tile % 2 == 1:
             self.cores[tile // 2].start()
-            return
+        else:
+            self.settle(tile)
+
+    def settle(self, tile):
         self.cores[tile // 2].wait_recv()
         self.add(tile, self.core_buf.at[tile // 2])
         if tile == 6 or tile == 2:
             for copy in self.hops[tile]:
                 copy.start()
-        if tile == 2:
-            self.pass_on()
-
-    def pass_on(self):
-        for copy in self.hops[6]:
-            copy.wait_recv()
-        self.add(4, self.chip_buf.at[2])
-        for copy in self.hops[4]:
-            copy.start()
+        if tile == 4:
+            for copy in self.hops[6]:
+                copy.wait_recv()
+            self.add(4, self.chip_buf.at[2])
+            for copy in self.hops[4]:
+                copy.start()
 
     def finish(self, out):
         for tile in (2, 4):
@@ -709,40 +735,53 @@
                 self.parts[0, at].astype(jnp.float32)
                 + self.chip_buf[0, at].astype(jnp.float32)
                 + self.chip_buf[1, at].astype(jnp.float32)
-            )
+            ).astype(out.dtype)
 
         for copies in self.hops.values():
             for copy in copies:
                 copy.wait_send()
-        for copy in self.cores:
-            copy.wait_send()
+        for tile in (4, 0):
+            self.cores[tile // 2].wait_send()
 
 
 def scatter_scratch(rows, width):
     return [
-        pltpu.VMEM((8, rows, width), jnp.bfloat16),
+        pltpu.VMEM((6, rows, width), jnp.bfloat16),
         pltpu.VMEM((4, rows, width), jnp.bfloat16),
         pltpu.VMEM((3, rows, width), jnp.bfloat16),
     ] + gather_sems()
 
 
-def produce_run(produce, count, *refs):
+def produce_run(produce, batch, late, count, *refs):
     inputs, (out, *scratch) = refs[:count], refs[count:]
     me = lax.axis_index("ctx")
     scatter = TileScatter(*scratch)
-    for tile in range(7, -1, -1):
-        scatter.parts[tile] = produce(inputs, tile, me).astype(jnp.bfloat16)
-        scatter.after(tile)
+    last = None
+    for tile in SCATTER_ORDER:
+        scatter.before(tile)
+        scatter.parts[part_slot(tile)] = produce(inputs, tile, me).astype(jnp.bfloat16)
+        if tile % 2 == 1:
+            scatter.after(tile)
+            if batch == 1 and last is not None:
+                scatter.settle(last)
+        last = tile
+        if tile % batch == 0:
+            yield
+            if batch > 1:
+                scatter.settle(tile)
+    if batch == 1:
+        scatter.settle(0)
+    for _ in range(late):
         yield
     scatter.finish(out)
 
 
-def produce_op(produce, rows, width, *inputs):
+def produce_op(produce, rows, width, *inputs, batch=1, late=0, kind=jnp.float32):
     return dict(
-        run=functools.partial(produce_run, produce, len(inputs)),
+        run=functools.partial(produce_run, produce, batch, late, len(inputs)),
         inputs=list(inputs),
         in_space=pltpu.VMEM,
-        outs=[jax.ShapeDtypeStruct((rows, width), jnp.float32)],
+        outs=[jax.ShapeDtypeStruct((rows, width), kind)],
         out_space=pltpu.VMEM,
         scratch=scatter_scratch(rows, width),
         moved=32 * rows * width,
@@ -758,10 +797,6 @@
 
 def product_of_rows(refs, tile, me):
     return times_transposed(tile_rows(refs[0], tile, me), refs[1][...])
-
-
-def product_of_tiles(refs, tile, me):
-    return jnp.dot(refs[0][tile], refs[1][...], preferred_element_type=jnp.float32)
 
 
 def product_of_columns(refs, tile, me):
@@ -805,7 +840,7 @@
         in_specs=[pl.BlockSpec((count, step, width), lambda i: (0, i, 0))],
         out_specs=[block, block],
         out_shape=[jax.ShapeDtypeStruct((rows, count * width // 2), jnp.float32)] * 2,
-        compiler_params=pltpu.CompilerParams(vmem_limit_bytes=32 << 20),
+        compiler_params=pltpu.CompilerParams(vmem_limit_bytes=60 << 20),
         cost_estimate=pl.CostEstimate(
             flops=0, bytes_accessed=6 * gathered.size, transcendentals=0
         ),
@@ -816,6 +851,202 @@
     me = lax.axis_index("ctx")
     bits = size.bit_length() - 1
     greet([flipped(me, 1 << bit, bits) for bit in range(bits)])
+
+
+def centre(values):
+    centered = values - jnp.mean(values, -1, keepdims=True)
+    inverse = lax.rsqrt(jnp.mean(centered * centered, -1, keepdims=True) + NORM_EPSILON)
+    return centered * inverse, inverse
+
+
+def join_kernel(
+    size,
+    mixed,
+    weights,
+    tokens,
+    gain,
+    shift,
+    mixed_rows,
+    residual,
+    normed,
+    weights_buf,
+    load_sem,
+    send_sem,
+    recv_sem,
+    local_sem,
+):
+    me = lax.axis_index("ctx")
+    cols = mixed.shape[2]
+
+    def load(owner):
+        at = pl.ds(pl.multiple_of(owner * cols, cols), cols)
+        return pltpu.make_async_copy(weights.at[at], weights_buf.at[at], load_sem.at[owner])
+
+    others = [lax.rem(me + step, size) for step in range(size)]
+    for step in range(size):
+        load(lax.rem(me + size - step, size)).start()
+    greet(others[1:])
+    here = column_view(mixed_rows, me, cols)
+    local = pltpu.make_async_copy(mixed.at[me], here, local_sem)
+    local.start()
+    copies = []
+    for step in range(1, size):
+        copy = pltpu.make_async_remote_copy(
+            src_ref=mixed.at[others[step]],
+            dst_ref=here,
+            send_sem=send_sem.at[step - 1],
+            recv_sem=recv_sem.at[step - 1],
+            device_id={"ctx": others[step]},
+            device_id_type=MESH_IDS,
+        )
+        copy.start()
+        copies.append(copy)
+    local.wait()
+    residual[...] = tokens[...].astype(jnp.float32)
+    for step in range(size):
+        owner = lax.rem(me + size - step, size)
+        if step > 0:
+            copies[step - 1].wait_recv()
+        load(owner).wait()
+        at = pl.ds(pl.multiple_of(owner * cols, cols), cols)
+        residual[...] += jnp.dot(
+            mixed_rows[:, at], weights_buf[at], preferred_element_type=jnp.float32
+        )
+    unit = centre(residual[...])[0]
+    normed[...] = (unit * gain[...] + shift[...]).astype(jnp.bfloat16)
+    for copy in copies:
+        copy.wait_send()
+
+
+def join_rows(mixed, weights, tokens, gain, shift, collective_id):
+    size, rows, cols = mixed.shape
+    width = size * cols
+    vmem = pl.BlockSpec(memory_space=pltpu.VMEM)
+    any_space = pl.BlockSpec(memory_space=pl.ANY)
+    low = jnp.bfloat16
+    dma = pltpu.SemaphoreType.DMA
+    return pl.pallas_call(
+        functools.partial(join_kernel, size),
+        in_specs=[any_space] * 2 + [vmem] * 3,
+        out_specs=[vmem] * 3,
+        out_shape=[
+            jax.ShapeDtypeStruct((rows, width), low),
+            jax.ShapeDtypeStruct((rows, width), jnp.float32),
+            jax.ShapeDtypeStruct((rows, width), low),
+        ],
+        scratch_shapes=[
+            pltpu.VMEM((width, width), low),
+            dma((size,)),
+            dma((size - 1,)),
+            dma((size - 1,)),
+            dma,
+        ],
+        compiler_params=pltpu.CompilerParams(
+            collective_id=collective_id, has_side_effects=True, vmem_limit_bytes=60 << 20
+        ),
+        cost_estimate=pl.CostEstimate(
+            flops=2 * rows * width * width, bytes_accessed=2 * width * width, transcendentals=0
+        ),
+    )(mixed, weights, tokens, gain, shift)
+
+
+def part_kernel(
+    size,
+    grad_normed,
+    residual,
+    cotangent,
+    gain,
+    weights,
+    grad_residual,
+    grad_branch,
+    sums,
+    grad_mixed,
+    weights_buf,
+    staged,
+    load_sem,
+    send_sem,
+    recv_sem,
+    local_sem,
+):
+    me = lax.axis_index("ctx")
+    cols = staged.shape[2]
+    others = [lax.rem(me + step, size) for step in range(size)]
+
+    def load(owner):
+        at = pl.ds(pl.multiple_of(owner * cols, cols), cols)
+        return pltpu.make_async_copy(weights.at[at], weights_buf.at[at], load_sem.at[owner])
+
+    order = list(range(1, size)) + [0]
+    for step in order:
+        load(others[step]).start()
+    greet(others[1:])
+    unit, inverse = centre(residual[...])
+    grads = grad_normed[...]
+    scaled = grads * gain[...]
+    total = cotangent[...].astype(jnp.float32) + inverse * (
+        scaled
+        - jnp.mean(scaled, -1, keepdims=True)
+        - unit * jnp.mean(scaled * unit, -1, keepdims=True)
+    )
+    grad_residual[...] = total
+    grad_branch[...] = total.astype(jnp.bfloat16)
+    copies = []
+    for step in order:
+        other = others[step]
+        load(other).wait()
+        at = pl.ds(pl.multiple_of(other * cols, cols), cols)
+        staged[step] = times_transposed(grad_branch[...], weights_buf[at]).astype(jnp.bfloat16)
+        if step == 0:
+            copy = pltpu.make_async_copy(staged.at[0], grad_mixed.at[me], local_sem)
+        else:
+            copy = pltpu.make_async_remote_copy(
+                src_ref=staged.at[step],
+                dst_ref=grad_mixed.at[me],
+                send_sem=send_sem.at[step - 1],
+                recv_sem=recv_sem.at[step - 1],
+                device_id={"ctx": other},
+                device_id_type=MESH_IDS,
+            )
+        copy.start()
+        copies.append(copy)
+    sums[:1] = jnp.sum(grads * unit, 0, keepdims=True)
+    sums[1:] = jnp.sum(grads, 0, keepdims=True)
+    for copy in copies:
+        copy.wait()
+
+
+def part_rows(grad_normed, residual, cotangent, gain, weights, size, collective_id):
+    rows, width = grad_normed.shape
+    cols = width // size
+    vmem = pl.BlockSpec(memory_space=pltpu.VMEM)
+    any_space = pl.BlockSpec(memory_space=pl.ANY)
+    low = jnp.bfloat16
+    dma = pltpu.SemaphoreType.DMA
+    return pl.pallas_call(
+        functools.partial(part_kernel, size),
+        in_specs=[vmem] * 4 + [any_space],
+        out_specs=[vmem] * 3 + [any_space],
+        out_shape=[
+            jax.ShapeDtypeStruct((rows, width), jnp.float32),
+            jax.ShapeDtypeStruct((rows, width), low),
+            jax.ShapeDtypeStruct((2, width), jnp.float32),
+            jax.ShapeDtypeStruct((size, rows, cols), low),
+        ],
+        scratch_shapes=[
+            pltpu.VMEM((width, width), low),
+            pltpu.VMEM((size, rows, cols), low),
+            dma((size,)),
+            dma((size - 1,)),
+            dma((size - 1,)),
+            dma,
+        ],
+        compiler_params=pltpu.CompilerParams(
+            collective_id=collective_id, has_side_effects=True, vmem_limit_bytes=60 << 20
+        ),
+        cost_estimate=pl.CostEstimate(
+            flops=2 * rows * width * width, bytes_accessed=2 * width * width, transcendentals=0
+        ),
+    )(grad_normed, residual, cotangent, gain, weights)
 
 
 def forward_kernel(
@@ -952,8 +1183,10 @@
     weights,
     down,
     normed_t,
+    hidden,
     grad_normed,
     grad_both_w,
+    layer_part,
     grads_buf,
     values_buf,
     weights_buf,
@@ -961,13 +1194,15 @@
     normed_buf,
     grad_both,
     out_buf,
+    hidden_buf,
     load_sem,
     tile_sem,
     out_sem,
     *scatter_refs,
 ):
     greet_near(8)
-    scatter = TileScatter(*scatter_refs)
+    scatter = TileScatter(*scatter_refs[: len(scatter_refs) // 2])
+    layer = TileScatter(*scatter_refs[len(scatter_refs) // 2 :])
     rows = grads_buf.shape[1]
     main = hidden_size // 128 * 128
     load_weights = pltpu.make_async_copy(weights, weights_buf, load_sem.at[0])
@@ -977,6 +1212,7 @@
         return [
             pltpu.make_async_copy(grads.at[tile], grads_buf.at[slot], tile_sem.at[0, slot]),
             pltpu.make_async_copy(values.at[tile], values_buf.at[slot], tile_sem.at[1, slot]),
+            pltpu.make_async_copy(hidden.at[tile], hidden_buf.at[slot], tile_sem.at[3, slot]),
         ]
 
     def load_chunk(i):
@@ -991,12 +1227,12 @@
 
     @pl.loop(0, 8)
     def _(u):
-        t = 7 - u
+        t = 7 - swapped(u)
         slot = t % 2
 
         @pl.when(u < 7)
         def _():
-            for copy in load_tile(t - 1, 1 - slot):
+            for copy in load_tile(7 - swapped(u + 1), 1 - slot):
                 copy.start()
 
         @pl.when(u == 0)
@@ -1031,7 +1267,14 @@
         def _():
             load_weights.wait()
 
-        scatter.parts[t] = lax.dot_general(
+        for tile in (5, 1):
+
+            @pl.when(t == tile)
+            def _():
+                scatter.before(tile)
+                layer.before(tile)
+
+        scatter.parts[part_slot(t)] = lax.dot_general(
             grad_both[t],
             weights_buf[...],
             (((1,), (1,)), ((), ())),
@@ -1043,6 +1286,15 @@
             def _():
                 scatter.after(tile)
 
+        layer.parts[part_slot(t)] = jnp.dot(
+            hidden_buf[slot], down_buf[...], preferred_element_type=jnp.float32
+        ).astype(jnp.bfloat16)
+        for tile in range(8):
+
+            @pl.when(t == tile)
+            def _():
+                layer.after(tile)
+
     chunks = normed_t.shape[0] // rows
 
     def store_chunk(i):
@@ -1071,9 +1323,10 @@
     store_chunk(chunks - 2).wait()
     store_chunk(chunks - 1).wait()
     scatter.finish(grad_normed)
-
-
-def backward_mlp(grads, values, weights, down, normed_t, collective_id):
+    layer.finish(layer_part)
+
+
+def backward_mlp(grads, values, weights, down, normed_t, hidden, collective_id):
     size, rows, width = grads.shape
     hidden_size = down.shape[0]
     wide = weights.shape[1]
@@ -1083,11 +1336,12 @@
     dma = pltpu.SemaphoreType.DMA
     return pl.pallas_call(
         functools.partial(backward_kernel, hidden_size),
-        in_specs=[any_space] * 5,
-        out_specs=[vmem, any_space],
+        in_specs=[any_space] * 6,
+        out_specs=[vmem, any_space, vmem],
         out_shape=[
             jax.ShapeDtypeStruct((rows, width), jnp.float32),
             jax.ShapeDtypeStruct((width, wide), low),
+            jax.ShapeDtypeStruct((rows, width), jnp.float32),
         ],
         scratch_shapes=[
             pltpu.VMEM((2, rows, width), low),
@@ -1097,11 +1351,12 @@
             pltpu.VMEM((2, rows, 8 * rows), low),
             pltpu.VMEM((8, rows, wide), low),
             pltpu.VMEM((2, rows, wide), low),
+            pltpu.VMEM((2, rows, hidden_size), low),
             dma((2,)),
-            dma((3, 2)),
+            dma((4, 2)),
             dma((2,)),
         ]
-        + scatter_scratch(rows, width),
+        + scatter_scratch(rows, width) * 2,
         compiler_params=pltpu.CompilerParams(
             collective_id=collective_id, has_side_effects=True, vmem_limit_bytes=60 << 20
         ),
@@ -1110,7 +1365,27 @@
             bytes_accessed=64 * rows * width,
             transcendentals=0,
         ),
-    )(grads, values, weights, down, normed_t)
+    )(grads, values, weights, down, normed_t, hidden)
+
+
+def unpack_rows_kernel(source, out):
+    out[...] = source[...].astype(jnp.float32)
+
+
+def unpack_rows(gathered, rows):
+    count, _, width = gathered.shape
+    out = pl.pallas_call(
+        unpack_rows_kernel,
+        grid=(count,),
+        in_specs=[pl.BlockSpec((None, rows, width), lambda i: (i, 0, 0))],
+        out_specs=pl.BlockSpec((None, rows, width), lambda i: (i, 0, 0)),
+        out_shape=jax.ShapeDtypeStruct((count, rows, width), jnp.float32),
+        compiler_params=pltpu.CompilerParams(vmem_limit_bytes=60 << 20),
+        cost_estimate=pl.CostEstimate(
+            flops=0, bytes_accessed=6 * gathered.size, transcendentals=0
+        ),
+    )(gathered)
+    return out.reshape(count * rows, width)
 
 
 def unpack_kernel(segments, count, source, out):
@@ -1131,7 +1406,7 @@
         in_specs=[pl.BlockSpec((count, step, width), lambda i: (0, i, 0))],
         out_specs=pl.BlockSpec((step, count * width), lambda i: (i, 0)),
         out_shape=jax.ShapeDtypeStruct((rows, count * width), jnp.float32),
-        compiler_params=pltpu.CompilerParams(vmem_limit_bytes=32 << 20),
+        compiler_params=pltpu.CompilerParams(vmem_limit_bytes=60 << 20),
         cost_estimate=pl.CostEstimate(
             flops=0, bytes_accessed=6 * gathered.size, transcendentals=0
         ),
@@ -1176,12 +1451,12 @@
     return jnp.concatenate([jnp.where(owner == h, rows, zero) for h in range(heads)], 0)
 
 
-def allowed_pairs(query_tile, key_tile, tile, heads, starts):
-    query_place = query_tile * tile + lax.broadcasted_iota(jnp.int32, (1, tile), 1)
-    query_place = jnp.concatenate([query_place] * heads, 1)
-    first_key = jnp.concatenate([starts] * heads, 1)
-    key_place = key_tile * tile + lax.broadcasted_iota(jnp.int32, (tile, 1), 0)
-    return (key_place <= query_place) & (key_place >= first_key)
+def pair_bias(key_tile, tile, heads, first_keys, diagonal):
+    key_place = lax.broadcasted_iota(jnp.int32, (tile, tile), 0)
+    allowed = key_place + key_tile * tile >= first_keys
+    if diagonal:
+        allowed &= key_place <= lax.broadcasted_iota(jnp.int32, (tile, tile), 1)
+    return jnp.concatenate([jnp.where(allowed, 0.0, MASKED_SCORE)] * heads, 1)
 
 
 def transposed(rows):
@@ -1224,15 +1499,12 @@
         total[...] = jnp.zeros_like(total)
         summed[...] = jnp.zeros_like(summed)
 
-        @pl.loop(lowest[i], i + 1)
-        def _(j):
+        def step(j, diagonal):
             keys_at = pl.ds(pl.multiple_of(j * tile, tile), tile)
             scores = jnp.dot(
                 qkv[keys_at, cols : 2 * cols], query_t, preferred_element_type=jnp.float32
             )
-            scores = jnp.where(
-                allowed_pairs(i, j, tile, heads, first_keys), scores, MASKED_SCORE
-            )
+            scores += pair_bias(j, tile, heads, first_keys, diagonal)
             old_top = top[...]
             new_top = jnp.maximum(old_top, jnp.max(scores, 0, keepdims=True))
             exps = jnp.exp(scores - new_top)
@@ -1246,6 +1518,12 @@
                 summed[features] = summed[features] * fade[:, own] + jnp.dot(
                     value_t[features, keys_at], low[:, own], preferred_element_type=jnp.float32
                 )
+
+        @pl.loop(lowest[i], i)
+        def _(j):
+            step(j, False)
+
+        step(i, True)
 
         log_total[i] = top[...] + jnp.log(total[...])
         scale = 1.0 / total[...]
@@ -1289,11 +1567,11 @@
     )(order, lowest, projected, starts)
 
 
-def attend_back_kernel(
+def attend_back_run(
     block,
     heads,
     order,
-    lowest,
+    places,
     qkv,
     grad_mixed,
     attended,
@@ -1305,10 +1583,10 @@
     out,
     sums,
     key_t,
-    grad_rows,
     grad_key,
     grad_value,
     grad_query,
+    query_sum,
 ):
     cols = heads * HEAD
     seq = qkv.shape[0]
@@ -1318,26 +1596,20 @@
     def _(p):
         at = pl.ds(pl.multiple_of(p * block, block), block)
         key_t[:, at] = transposed(qkv[at, cols : 2 * cols])
-        grad_rows[at] = grad_mixed[pl.ds(pl.multiple_of(order[p] * block, block), block)]
-        grad_key[at] = jnp.zeros((block, cols), jnp.float32)
-        grad_value[at] = jnp.zeros((block, cols), jnp.float32)
-
-    sums[...] = jnp.zeros_like(sums)
-
-    def finish(p, columns, rows):
-        low = rows.astype(jnp.bfloat16)
-        out[pl.ds(pl.multiple_of(order[p] * block, block), block), columns] = low
-        sums[:, columns] += jnp.sum(low.astype(jnp.float32), 0, keepdims=True)
-
-    def turned_back(p, rows):
-        at = pl.ds(pl.multiple_of(order[p] * block, block), block)
-        return turn(rows, cosine[at], -sine_low[at], -sine_high[at], cols)
-
-    @pl.loop(0, seq // tile)
-    def _(i):
-        at = pl.ds(pl.multiple_of(i * tile, tile), tile)
+        grad_key[p] = jnp.zeros((block, cols), jnp.float32)
+        grad_value[p] = jnp.zeros((block, cols), jnp.float32)
+
+    yield
+    for i in reversed(range(seq // tile)):
+        at = pl.ds(i * tile, tile)
         query = qkv[at, :cols]
-        grad = grad_rows[at]
+        grad = jnp.concatenate(
+            [
+                grad_mixed[order[2 * i + part]]
+                for part in range(2)
+            ],
+            0,
+        )
         query_t = head_stack(transposed(query), heads)
         query_rows = row_stack(query, heads)
         grad_t = head_stack(transposed(grad), heads)
@@ -1352,86 +1624,113 @@
         )
         logs = log_total[i]
         first_keys = starts[:, at]
-        grad_query[...] = jnp.zeros_like(grad_query)
-
-        @pl.loop(lowest[i], i + 1)
-        def _(j):
+        query_sum[...] = jnp.zeros_like(query_sum)
+
+        def step(j, diagonal):
             keys_at = pl.ds(pl.multiple_of(j * tile, tile), tile)
             scores = jnp.dot(
                 qkv[keys_at, cols : 2 * cols], query_t, preferred_element_type=jnp.float32
             )
-            weights = jnp.where(
-                allowed_pairs(i, j, tile, heads, first_keys), jnp.exp(scores - logs), 0.0
-            )
+            scores += pair_bias(j, tile, heads, first_keys, diagonal)
+            weights = jnp.exp(scores - logs)
             grad_soft = jnp.dot(
                 qkv[keys_at, 2 * cols :], grad_t, preferred_element_type=jnp.float32
             )
-            grad_value[keys_at] += jnp.dot(
+            pair = pl.ds(2 * j, 2)
+            grad_value[pair] += jnp.dot(
                 weights.astype(jnp.bfloat16), grads, preferred_element_type=jnp.float32
-            )
+            ).reshape(2, block, cols)
             grad_scores = (weights * (grad_soft - delta)).astype(jnp.bfloat16)
-            grad_key[keys_at] += jnp.dot(
+            grad_key[pair] += jnp.dot(
                 grad_scores, query_rows, preferred_element_type=jnp.float32
-            )
+            ).reshape(2, block, cols)
             for h in range(heads):
                 features = slice(h * HEAD, (h + 1) * HEAD)
-                grad_query[features] += jnp.dot(
+                query_sum[features] += jnp.dot(
                     key_t[features, keys_at],
                     grad_scores[:, h * tile : (h + 1) * tile],
                     preferred_element_type=jnp.float32,
                 )
 
-        rows = jnp.transpose(grad_query[...]) * HEAD ** (-0.5)
-        for part in range(2):
-            p = 2 * i + part
-            finish(p, slice(0, cols), turned_back(p, rows[part * block : (part + 1) * block]))
+        if i > 0:
+
+            @pl.loop(0, i)
+            def _(j):
+                step(j, False)
+
+        step(i, True)
+        grad_query[2 * i : 2 * i + 2] = (
+            jnp.transpose(query_sum[...]) * HEAD ** (-0.5)
+        ).reshape(2, block, cols)
+        yield
+    sums[...] = jnp.zeros_like(sums)
 
     @pl.loop(0, seq // block)
-    def _(p):
-        at = pl.ds(pl.multiple_of(p * block, block), block)
-        finish(p, slice(cols, 2 * cols), turned_back(p, grad_key[at]))
-        finish(p, slice(2 * cols, 3 * cols), grad_value[at])
-
-
-def attend_back(qkv, grad_mixed, attended, log_total, order, lowest, starts, tables, heads):
+    def _(d):
+        at = pl.ds(pl.multiple_of(d * block, block), block)
+        place = places[d]
+        tables = (cosine[at], -sine_low[at], -sine_high[at])
+        for k, rows in enumerate(
+            (
+                turn(grad_query[place], *tables, cols),
+                turn(grad_key[place], *tables, cols),
+                grad_value[place],
+            )
+        ):
+            columns = slice(k * cols, (k + 1) * cols)
+            low = rows.astype(jnp.bfloat16)
+            out[at, columns] = low
+            sums[:, columns] += jnp.sum(low.astype(jnp.float32), 0, keepdims=True)
+
+
+def attend_back_op(qkv, grad_mixed, attended, log_total, order, places, starts, tables, heads):
     seq, wide = qkv.shape
     cols = wide // 3
     block = seq // order.shape[0]
     tile = 2 * block
-    vmem = pl.BlockSpec(memory_space=pltpu.VMEM)
-    smem = pl.BlockSpec(memory_space=pltpu.SMEM)
-    return pl.pallas_call(
-        functools.partial(attend_back_kernel, block, heads),
-        in_specs=[smem, smem] + [vmem] * 8,
-        out_specs=[vmem] * 2,
-        out_shape=[
-            jax.ShapeDtypeStruct((seq, wide), jnp.bfloat16),
+    low = jnp.bfloat16
+    return dict(
+        run=functools.partial(attend_back_run, block, heads),
+        inputs=[order, places, qkv, grad_mixed, attended, log_total, starts, *tables],
+        in_spaces=[pltpu.SMEM] * 2 + [pltpu.VMEM] * 8,
+        outs=[
+            jax.ShapeDtypeStruct((seq, wide), low),
             jax.ShapeDtypeStruct((1, wide), jnp.float32),
         ],
-        scratch_shapes=[
-            pltpu.VMEM((cols, seq), jnp.bfloat16),
-            pltpu.VMEM((seq, cols), jnp.bfloat16),
-            pltpu.VMEM((seq, cols), jnp.float32),
-            pltpu.VMEM((seq, cols), jnp.float32),
+        out_spaces=[pltpu.VMEM] * 2,
+        scratch=[
+            pltpu.VMEM((cols, seq), low),
+            pltpu.VMEM((seq // block, block, cols), jnp.float32),
+            pltpu.VMEM((seq // block, block, cols), jnp.float32),
+            pltpu.VMEM((seq // block, block, cols), jnp.float32),
             pltpu.VMEM((cols, tile), jnp.float32),
         ],
-        compiler_params=pltpu.CompilerParams(vmem_limit_bytes=48 << 20),
-        cost_estimate=pl.CostEstimate(
-            flops=10 * seq * seq * cols, bytes_accessed=20 * seq * cols, transcendentals=0
-        ),
-    )(order, lowest, qkv, grad_mixed, attended, log_total, starts, *tables)
+        moved=20 * seq * cols,
+    )
 
 
 def rotary_tables(places):
+    half_rot = ROT // 2
+    turns = jnp.arange(half_rot, dtype=jnp.int32)[:, None]
+    freq = ROTARY_BASE ** (-turns.astype(jnp.float32) * 2.0 / ROT)
+    angles = places.astype(jnp.float32)[None, :] * freq
+    cosine, sine = lax.optimization_barrier((jnp.cos(angles), jnp.sin(angles)))
     lane = jnp.arange(128, dtype=jnp.int32)[None, :] % HEAD
-    half_rot = ROT // 2
-    freq = ROTARY_BASE ** (-(lane % half_rot).astype(jnp.float32) * 2.0 / ROT)
-    angles = places.astype(jnp.float32)[:, None] * freq
-    sine = jnp.sin(angles)
+    chosen = (lane % half_rot == turns) & (lane < ROT)
+
+    def spread_out(values, picks):
+        return lax.dot_general(
+            values,
+            picks.astype(jnp.float32),
+            (((0,), (0,)), ((), ())),
+            precision=lax.Precision.HIGHEST,
+            preferred_element_type=jnp.float32,
+        )
+
     return (
-        jnp.where(lane < ROT, jnp.cos(angles), 1.0),
-        jnp.where(lane < half_rot, -sine, 0.0),
-        jnp.where((lane >= half_rot) & (lane < ROT), sine, 0.0),
+        spread_out(cosine, chosen) + (lane >= ROT).astype(jnp.float32),
+        -spread_out(sine, chosen & (lane < half_rot)),
+        spread_out(sine, chosen & (lane >= half_rot)),
     )
 
 
@@ -1506,7 +1805,6 @@
     device_blocks = jnp.stack([block_pairs, 2 * ctx_size - 1 - block_pairs], 1).reshape(-1, 1)
     half_rows = rows_here // 2
     places = device_blocks * half_rows + jnp.arange(half_rows, dtype=jnp.int32)[None, :]
-    tables = rotary_tables(places.reshape(-1))
 
     def strips(w, count, size):
         stride = w.shape[1] // count
@@ -1538,6 +1836,8 @@
     gather_grads = gather_op(grad_out, ctx_size)
     if fused:
         gather_grads = gather_op(grad_out, ctx_size, row_half, tile_put, relative=True)
+    tables = rotary_tables(places.reshape(-1))
+    small, *tables = lax.optimization_barrier((small, *tables))
     small, out_here, tokens_all, grad_out_all = plane(
         ctx_size,
         1,
@@ -1574,24 +1874,19 @@
         projected.reshape(seq_rows, 3 * cols), order, lowest, starts, heads_here
     )
     mixed_here = mixed_here.reshape(ctx_size, rows_here, cols)
-    to_columns = functools.partial(column_view, width=cols)
-    mixed_rows = plane(
-        ctx_size,
-        12,
-        exchange_op(mixed_here, ctx_size, (rows_here, width), block_view, to_columns),
-    )
-    residual = tokens_in + times(mixed_rows, out_full)
-    normed_two, unit_two, inverse_two = norm_rows(residual, gain_two, shift_two)
+    mixed_rows, residual, normed_two_low = join_rows(
+        mixed_here, out_full, tokens[0], gain_two, shift_two, 12
+    )
+
     def blocks(rows):
         return rows.astype(jnp.bfloat16).reshape(ctx_size, rows_here, width)
 
-    normed_two_low = normed_two.astype(jnp.bfloat16)
     if fused:
         normed_two_t, both_value, hidden, grad_down_w = forward_mlp(
             normed_two_low, both_here, grad_out_all, hidden_here, 3
         )
-        grad_normed_two, grad_both_w = backward_mlp(
-            grad_out_all, both_value, both_here, down_here, normed_two_t, 4
+        grad_normed_two, grad_both_w, layer_part = backward_mlp(
+            grad_out_all, both_value, both_here, down_here, normed_two_t, hidden, 4
         )
     else:
         grad_out_all = grad_out_all.reshape(seq_rows, width)
@@ -1621,65 +1916,62 @@
             4,
             scatter_op(blocks(times_transposed(after(grad_both, grad_both_w), both_here)), ctx_size),
         )
-    grad_residual = grad_out.astype(jnp.float32) + norm_back(
-        grad_normed_two, unit_two, inverse_two, gain_two
-    )
-    grad_branch = grad_residual.astype(jnp.bfloat16)
-    grad_mixed_rows = times_transposed(grad_branch, out_full).astype(jnp.bfloat16)
-    grad_mixed = plane(
-        ctx_size,
-        5,
-        exchange_op(
-            grad_mixed_rows, ctx_size, (ctx_size, rows_here, cols), to_columns, block_view
-        ),
-    )
-    grad_projected, grad_bias = attend_back(
+    grad_residual, grad_branch, norm_two_sums, grad_mixed = part_rows(
+        grad_normed_two, residual, grad_out, gain_two, out_full, ctx_size, 5
+    )
+
+    def reduced(grad):
+        return lax.psum_scatter(
+            grad.astype(jnp.bfloat16), "fsdp", scatter_dimension=0, tiled=True
+        )
+
+    grad_down_w, grad_both_w = reduced(grad_down_w), reduced(grad_both_w)
+    attend_op = attend_back_op(
         qkv_rows,
-        grad_mixed.reshape(seq_rows, cols),
+        grad_mixed.reshape(2 * ctx_size, half_rows, cols),
         attended,
         log_total,
         order,
-        lowest,
+        places[:, 0] // half_rows,
         starts,
         tables,
         heads_here,
     )
-    grad_qkv_w = inner(normed_all, grad_projected).astype(jnp.bfloat16)
-
-    def reduced(grad):
-        return lax.psum_scatter(
-            grad.astype(jnp.bfloat16), "fsdp", scatter_dimension=0, tiled=True
-        )
-
-    hidden = after(hidden, grad_qkv_w)
-    grad_down_w, grad_both_w = reduced(grad_down_w), reduced(grad_both_w)
+    down_op = gather_op(grad_down_w, ctx_size, column_half, stacked_columns)
     if fused:
         mixed_t = jnp.transpose(
             mixed_rows.reshape(rows_here, fsdp_size, ctx_size, out_piece), (2, 1, 3, 0)
         ).reshape(ctx_size, fsdp_size * out_piece, rows_here)
-        layer_op = produce_op(product_of_tiles, rows_here, width, hidden, down_here)
-        out_op = produce_op(product_of_columns, rows_here, width, mixed_t, grad_branch)
+        out_op = produce_op(
+            product_of_columns,
+            rows_here,
+            width,
+            mixed_t,
+            grad_branch,
+            batch=2,
+            late=4,
+            kind=jnp.bfloat16,
+        )
     else:
         mixed_blocks = jnp.transpose(
             mixed_rows.reshape(rows_here, fsdp_size, ctx_size, out_piece), (0, 2, 1, 3)
         ).reshape(rows_here, width)
-        layer_op = scatter_op(blocks(times(hidden, down_here)), ctx_size)
         out_op = scatter_op(
-            inner(mixed_blocks, after(grad_branch, grad_qkv_w))
+            inner(mixed_blocks, grad_branch)
             .astype(jnp.bfloat16)
             .reshape(ctx_size, fsdp_size * out_piece, width),
             ctx_size,
         )
-    grad_down_w, layer_part, grad_out_w = plane_groups(
-        ctx_size,
-        6,
-        gather_op(grad_down_w, ctx_size, column_half, stacked_columns),
-        layer_op,
-        out_op,
-    )
-    layer_out = residual + layer_part
-    grad_qkv_w = reduced(after(grad_qkv_w, layer_part, grad_both_w))
-    grad_projected = after(grad_projected, layer_part)
+    if fused:
+        grad_down_w, grad_out_w, grad_projected, grad_bias = plane(
+            ctx_size, 6, down_op, out_op, attend_op
+        )
+    else:
+        grad_projected, grad_bias = plane(ctx_size, 6, attend_op)
+        grad_down_w, grad_out_w = plane(ctx_size, 7, down_op, out_op)
+        layer_part = plane(ctx_size, 10, scatter_op(blocks(times(hidden, down_here)), ctx_size))
+    grad_qkv_w = inner(normed_all, grad_projected).astype(jnp.bfloat16)
+    grad_projected = after(grad_projected, grad_qkv_w)
     if fused:
         normed_op = produce_op(
             product_of_rows,
@@ -1690,17 +1982,18 @@
         )
     else:
         normed_op = scatter_op(blocks(times_transposed(grad_projected, qkv_here)), ctx_size)
-    grad_both_w, grad_normed = plane_groups(
-        ctx_size, 9, gather_op(grad_both_w, ctx_size), normed_op
-    )
+    grad_normed = plane(ctx_size, 8, normed_op)
+    grad_down_w = unpack_rows(after(grad_down_w, grad_normed), strip)
+    layer_out = residual + layer_part
+    grad_qkv_w = reduced(grad_qkv_w)
     grad_tokens = grad_residual + norm_back(grad_normed, unit_one, inverse_one, gain_one)
 
     norm_sums = jnp.stack(
         [
             jnp.sum(grad_normed * unit_one, 0),
             jnp.sum(grad_normed, 0),
-            jnp.sum(grad_normed_two * unit_two, 0),
-            jnp.sum(grad_normed_two, 0),
+            norm_two_sums[0],
+            norm_two_sums[1],
         ]
     )
     norm_sums = jnp.transpose(norm_sums.reshape(4, fsdp_size, shard_rows), (1, 0, 2)).reshape(
@@ -1719,16 +2012,17 @@
         [grad_out_w.reshape(fsdp_size, out_piece, width)] + padded, 1
     )
     grad_out_w = grad_out_w.astype(jnp.bfloat16)
-    grad_out_w, grad_qkv_w = plane(
+    grad_both_w, grad_qkv_w, grad_out_w = plane(
         ctx_size,
         13,
+        gather_op(after(grad_both_w, grad_down_w), ctx_size),
+        gather_op(grad_qkv_w, ctx_size),
         z_sum_gather_op(grad_out_w, fsdp_size, ctx_size),
-        gather_op(grad_qkv_w, ctx_size),
     )
     sums = jnp.sum(grad_out_w[:, out_piece : out_piece + 2].astype(jnp.float32), 0)
     norm_sums = sums[0, : 4 * shard_rows].reshape(4, shard_rows)
     bias_sums = sums[1, : b_qkv.shape[0]]
-    grad_out_w = grad_out_w[:, :out_piece]
+    grad_out_w = unpack_rows(grad_out_w, out_piece)
     grad_gate_w, grad_up_w = unpack_both(grad_both_w, fsdp_size)
     float32 = jnp.float32
     return (
@@ -1738,12 +2032,12 @@
         norm_sums[1],
         unpack_columns(grad_qkv_w, 3),
         bias_sums,
-        grad_out_w.reshape(w_out.shape).astype(float32),
+        grad_out_w,
         norm_sums[2],
         norm_sums[3],
         grad_gate_w,
         grad_up_w,
-        grad_down_w.reshape(w_down.shape).astype(float32),
+        grad_down_w,
     )
 
 

time: 721 us -> 671 us (0.931)
  other arithmetic: 39 us -> 15.8 us
  local copies, waits for them, and re-layouts: 37.8 us -> 25.6 us
  Pallas kernels: 598 us -> 590 us
  matrix products: 25.2 us -> 17.5 us
    pallas_call x7 -> x5, Pallas kernels: 416 us -> 350 us  [plane(): pl.pallas_call(functools.partial(plane_kernel, size, parts, far, z_size),...]
    pallas_call x1, Pallas kernels: 53.6 us -> 84.5 us  [backward_mlp(): pl.pallas_call(functools.partial(backward_kernel, hidden_size), in_specs=...]
    pallas_call x1 -> x4, Pallas kernels: 34.5 us -> 54.5 us  [the longest x1 21.5 us: part_rows(): pl.pallas_call(functools.partial(part_kernel, size), in_specs=[vmem] * 4...]
    convert_element_type x5 -> x1, other arithmetic: 12.8 us -> 0.01 us  [rotary_tables(): (lane >= ROT).astype(jnp.float32)]
    dot_general x2 -> x3, matrix products: 13.9 us -> 5.92 us  [spread_out(): lax.dot_general(values, picks.astype(jnp.float32), (((0,), (0,)), ((), ()...]
    unnamed x65 -> x55, local copies, waits for them, and re-layouts: 16.1 us -> 8.84 us
  transfers between devices with their start and end apart: 6 -> 6, of which waited for: 0 -> 0; matrix products, arithmetic and copies ran while one was open for 11% -> 7% of each run, Pallas kernels for 76% -> 70%
where the time goes in v4:
time: 671 us; the launch traced here: 664 us
  Pallas kernels  590 us (88%)
  local copies, waits for them, and re-layouts  25.6 us (4%)
  matrix products  17.5 us (3%)
  other arithmetic  15.8 us (2%)
  between operations  15.1 us (2%)
    pallas_call x5, Pallas kernels, plane(): pl.pallas_call(functools.partial(plane_kernel, size, parts, far, z_size),...  350 us
    pallas_call x1, Pallas kernels, backward_mlp(): pl.pallas_call(functools.partial(backward_kernel, hidden_size), in_specs=...  84.5 us
    pallas_call x1, Pallas kernels, forward_mlp(): pl.pallas_call(functools.partial(forward_kernel, hidden_size), in_specs=[...  54.2 us
    pallas_call x1, Pallas kernels, attend(): pl.pallas_call(functools.partial(attend_kernel, block, heads), in_specs=[...  23.4 us
    pallas_call x1, Pallas kernels, part_rows(): pl.pallas_call(functools.partial(part_kernel, size), in_specs=[vmem] * 4...  21.5 us
    pallas_call x1, Pallas kernels, join_rows(): pl.pallas_call(functools.partial(join_kernel, size), in_specs=[any_space]...  18.2 us
    pallas_call x2, Pallas kernels, unpack_rows(): pl.pallas_call(unpack_rows_kernel, grid=(count,), in_specs=[pl.BlockSpec(...  14.8 us
    pallas_call x1, Pallas kernels, unpack_both(): pl.pallas_call(functools.partial(unpack_both_kernel, segments, count), gr...  13.7 us
  transfers between devices with their start and end apart: 6, of which 0 were waited for; matrix products, arithmetic and copies ran while one was open for 7% of the time, Pallas kernels for 70%

profile of v4, /device:TPU:0, one launch (start us, length us, event | category | flops | bytes accessed | tf_op | source)
XLA Modules:
  0.0 664.2 jit_solution(3875713967837856537)
XLA Ops:
  11.4 2.9 constant_dynamic-slice_fusion.5
  15.0 3.3 concatenate.25
  18.4 2.2 constant_dynamic-slice_fusion.1
  21.3 2.0 convolution_negate_fusion.refs_7_.refs_11_
  23.3 2.0 fusion.22.refs_8_.refs_12_
  26.9 2.0 convolution_add_fusion.refs_6_.refs_10_
  29.6 78.8 %shard_map.229 = (bf16[4,32,128]{2,1,0:T(8,128)(2,1)}, bf16[4,64,2048]{2,1,0:T(8,128)(2,1)}, bf16[8,256,2048]{2,1,0:T(8,128)(2,1)}, bf16[8,256,2048]{2,1,0:T(8,128)(2,1)}) custom-call(bf16[32,128]{1,0:T(8,128)(2,1)} %pad_bitcast_fusion.refs_0_, bf16[64,2048]{1,0:T(8,128)(2,1)} %constant_dynamic-slice_fusion.14.refs_1_, bf16[256,2048]{1,0:T(8,128)(2,1)} %bitcast.72, ...), custom_call_target="tpu_custom_call" | custom-call | bytes 34635776 | tf_op jit(solution)/shard_map/pallas_call | solution.py:537
  114.5 57.8 %shard_map.230 = (bf16[4,8,64,2048]{3,2,1,0:T(8,128)(2,1)}, bf16[8,256,768]{2,1,0:T(8,128)(2,1)}, bf16[8,256,2048]{2,1,0:T(8,128)(2,1)}) custom-call(bf16[4,64,2048]{2,1,0:T(8,128)(2,1)} %get-tuple-element.58.refs_0_, bf16[8,256,2048]{2,1,0:T(8,128)(2,1)} %get-tuple-element.59.refs_1_, bf16[2048,768]{1,0:T(8,128)(2,1)} %all-gather.4.cloned.1.call-done.refs_2_.refs_1_, ...), custom_call_target="tpu_custom_call" | custom-call | bytes 33554432 | tf_op jit(solution)/shard_map/pallas_call | solution.py:537
  172.4 23.4 %shard_map.231 = (bf16[2048,768]{1,0:T(8,128)(2,1)}, f32[2048,256]{1,0:T(8,128)S(1)}, bf16[2048,256]{1,0:T(8,128)(2,1)S(1)}, f32[8,1,1024]{2,1,0:T(1,128)S(1)}) custom-call(s32[16]{0:T(128)S(1)} %select_reduce_fusion.order.refs_3_, s32[8]{0:T(128)S(1)} %and_select_fusion.3.lowest, bf16[2048,768]{1,0:T(8,128)(2,1)} %bitcast.103, ...), custom_call_target="tpu_custom_call" | custom-call | flops 4294967296 | bytes 6291456 | tf_op jit(solution)/shard_map/pallas_call | solution.py:1547
  198.7 18.2 %shard_map.232 = (bf16[256,2048]{1,0:T(8,128)(2,1)}, f32[256,2048]{1,0:T(8,128)}, bf16[256,2048]{1,0:T(8,128)(2,1)}) custom-call(bf16[8,256,256]{2,1,0:T(8,128)(2,1)} %bitcast.70, bf16[2048,2048]{1,0:T(8,128)(2,1)} %bitcast.74, bf16[256,2048]{1,0:T(8,128)(2,1)} %bitcast.73, f32[1,2048]{1,0:T(1,128)} %bitcast.87, f32[1,2048]{1,0:T(1,128)} %bitcast.93), custom_call_target="tpu_custom_call" | custom-call | flops 2147483648 | bytes 8388608 | tf_op jit(solution)/shard_map/pallas_call | solution.py:928
  216.9 54.2 %shard_map.233 = (bf16[2048,2048]{1,0:T(8,128)(2,1)}, f32[8,256,1408]{2,1,0:T(8,128)}, bf16[8,256,704]{2,1,0:T(8,128)(2,1)}, bf16[704,2048]{1,0:T(8,128)(2,1)}) custom-call(bf16[256,2048]{1,0:T(8,128)(2,1)} %get-tuple-element.69.normed, bf16[2048,1408]{1,0:T(8,128)(2,1)} %all-gather.6.cloned.1.call-done.weights, bf16[8,256,2048]{2,1,0:T(8,128)(2,1)} %get-tuple-element.68.grads), custom_call_target="tpu_custom_call" | custom-call | flops 17716740096 | bytes 33554432 | tf_op jit(solution)/shard_map/pallas_call | solution.py:1147
  271.2 84.5 %shard_map.234 = (f32[256,2048]{1,0:T(8,128)}, bf16[2048,1408]{1,0:T(8,128)(2,1)}, f32[256,2048]{1,0:T(8,128)}) custom-call(bf16[8,256,2048]{2,1,0:T(8,128)(2,1)} %get-tuple-element.68.grads, f32[8,256,1408]{2,1,0:T(8,128)} %get-tuple-element.70.values, bf16[2048,1408]{1,0:T(8,128)(2,1)} %all-gather.6.cloned.1.call-done.weights, ...), custom_call_target="tpu_custom_call" | custom-call | flops 29527900160 | bytes 33554432 | tf_op jit(solution)/shard_map/pallas_call | solution.py:1337
  358.7 21.5 %shard_map.235 = (f32[256,2048]{1,0:T(8,128)}, bf16[256,2048]{1,0:T(8,128)(2,1)}, f32[2,2048]{1,0:T(2,128)}, bf16[8,256,256]{2,1,0:T(8,128)(2,1)}) custom-call(f32[256,2048]{1,0:T(8,128)} %get-tuple-element.74.grad_normed, f32[256,2048]{1,0:T(8,128)} %get-tuple-element.67.residual, bf16[256,2048]{1,0:T(8,128)(2,1)} %bitcast.78, f32[1,2048]{1,0:T(1,128)} %bitcast.88, ...), custom_call_target="tpu_custom_call" | custom-call | flops 2147483648 | bytes 8388608 | tf_op jit(solution)/shard_map/pallas_call | solution.py:1025
  380.2 73.1 %shard_map.236 = (bf16[8,176,2048]{2,1,0:T(8,128)(2,1)}, bf16[256,2048]{1,0:T(8,128)(2,1)}, bf16[2048,768]{1,0:T(8,128)(2,1)}, f32[1,768]{1,0:T(1,128)}) custom-call(bf16[176,2048]{1,0:T(8,128)(2,1)} %reduce-scatter.4.cloned.1.call-done.refs_0_, bf16[8,256,256]{2,1,0:T(8,128)(2,1)} %bitcast.81, bf16[256,2048]{1,0:T(8,128)(2,1)} %get-tuple-element.78.refs_2_, ...), custom_call_target="tpu_custom_call" | custom-call | bytes 38797312 | tf_op jit(solution)/shard_map/pallas_call | solution.py:537
  453.4 11.6 %convolution_convert_fusion = bf16[2048,768]{1,0:T(8,128)(2,1)} fusion(bf16[2048,2048]{1,0:T(8,128)(2,1)} %bitcast.102, bf16[2048,768]{1,0:T(8,128)(2,1)} %get-tuple-element.85), kind=kOutput, calls=%fused_computation | convolution fusion | flops 6444023808 | bytes 14680064 | tf_op jit(solution)/shard_map/dot_general | solution.py:1752
  468.8 45.7 %shard_map.237 = f32[256,2048]{1,0:T(8,128)} custom-call(bf16[8,256,768]{2,1,0:T(8,128)(2,1)} %bitcast.82, bf16[2048,768]{1,0:T(8,128)(2,1)} %all-gather.4.cloned.1.call-done.refs_2_.refs_1_), custom_call_target="tpu_custom_call" | custom-call | bytes 16777216 | tf_op jit(solution)/shard_map/pallas_call | solution.py:537
  514.6 2.6 fusion.11
  517.4 8.8 %shard_map.238 = f32[8,176,2048]{2,1,0:T(8,128)} custom-call(bf16[8,176,2048]{2,1,0:T(8,128)(2,1)} %get-tuple-element.88.source), custom_call_target="tpu_custom_call" | custom-call | bytes 17301504 | tf_op jit(solution)/shard_map/pallas_call | solution.py:1377
  526.2 2.7 fusion.13.refs_2_
  528.8 2.1 fusion.10
  531.0 95.1 %shard_map.239 = (bf16[8,512,1408]{2,1,0:T(8,128)(2,1)}, bf16[8,512,768]{2,1,0:T(8,128)(2,1)}, bf16[8,80,2048]{2,1,0:T(8,128)(2,1)}) custom-call(bf16[512,1408]{1,0:T(8,128)(2,1)} %reduce-scatter.6.cloned.1.call-done.refs_0_, bf16[512,768]{1,0:T(8,128)(2,1)} %reduce-scatter.8.cloned.1.call-done.refs_1_, bf16[4,80,2048]{2,1,0:T(8,128)(2,1)} %fusion.13.refs_2_), custom_call_target="tpu_custom_call" | custom-call | bytes 43515904 | tf_op jit(solution)/shard_map/pallas_call | solution.py:537
  626.0 6.0 shard_map.241
  634.2 13.7 %shard_map.242 = (f32[512,5632]{1,0:T(8,128)}, f32[512,5632]{1,0:T(8,128)}) custom-call(bf16[8,512,1408]{2,1,0:T(8,128)(2,1)} %get-tuple-element.95.source), custom_call_target="tpu_custom_call" | custom-call | bytes 34603008 | tf_op jit(solution)/shard_map/pallas_call | solution.py:837
  648.0 8.9 %shard_map.240 = f32[512,6144]{1,0:T(8,128)} custom-call(bf16[8,512,768]{2,1,0:T(8,128)(2,1)} %get-tuple-element.94.source), custom_call_target="tpu_custom_call" | custom-call | bytes 18874368 | tf_op jit(solution)/shard_map/pallas_call | solution.py:1403
  (124 shorter events, 26.2 us)
Async XLA Ops:
  7.2 21.7 %copy-start = (bf16[512,2048]{1,0:T(8,128)(2,1)S(1)}, bf16[512,2048]{1,0:T(8,128)(2,1)}, u32[]{:S(2)}) copy-start(bf16[512,2048]{1,0:T(8,128)(2,1)} %param.21) | copy-start | bytes 6291460
  7.2 107.3 %all-gather.4.cloned.1.call-start = ((), (), s32[]{:S(2)}) async-start(), calls=%async_computation.3 | async-start | bytes 3932160 | tf_op jit(solution)/shard_map/all_gather | solution.py:1828
  9.5 207.4 %all-gather.6.cloned.1.call-start = ((), (), s32[]{:S(2)}) async-start(), calls=%async_computation.4 | async-start | bytes 7208960 | tf_op jit(solution)/shard_map/all_gather | solution.py:1829
  18.3 2.4 copy-start.21
  18.3 252.9 %all-gather.8.cloned.1.call-start = ((), (), s32[]{:S(2)}) async-start(), calls=%async_computation.5 | async-start | bytes 3604480 | tf_op jit(solution)/shard_map/all_gather | solution.py:1830
  18.4 6.9 %copy-start.17 = (bf16[512]{0:T(512)(128)(2,1)S(1)}, bf16[512]{0:T(512)(128)(2,1)}, u32[]{:S(2)}) copy-start(bf16[512]{0:T(512)(128)(2,1)} %param.17) | copy-start | bytes 3076
  18.4 7.1 %copy-start.18 = (bf16[512]{0:T(512)(128)(2,1)S(1)}, bf16[512]{0:T(512)(128)(2,1)}, u32[]{:S(2)}) copy-start(bf16[512]{0:T(512)(128)(2,1)} %param.18) | copy-start | bytes 3076
  18.4 7.3 %copy-start.19 = (bf16[512]{0:T(512)(128)(2,1)S(1)}, bf16[512]{0:T(512)(128)(2,1)}, u32[]{:S(2)}) copy-start(bf16[512]{0:T(512)(128)(2,1)} %param.22) | copy-start | bytes 3076
  18.4 7.5 %copy-start.20 = (bf16[512]{0:T(512)(128)(2,1)S(1)}, bf16[512]{0:T(512)(128)(2,1)}, u32[]{:S(2)}) copy-start(bf16[512]{0:T(512)(128)(2,1)} %param.23) | copy-start | bytes 3076
  18.4 7.9 %copy-start.15 = (bf16[1536]{0:T(1024)(128)(2,1)S(1)}, bf16[1536]{0:T(1024)(128)(2,1)}, u32[]{:S(2)}) copy-start(bf16[1536]{0:T(1024)(128)(2,1)} %param.20) | copy-start | bytes 9220
  20.6 359.6 %reduce-scatter.4.cloned.1.call-start = ((), (), s32[]{:S(2)}) async-start(), calls=%async_computation.6 | async-start | bytes 3604480 | tf_op jit(solution)/shard_map/reduce_scatter | solution.py:1924
  26.9 83.6 %copy-start.13 = (s32[1,2048]{1,0:T(1,128)S(1)}, s32[1,2048]{1,0:T(1,128)}, u32[]{:S(2)}) copy-start(s32[1,2048]{1,0:T(1,128)} %param.15) | copy-start | bytes 24580
  112.5 59.9 %copy-start.5 = (s32[1,2048]{1,0:T(1,128)}, s32[1,2048]{1,0:T(1,128)S(1)}, u32[]{:S(2)}) copy-start(s32[1,2048]{1,0:T(1,128)S(1)} %compare_select_fusion.1.starts.refs_9_) | copy-start | bytes 24580
  114.5 57.9 %copy-start.6 = (s32[16]{0:T(128)}, s32[16]{0:T(128)S(1)}, u32[]{:S(2)}) copy-start(s32[16]{0:T(128)S(1)} %select_reduce_fusion.order.refs_3_) | copy-start | bytes 196
  195.8 1.3 copy-start.2
  271.1 259.8 %reduce-scatter.6.cloned.1.call-start = ((), (), s32[]{:S(2)}) async-start(), calls=%async_computation.7 | async-start | bytes 7208960 | tf_op jit(solution)/shard_map/reduce_scatter | solution.py:1924
  355.8 175.2 %reduce-scatter.8.cloned.1.call-start = ((), (), s32[]{:S(2)}) async-start(), calls=%async_computation.8 | async-start | bytes 3932160 | tf_op jit(solution)/shard_map/reduce_scatter | solution.py:1924
  465.0 1.9 copy-start.14
  465.0 1.9 copy-start.9
  465.0 2.5 copy-start.10
  514.6 2.7 copy-start.16
  517.4 11.5 %copy-start.11 = (f32[256,2048]{1,0:T(8,128)S(1)}, f32[256,2048]{1,0:T(8,128)}, u32[]{:S(2)}) copy-start(f32[256,2048]{1,0:T(8,128)} %get-tuple-element.75) | copy-start | bytes 6291460
  526.2 2.7 copy-start.8
  648.0 8.9 %copy-start.1 = (bf16[512,2048]{1,0:T(8,128)(2,1)S(1)}, bf16[512,2048]{1,0:T(8,128)(2,1)}, u32[]{:S(2)}) copy-start(bf16[512,2048]{1,0:T(8,128)(2,1)} %param.21) | copy-start | bytes 6291460
  (4 other events, 4.0 us)
Sparse Core Ops, SparseCore 0:
  10.2 88.9 all-gather.3
  101.3 105.3 all-gather.5
  208.3 57.4 all-gather.7
  271.3 54.8 reduce-scatter.3
  355.9 100.8 reduce-scatter.5
  465.2 58.3 reduce-scatter.7

commit v5 on v4

--- a/solution.py
+++ b/solution.py
@@ -76,8 +76,14 @@
     return column_half(ref.at[block], half)
 
 
-def middle_columns(ref, block, half):
-    return column_half(ref.at[:, block], half)
+def column_strip(ref, block, half, cols):
+    rows = ref.shape[0] // 2
+    at = block * cols if isinstance(block, int) else pl.multiple_of(block * cols, cols)
+    return ref.at[pl.ds(half * rows, rows), pl.ds(at, cols)]
+
+
+def last_strip(cols, ref, half):
+    return column_strip(ref, ref.shape[1] // cols - 1, half, cols)
 
 
 def block_view(ref, block):
@@ -89,7 +95,7 @@
 
 
 def gather_run(
-    bits, take, put, relative, source, out, send_sem, recv_sem, core_send, core_recv, local_sem
+    bits, take, put, relative, pace, source, out, send_sem, recv_sem, core_send, core_recv, local_sem
 ):
     me = lax.axis_index("ctx")
     steps = gather_plan(bits)
@@ -132,7 +138,8 @@
             hop(half, phase, 0)
     for half in range(2):
         to_core(half, 0)
-    yield
+    for _ in range(pace):
+        yield
     for phase in range(phases):
         for half in range(2):
             bit, masks = steps[half][0][phase]
@@ -142,17 +149,20 @@
                 for later in range(phase + 1, phases):
                     hop(half, later, arrived)
                 to_core(half, arrived)
-        yield
+        for _ in range(pace):
+            yield
     for wait in finals:
         wait()
 
 
-def gather_op(x, size, take=row_half, put=stacked_rows, out_shape=None, relative=False):
+def gather_op(
+    x, size, take=row_half, put=stacked_rows, out_shape=None, relative=False, pace=1
+):
     bits = size.bit_length() - 1
     steps = size // 2 - 1
     dma = pltpu.SemaphoreType.DMA
     return dict(
-        run=functools.partial(gather_run, bits, take, put, relative),
+        run=functools.partial(gather_run, bits, take, put, relative, pace),
         inputs=[x],
         in_space=pl.ANY,
         outs=[jax.ShapeDtypeStruct(out_shape or (size,) + x.shape, x.dtype)],
@@ -397,7 +407,7 @@
 
 def z_sum_gather_run(bits, size, source, out, low, buf, send_sem, recv_sem, *sems):
     yield from z_scatter_run(size, source, low, buf, send_sem, recv_sem)
-    yield from gather_run(bits, column_half, stacked_columns, False, low, out, *sems)
+    yield from gather_run(bits, column_half, stacked_columns, False, 1, low, out, *sems)
 
 
 def z_sum_gather_op(x, z_size, size):
@@ -445,7 +455,9 @@
         slot = block % 2
         return pltpu.make_async_copy(normed_buf.at[slot], normed.at[block], store_sem.at[slot])
 
-    load_weights = pltpu.make_async_copy(weights, weights_buf, weights_sem)
+    load_weights = pltpu.make_async_copy(
+        weights.at[:, pl.ds(0, 3 * cols)], weights_buf, weights_sem
+    )
     load(0).start()
     load_weights.start()
     yield
@@ -479,7 +491,7 @@
 
 def project_op(tokens, weights, gain, shift, bias, tables):
     size, rows, width = tokens.shape
-    wide = weights.shape[1]
+    wide = bias.shape[1]
     low = jnp.bfloat16
     dma = pltpu.SemaphoreType.DMA
     return dict(
@@ -494,7 +506,7 @@
         scratch=[
             pltpu.VMEM((2, rows, width), low),
             pltpu.VMEM((2, rows, width), low),
-            pltpu.VMEM(weights.shape, low),
+            pltpu.VMEM((width, wide), low),
             dma((2,)),
             dma((2,)),
             dma,
@@ -796,7 +808,8 @@
 
 
 def product_of_rows(refs, tile, me):
-    return times_transposed(tile_rows(refs[0], tile, me), refs[1][...])
+    rows = tile_rows(refs[0], tile, me)
+    return times_transposed(rows, refs[1][:, : rows.shape[1]])
 
 
 def product_of_columns(refs, tile, me):
@@ -1241,6 +1254,22 @@
 
         for copy in load_tile(t, slot):
             copy.wait()
+        for tile in (5, 1):
+
+            @pl.when(t == tile)
+            def _():
+                scatter.before(tile)
+                layer.before(tile)
+
+        layer.parts[part_slot(t)] = jnp.dot(
+            hidden_buf[slot], down_buf[...], preferred_element_type=jnp.float32
+        ).astype(jnp.bfloat16)
+        for tile in range(8):
+
+            @pl.when(t == tile)
+            def _():
+                layer.after(tile)
+
         grad_hidden = lax.dot_general(
             grads_buf[slot],
             down_buf[...],
@@ -1267,13 +1296,6 @@
         def _():
             load_weights.wait()
 
-        for tile in (5, 1):
-
-            @pl.when(t == tile)
-            def _():
-                scatter.before(tile)
-                layer.before(tile)
-
         scatter.parts[part_slot(t)] = lax.dot_general(
             grad_both[t],
             weights_buf[...],
@@ -1286,14 +1308,6 @@
             def _():
                 scatter.after(tile)
 
-        layer.parts[part_slot(t)] = jnp.dot(
-            hidden_buf[slot], down_buf[...], preferred_element_type=jnp.float32
-        ).astype(jnp.bfloat16)
-        for tile in range(8):
-
-            @pl.when(t == tile)
-            def _():
-                layer.after(tile)
 
     chunks = normed_t.shape[0] // rows
 
@@ -1709,28 +1723,39 @@
     )
 
 
-def rotary_tables(places):
+def tables_run(cosines, sines, cosine, sine_low, sine_high):
     half_rot = ROT // 2
-    turns = jnp.arange(half_rot, dtype=jnp.int32)[:, None]
+    step = 256
+    yield
+
+    @pl.loop(0, cosine.shape[0] // step)
+    def _(i):
+        at = pl.ds(pl.multiple_of(i * step, step), step)
+        cos_rows, sin_rows = jnp.transpose(cosines[:, at]), jnp.transpose(sines[:, at])
+        lane = lax.broadcasted_iota(jnp.int32, (step, 128), 1) % HEAD
+        cos_wide = jnp.ones((step, 128), jnp.float32)
+        sin_wide = jnp.zeros((step, 128), jnp.float32)
+        for k in range(half_rot):
+            own = (lane == k) | (lane == k + half_rot)
+            cos_wide = jnp.where(own, cos_rows[:, k : k + 1], cos_wide)
+            sin_wide = jnp.where(own, sin_rows[:, k : k + 1], sin_wide)
+        cosine[at] = cos_wide
+        sine_low[at] = jnp.where(lane < half_rot, -sin_wide, 0.0)
+        sine_high[at] = jnp.where(lane >= half_rot, sin_wide, 0.0)
+
+
+def tables_op(places):
+    turns = jnp.arange(ROT // 2, dtype=jnp.int32)[:, None]
     freq = ROTARY_BASE ** (-turns.astype(jnp.float32) * 2.0 / ROT)
     angles = places.astype(jnp.float32)[None, :] * freq
-    cosine, sine = lax.optimization_barrier((jnp.cos(angles), jnp.sin(angles)))
-    lane = jnp.arange(128, dtype=jnp.int32)[None, :] % HEAD
-    chosen = (lane % half_rot == turns) & (lane < ROT)
-
-    def spread_out(values, picks):
-        return lax.dot_general(
-            values,
-            picks.astype(jnp.float32),
-            (((0,), (0,)), ((), ())),
-            precision=lax.Precision.HIGHEST,
-            preferred_element_type=jnp.float32,
-        )
-
-    return (
-        spread_out(cosine, chosen) + (lane >= ROT).astype(jnp.float32),
-        -spread_out(sine, chosen & (lane < half_rot)),
-        spread_out(sine, chosen & (lane >= half_rot)),
+    return dict(
+        run=tables_run,
+        inputs=[jnp.cos(angles), jnp.sin(angles)],
+        in_space=pltpu.VMEM,
+        outs=[jax.ShapeDtypeStruct((places.size, 128), jnp.float32)] * 3,
+        out_space=pltpu.VMEM,
+        scratch=[],
+        moved=1024 * places.size,
     )
 
 
@@ -1813,7 +1838,7 @@
             for i in range(count)
         ]
 
-    qkv_strip = jnp.concatenate(strips(w_qkv, 3, cols), 1)
+    qkv_strip = jnp.concatenate(strips(w_qkv, 3, cols) + strips(w_out, 1, cols), 1)
     hidden_here = fsdp_size * strip
     main = hidden_here // 128 * 128
     fused = ctx_size == 8 and hidden_here - main == 64 and rows_here == 256
@@ -1824,7 +1849,6 @@
     )
     down_strip = lax.dynamic_slice_in_dim(w_down, position * strip, strip, 0)
     out_piece = shard_rows // ctx_size
-    out_strip = lax.dynamic_slice_in_dim(w_out, position * out_piece, out_piece, 0)
     qkv_here = lax.all_gather(qkv_strip, "fsdp", axis=0, tiled=True)
     both_here = lax.all_gather(both_strip, "fsdp", axis=0, tiled=True)
     down_here = lax.all_gather(down_strip, "fsdp", axis=0, tiled=True)
@@ -1836,13 +1860,11 @@
     gather_grads = gather_op(grad_out, ctx_size)
     if fused:
         gather_grads = gather_op(grad_out, ctx_size, row_half, tile_put, relative=True)
-    tables = rotary_tables(places.reshape(-1))
-    small, *tables = lax.optimization_barrier((small, *tables))
-    small, out_here, tokens_all, grad_out_all = plane(
+    *tables, small, tokens_all, grad_out_all = plane(
         ctx_size,
         1,
+        tables_op(places.reshape(-1)),
         z_gather_op(small, fsdp_size),
-        z_gather_op(out_strip, fsdp_size),
         gather_op(tokens[0], ctx_size),
         gather_grads,
     )
@@ -1858,15 +1880,15 @@
         ctx_size,
         2,
         gather_op(
-            out_here,
+            qkv_here,
             ctx_size,
-            column_half,
-            middle_columns,
-            (fsdp_size, ctx_size, out_piece, width),
+            functools.partial(last_strip, cols),
+            functools.partial(column_strip, cols=cols),
+            (width, width),
+            pace=4,
         ),
         project_op(tokens_all, qkv_here, gain_one, shift_one, bias_here, tables),
     )
-    out_full = out_full.reshape(width, width)
     normed_all = normed_all.reshape(seq_rows, width)
     tokens_in = tokens[0].astype(jnp.float32)
     unit_one, inverse_one = norm_rows(tokens_in, gain_one, shift_one)[1:]
@@ -1981,19 +2003,22 @@
             qkv_here,
         )
     else:
-        normed_op = scatter_op(blocks(times_transposed(grad_projected, qkv_here)), ctx_size)
-    grad_normed = plane(ctx_size, 8, normed_op)
-    grad_down_w = unpack_rows(after(grad_down_w, grad_normed), strip)
+        normed_op = scatter_op(
+            blocks(times_transposed(grad_projected, qkv_here[:, : 3 * cols])), ctx_size
+        )
+    grad_both_w, grad_normed = plane_groups(
+        ctx_size, 8, gather_op(grad_both_w, ctx_size), normed_op
+    )
+    grad_out_w = reduced(grad_out_w)
     layer_out = residual + layer_part
     grad_qkv_w = reduced(grad_qkv_w)
     grad_tokens = grad_residual + norm_back(grad_normed, unit_one, inverse_one, gain_one)
 
-    norm_sums = jnp.stack(
+    norm_sums = jnp.concatenate(
         [
-            jnp.sum(grad_normed * unit_one, 0),
-            jnp.sum(grad_normed, 0),
-            norm_two_sums[0],
-            norm_two_sums[1],
+            jnp.sum(grad_normed * unit_one, 0, keepdims=True),
+            jnp.sum(grad_normed, 0, keepdims=True),
+            norm_two_sums,
         ]
     )
     norm_sums = jnp.transpose(norm_sums.reshape(4, fsdp_size, shard_rows), (1, 0, 2)).reshape(
@@ -2004,22 +2029,21 @@
         grad_bias.reshape(3, 1, cols),
         (0, position, 0),
     ).reshape(fsdp_size, 1, 3 * width // fsdp_size)
-    padded = [
-        jnp.pad(rows, ((0, 0), (0, extra), (0, width - rows.shape[2])))
-        for rows, extra in ((norm_sums, 0), (bias_sums, 14))
-    ]
-    grad_out_w = jnp.concatenate(
-        [grad_out_w.reshape(fsdp_size, out_piece, width)] + padded, 1
-    )
-    grad_out_w = grad_out_w.astype(jnp.bfloat16)
-    grad_both_w, grad_qkv_w, grad_out_w = plane(
+    sums = jnp.concatenate(
+        [
+            jnp.pad(rows, ((0, 0), (0, extra), (0, width - rows.shape[2])))
+            for rows, extra in ((norm_sums, 0), (bias_sums, 6))
+        ],
+        1,
+    )
+    grad_qkv_w, grad_out_w, sums = plane(
         ctx_size,
         13,
-        gather_op(after(grad_both_w, grad_down_w), ctx_size),
-        gather_op(grad_qkv_w, ctx_size),
-        z_sum_gather_op(grad_out_w, fsdp_size, ctx_size),
-    )
-    sums = jnp.sum(grad_out_w[:, out_piece : out_piece + 2].astype(jnp.float32), 0)
+        gather_op(grad_qkv_w, ctx_size, pace=2),
+        gather_op(grad_out_w, ctx_size, column_half, stacked_columns, pace=2),
+        z_sum_gather_op(sums, fsdp_size, ctx_size),
+    )
+    sums = jnp.sum(sums, 0)
     norm_sums = sums[0, : 4 * shard_rows].reshape(4, shard_rows)
     bias_sums = sums[1, : b_qkv.shape[0]]
     grad_out_w = unpack_rows(grad_out_w, out_piece)
@@ -2037,7 +2061,7 @@
         norm_sums[3],
         grad_gate_w,
         grad_up_w,
-        grad_down_w,
+        unpack_rows(grad_down_w, strip),
     )
 
 

time: 671 us -> 653 us (0.973)
  Pallas kernels: 590 us -> 570 us
  waiting for transfers between devices: 0.18 us -> 11.7 us
    pallas_call x5, Pallas kernels: 350 us -> 336 us  [plane(): pl.pallas_call(functools.partial(plane_kernel, size, parts, far, z_size),...]
  transfers between devices with their start and end apart: 6 -> 7, of which waited for: 0 -> 2; matrix products, arithmetic and copies ran while one was open for 7% -> 6% of each run, Pallas kernels for 70% -> 79%
where the time goes in v5:
time: 653 us; the launch traced here: 648 us
  Pallas kernels  570 us (87%)
  local copies, waits for them, and re-layouts  22.8 us (3%)
  other arithmetic  16.3 us (2%)
  between operations  14.9 us (2%)
  waiting for transfers between devices  11.7 us (2%)
  matrix products  11.5 us (2%)
    pallas_call x5, Pallas kernels, plane(): pl.pallas_call(functools.partial(plane_kernel, size, parts, far, z_size),...  336 us
    pallas_call x1, Pallas kernels, backward_mlp(): pl.pallas_call(functools.partial(backward_kernel, hidden_size), in_specs=...  82.7 us
    pallas_call x1, Pallas kernels, forward_mlp(): pl.pallas_call(functools.partial(forward_kernel, hidden_size), in_specs=[...  53.1 us
    pallas_call x1, Pallas kernels, attend(): pl.pallas_call(functools.partial(attend_kernel, block, heads), in_specs=[...  22 us
    pallas_call x1, Pallas kernels, part_rows(): pl.pallas_call(functools.partial(part_kernel, size), in_specs=[vmem] * 4...  20.8 us
    pallas_call x1, Pallas kernels, join_rows(): pl.pallas_call(functools.partial(join_kernel, size), in_specs=[any_space]...  18.2 us
    pallas_call x2, Pallas kernels, unpack_rows(): pl.pallas_call(unpack_rows_kernel, grid=(count,), in_specs=[pl.BlockSpec(...  14.6 us
    pallas_call x1, Pallas kernels, unpack_both(): pl.pallas_call(functools.partial(unpack_both_kernel, segments, count), gr...  13.9 us
  transfers between devices with their start and end apart: 7, of which 2 were waited for; matrix products, arithmetic and copies ran while one was open for 6% of the time, Pallas kernels for 79%

profile of v5, /device:TPU:0, one launch (start us, length us, event | category | flops | bytes accessed | tf_op | source)
XLA Modules:
  0.0 648.0 jit_solution(3635665393494700698)
XLA Ops:
  10.9 2.9 constant_dynamic-slice_fusion.5
  14.5 2.2 concatenate.32
  16.8 2.0 constant_dynamic-slice_fusion.1
  21.7 81.3 %shard_map.229 = (f32[2048,128]{1,0:T(8,128)}, f32[2048,128]{1,0:T(8,128)}, f32[2048,128]{1,0:T(8,128)}, bf16[4,32,128]{2,1,0:T(8,128)(2,1)}, bf16[8,256,2048]{2...) custom-call(f32[8,2048]{1,0:T(8,128)} %get-tuple-element.117.refs_0_, f32[8,2048]{1,0:T(8,128)} %get-tuple-element.116.refs_1_, ...), custom_call_target="tpu_custom_call" | custom-call | bytes 35684352 | tf_op jit(solution)/shard_map/pallas_call | solution.py:549
  105.7 1.3 compare_select_fusion.1.starts.refs_9_
  109.1 44.3 %shard_map.230 = (bf16[2048,2048]{1,0:T(8,128)(2,1)}, bf16[8,256,768]{2,1,0:T(8,128)(2,1)}, bf16[8,256,2048]{2,1,0:T(8,128)(2,1)}) custom-call(bf16[2048,1024]{1,0:T(8,128)(2,1)} %all-gather.4.cloned.1.call-done.refs_0_.refs_2_, bf16[8,256,2048]{2,1,0:T(8,128)(2,1)} %get-tuple-element.51.refs_1_, ...), custom_call_target="tpu_custom_call" | custom-call | bytes 83886080 | tf_op jit(solution)/shard_map/pallas_call | solution.py:549
  153.5 22.0 %shard_map.231 = (bf16[2048,768]{1,0:T(8,128)(2,1)}, f32[2048,256]{1,0:T(8,128)S(1)}, bf16[2048,256]{1,0:T(8,128)(2,1)S(1)}, f32[8,1,1024]{2,1,0:T(1,128)S(1)}) custom-call(s32[16]{0:T(128)S(1)} %select_reduce_fusion.order.refs_3_, s32[8]{0:T(128)S(1)} %and_select_fusion.1.lowest, bf16[2048,768]{1,0:T(8,128)(2,1)} %bitcast.99, ...), custom_call_target="tpu_custom_call" | custom-call | flops 4294967296 | bytes 6291456 | tf_op jit(solution)/shard_map/pallas_call | solution.py:1561
  175.5 1.3 copy-done
  178.4 18.2 %shard_map.232 = (bf16[256,2048]{1,0:T(8,128)(2,1)}, f32[256,2048]{1,0:T(8,128)}, bf16[256,2048]{1,0:T(8,128)(2,1)}) custom-call(bf16[8,256,256]{2,1,0:T(8,128)(2,1)} %bitcast.67, bf16[2048,2048]{1,0:T(8,128)(2,1)} %get-tuple-element.58.weights, bf16[256,2048]{1,0:T(8,128)(2,1)} %bitcast.70, f32[1,2048]{1,0:T(1,128)} %bitcast.81, f32[1,2048]{1,0:T(1,128)} %bitcast.86), custom_call_target="tpu_custom_call" | custom-call | flops 2147483648 | bytes 8388608 | tf_op jit(solution)/shard_map/pallas_call | solution.py:941
  196.5 5.1 all-gather.6.cloned.1.call-done.weights
  201.7 53.1 %shard_map.233 = (bf16[2048,2048]{1,0:T(8,128)(2,1)}, f32[8,256,1408]{2,1,0:T(8,128)}, bf16[8,256,704]{2,1,0:T(8,128)(2,1)}, bf16[704,2048]{1,0:T(8,128)(2,1)}) custom-call(bf16[256,2048]{1,0:T(8,128)(2,1)} %get-tuple-element.61.normed, bf16[2048,1408]{1,0:T(8,128)(2,1)} %all-gather.6.cloned.1.call-done.weights, bf16[8,256,2048]{2,1,0:T(8,128)(2,1)} %get-tuple-element.60.grads), custom_call_target="tpu_custom_call" | custom-call | flops 17716740096 | bytes 33554432 | tf_op jit(solution)/shard_map/pallas_call | solution.py:1160
  254.9 6.5 all-gather.8.cloned.1.call-done.down
  261.3 82.7 %shard_map.234 = (f32[256,2048]{1,0:T(8,128)}, bf16[2048,1408]{1,0:T(8,128)(2,1)}, f32[256,2048]{1,0:T(8,128)}) custom-call(bf16[8,256,2048]{2,1,0:T(8,128)(2,1)} %get-tuple-element.60.grads, f32[8,256,1408]{2,1,0:T(8,128)} %get-tuple-element.62.values, bf16[2048,1408]{1,0:T(8,128)(2,1)} %all-gather.6.cloned.1.call-done.weights, ...), custom_call_target="tpu_custom_call" | custom-call | flops 29527900160 | bytes 33554432 | tf_op jit(solution)/shard_map/pallas_call | solution.py:1351
  346.9 20.8 %shard_map.235 = (f32[256,2048]{1,0:T(8,128)}, bf16[256,2048]{1,0:T(8,128)(2,1)}, f32[2,2048]{1,0:T(2,128)}, bf16[8,256,256]{2,1,0:T(8,128)(2,1)}) custom-call(f32[256,2048]{1,0:T(8,128)} %get-tuple-element.66.grad_normed, f32[256,2048]{1,0:T(8,128)} %get-tuple-element.59.residual, bf16[256,2048]{1,0:T(8,128)(2,1)} %bitcast.73, f32[1,2048]{1,0:T(1,128)} %bitcast.82, ...), custom_call_target="tpu_custom_call" | custom-call | flops 2147483648 | bytes 8388608 | tf_op jit(solution)/shard_map/pallas_call | solution.py:1038
  367.8 74.1 %shard_map.236 = (bf16[8,176,2048]{2,1,0:T(8,128)(2,1)}, bf16[256,2048]{1,0:T(8,128)(2,1)}, bf16[2048,768]{1,0:T(8,128)(2,1)}, f32[1,768]{1,0:T(1,128)}) custom-call(bf16[176,2048]{1,0:T(8,128)(2,1)} %reduce-scatter.7.cloned.1.call-done.refs_0_, bf16[8,256,256]{2,1,0:T(8,128)(2,1)} %bitcast.76, bf16[256,2048]{1,0:T(8,128)(2,1)} %get-tuple-element.71.refs_2_, ...), custom_call_target="tpu_custom_call" | custom-call | bytes 38797312 | tf_op jit(solution)/shard_map/pallas_call | solution.py:549
  442.0 11.5 %convolution_convert_fusion = bf16[2048,768]{1,0:T(8,128)(2,1)} fusion(bf16[2048,2048]{1,0:T(8,128)(2,1)} %bitcast.98, bf16[2048,768]{1,0:T(8,128)(2,1)} %get-tuple-element.78), kind=kOutput, calls=%fused_computation | convolution fusion | flops 6444023808 | bytes 14680064 | tf_op jit(solution)/shard_map/dot_general | solution.py:1777
  457.4 8.6 %shard_map.242 = f32[8,176,2048]{2,1,0:T(8,128)} custom-call(bf16[8,176,2048]{2,1,0:T(8,128)(2,1)} %get-tuple-element.89.source), custom_call_target="tpu_custom_call" | custom-call | bytes 17301504 | tf_op jit(solution)/shard_map/pallas_call | solution.py:1391
  466.0 91.5 %shard_map.237 = (bf16[8,512,1408]{2,1,0:T(8,128)(2,1)}, f32[256,2048]{1,0:T(8,128)}) custom-call(bf16[512,1408]{1,0:T(8,128)(2,1)} %reduce-scatter.5.cloned.1.call-done.refs_0_, bf16[8,256,768]{2,1,0:T(8,128)(2,1)} %bitcast.77, bf16[2048,1024]{1,0:T(8,128)(2,1)} %all-gather.4.cloned.1.call-done.refs_0_.refs_2_), custom_call_target="tpu_custom_call" | custom-call | bytes 39845888 | tf_op jit(solution)/shard_map/pallas_call | solution.py:549
  557.4 2.6 fusion.10
  560.1 13.9 %shard_map.241 = (f32[512,5632]{1,0:T(8,128)}, f32[512,5632]{1,0:T(8,128)}) custom-call(bf16[8,512,1408]{2,1,0:T(8,128)(2,1)} %get-tuple-element.86.source), custom_call_target="tpu_custom_call" | custom-call | bytes 34603008 | tf_op jit(solution)/shard_map/pallas_call | solution.py:850
  574.8 3.7 fusion.9
  578.5 45.2 %shard_map.238 = (bf16[8,512,768]{2,1,0:T(8,128)(2,1)}, bf16[8,64,2048]{2,1,0:T(8,128)(2,1)}, f32[8,8,2048]{2,1,0:T(8,128)}) custom-call(bf16[512,768]{1,0:T(8,128)(2,1)} %reduce-scatter.9.cloned.1.call-done.refs_0_, bf16[64,2048]{1,0:T(8,128)(2,1)} %reduce-scatter.11.cloned.1.call-done.refs_1_, f32[4,8,2048]{2,1,0:T(8,128)} %select_maximum_fusion.refs_2_), custom_call_target="tpu_custom_call" | custom-call | bytes 17563648 | tf_op jit(solution)/shard_map/pallas_call | solution.py:549
  626.0 8.8 %shard_map.239 = f32[512,6144]{1,0:T(8,128)} custom-call(bf16[8,512,768]{2,1,0:T(8,128)(2,1)} %get-tuple-element.84.source), custom_call_target="tpu_custom_call" | custom-call | bytes 18874368 | tf_op jit(solution)/shard_map/pallas_call | solution.py:1417
  634.7 6.0 shard_map.240
  (111 shorter events, 23.6 us)
Async XLA Ops:
  7.2 101.9 %all-gather.4.cloned.1.call-start = ((), (), s32[]{:S(2)}) async-start(), calls=%async_computation.4 | async-start | bytes 5242880 | tf_op jit(solution)/shard_map/all_gather | solution.py:1852
  9.7 192.0 %all-gather.6.cloned.1.call-start = ((), (), s32[]{:S(2)}) async-start(), calls=%async_computation.5 | async-start | bytes 7208960 | tf_op jit(solution)/shard_map/all_gather | solution.py:1853
  16.7 2.2 copy-start.18
  16.7 2.5 copy-start.14
  16.7 2.7 copy-start.15
  16.7 2.9 copy-start.16
  16.7 3.2 copy-start.17
  16.7 3.4 copy-start.12
  16.8 244.5 %all-gather.8.cloned.1.call-start = ((), (), s32[]{:S(2)}) async-start(), calls=%async_computation.6 | async-start | bytes 3604480 | tf_op jit(solution)/shard_map/all_gather | solution.py:1854
  18.9 86.2 %copy-start.10 = (s32[1,2048]{1,0:T(1,128)S(1)}, s32[1,2048]{1,0:T(1,128)}, u32[]{:S(2)}) copy-start(s32[1,2048]{1,0:T(1,128)} %param.15) | copy-start | bytes 24580
  18.9 348.9 %reduce-scatter.7.cloned.1.call-start = ((), (), s32[]{:S(2)}) async-start(), calls=%async_computation.8 | async-start | bytes 3604480 | tf_op jit(solution)/shard_map/reduce_scatter | solution.py:1946
  107.1 46.4 %copy-start.3 = (s32[1,2048]{1,0:T(1,128)}, s32[1,2048]{1,0:T(1,128)S(1)}, u32[]{:S(2)}) copy-start(s32[1,2048]{1,0:T(1,128)S(1)} %compare_select_fusion.1.starts.refs_9_) | copy-start | bytes 24580
  109.1 44.4 %copy-start.4 = (s32[16]{0:T(128)}, s32[16]{0:T(128)S(1)}, u32[]{:S(2)}) copy-start(s32[16]{0:T(128)S(1)} %select_reduce_fusion.order.refs_3_) | copy-start | bytes 196
  175.5 1.3 copy-start
  254.8 211.2 %reduce-scatter.5.cloned.1.call-start = ((), (), s32[]{:S(2)}) async-start(), calls=%async_computation.7 | async-start | bytes 7208960 | tf_op jit(solution)/shard_map/reduce_scatter | solution.py:1946
  344.0 1.2 copy-start.9
  344.0 234.4 %reduce-scatter.11.cloned.1.call-start = ((), (), s32[]{:S(2)}) async-start(), calls=%async_computation.10 | async-start | bytes 1310720 | tf_op jit(solution)/shard_map/reduce_scatter | solution.py:1946
  441.9 136.5 %reduce-scatter.9.cloned.1.call-start = ((), (), s32[]{:S(2)}) async-start(), calls=%async_computation.9 | async-start | bytes 3932160 | tf_op jit(solution)/shard_map/reduce_scatter | solution.py:1946
  453.5 1.2 copy-start.5
  453.5 1.9 copy-start.6
  453.5 2.5 copy-start.8
  456.0 1.3 copy-start.13
  557.4 2.6 copy-start.11
  560.1 14.7 %copy-start.7 = (f32[256,2048]{1,0:T(8,128)S(1)}, f32[256,2048]{1,0:T(8,128)}, u32[]{:S(2)}) copy-start(f32[256,2048]{1,0:T(8,128)} %get-tuple-element.79) | copy-start | bytes 6291460
  (2 other events, 1.6 us)
Sparse Core Ops, SparseCore 0:
  10.2 84.1 all-gather.3
  96.5 105.1 all-gather.5
  203.8 57.4 all-gather.7
  263.5 54.8 reduce-scatter.6
  344.1 100.1 reduce-scatter.4
  446.5 27.6 reduce-scatter.10
  477.2 58.8 reduce-scatter.8

commit v6 on v5

--- a/solution.py
+++ b/solution.py
@@ -453,7 +453,8 @@
 
     def store(block):
         slot = block % 2
-        return pltpu.make_async_copy(normed_buf.at[slot], normed.at[block], store_sem.at[slot])
+        at = pl.ds(block * rows, rows)
+        return pltpu.make_async_copy(normed_buf.at[slot], normed.at[:, at], store_sem.at[slot])
 
     load_weights = pltpu.make_async_copy(
         weights.at[:, pl.ds(0, 3 * cols)], weights_buf, weights_sem
@@ -472,7 +473,7 @@
         low = (centered * inverse * gain[...] + shift[...]).astype(jnp.bfloat16)
         if block >= 2:
             store(block - 2).wait()
-        normed_buf[block % 2] = low
+        normed_buf[block % 2] = jnp.transpose(low)
         store(block).start()
         if block == 0:
             load_weights.wait()
@@ -500,12 +501,12 @@
         in_spaces=[pl.ANY] * 2 + [pltpu.VMEM] * 6,
         outs=[
             jax.ShapeDtypeStruct((size, rows, wide), low),
-            jax.ShapeDtypeStruct((size, rows, width), low),
+            jax.ShapeDtypeStruct((width, size * rows), low),
         ],
         out_spaces=[pltpu.VMEM, pl.ANY],
         scratch=[
             pltpu.VMEM((2, rows, width), low),
-            pltpu.VMEM((2, rows, width), low),
+            pltpu.VMEM((2, width, rows), low),
             pltpu.VMEM((width, wide), low),
             dma((2,)),
             dma((2,)),
@@ -845,7 +846,7 @@
 
 def unpack_both(gathered, segments):
     count, rows, width = gathered.shape
-    step = 64
+    step = min(128, rows)
     block = pl.BlockSpec((step, count * width // 2), lambda i: (i, 0))
     return pl.pallas_call(
         functools.partial(unpack_both_kernel, segments, count),
@@ -993,16 +994,25 @@
     for step in order:
         load(others[step]).start()
     greet(others[1:])
-    unit, inverse = centre(residual[...])
-    grads = grad_normed[...]
-    scaled = grads * gain[...]
-    total = cotangent[...].astype(jnp.float32) + inverse * (
-        scaled
-        - jnp.mean(scaled, -1, keepdims=True)
-        - unit * jnp.mean(scaled * unit, -1, keepdims=True)
-    )
-    grad_residual[...] = total
-    grad_branch[...] = total.astype(jnp.bfloat16)
+    sums[...] = jnp.zeros_like(sums)
+    chunk = 32
+
+    @pl.loop(0, residual.shape[0] // chunk)
+    def _(i):
+        at = pl.ds(pl.multiple_of(i * chunk, chunk), chunk)
+        unit, inverse = centre(residual[at])
+        grads = grad_normed[at]
+        sums[:1] += jnp.sum(grads * unit, 0, keepdims=True)
+        sums[1:] += jnp.sum(grads, 0, keepdims=True)
+        scaled = grads * gain[...]
+        total = cotangent[at].astype(jnp.float32) + inverse * (
+            scaled
+            - jnp.mean(scaled, -1, keepdims=True)
+            - unit * jnp.mean(scaled * unit, -1, keepdims=True)
+        )
+        grad_residual[at] = total
+        grad_branch[at] = total.astype(jnp.bfloat16)
+
     copies = []
     for step in order:
         other = others[step]
@@ -1022,8 +1032,6 @@
             )
         copy.start()
         copies.append(copy)
-    sums[:1] = jnp.sum(grads * unit, 0, keepdims=True)
-    sums[1:] = jnp.sum(grads, 0, keepdims=True)
     for copy in copies:
         copy.wait()
 
@@ -1388,11 +1396,12 @@
 
 def unpack_rows(gathered, rows):
     count, _, width = gathered.shape
+    group = min(count, 1 << max(1, 352 // rows).bit_length() - 1)
     out = pl.pallas_call(
         unpack_rows_kernel,
-        grid=(count,),
-        in_specs=[pl.BlockSpec((None, rows, width), lambda i: (i, 0, 0))],
-        out_specs=pl.BlockSpec((None, rows, width), lambda i: (i, 0, 0)),
+        grid=(count // group,),
+        in_specs=[pl.BlockSpec((group, rows, width), lambda i: (i, 0, 0))],
+        out_specs=pl.BlockSpec((group, rows, width), lambda i: (i, 0, 0)),
         out_shape=jax.ShapeDtypeStruct((count, rows, width), jnp.float32),
         compiler_params=pltpu.CompilerParams(vmem_limit_bytes=60 << 20),
         cost_estimate=pl.CostEstimate(
@@ -1413,7 +1422,7 @@
 
 def unpack_columns(gathered, segments):
     count, rows, width = gathered.shape
-    step = 64
+    step = min(128, rows)
     return pl.pallas_call(
         functools.partial(unpack_kernel, segments, count),
         grid=(rows // step,),
@@ -1594,8 +1603,12 @@
     cosine,
     sine_low,
     sine_high,
+    normed_t,
     out,
     sums,
+    grad_weights,
+    normed_buf,
+    load_sem,
     key_t,
     grad_key,
     grad_value,
@@ -1605,6 +1618,14 @@
     cols = heads * HEAD
     seq = qkv.shape[0]
     tile = 2 * block
+    chunk = normed_buf.shape[1]
+    chunks = normed_t.shape[0] // chunk
+
+    def load(i):
+        at = pl.ds(pl.multiple_of(i * chunk, chunk), chunk)
+        return pltpu.make_async_copy(normed_t.at[at], normed_buf.at[i % 2], load_sem.at[i % 2])
+
+    load(0).start()
 
     @pl.loop(0, seq // block)
     def _(p):
@@ -1696,8 +1717,22 @@
             out[at, columns] = low
             sums[:, columns] += jnp.sum(low.astype(jnp.float32), 0, keepdims=True)
 
-
-def attend_back_op(qkv, grad_mixed, attended, log_total, order, places, starts, tables, heads):
+    @pl.loop(0, chunks)
+    def _(i):
+        @pl.when(i < chunks - 1)
+        def _():
+            load(i + 1).start()
+
+        load(i).wait()
+        at = pl.ds(pl.multiple_of(i * chunk, chunk), chunk)
+        grad_weights[at] = jnp.dot(
+            normed_buf[i % 2], out[...], preferred_element_type=jnp.float32
+        ).astype(jnp.bfloat16)
+
+
+def attend_back_op(
+    qkv, grad_mixed, attended, log_total, order, places, starts, tables, normed_t, heads
+):
     seq, wide = qkv.shape
     cols = wide // 3
     block = seq // order.shape[0]
@@ -1705,14 +1740,17 @@
     low = jnp.bfloat16
     return dict(
         run=functools.partial(attend_back_run, block, heads),
-        inputs=[order, places, qkv, grad_mixed, attended, log_total, starts, *tables],
-        in_spaces=[pltpu.SMEM] * 2 + [pltpu.VMEM] * 8,
+        inputs=[order, places, qkv, grad_mixed, attended, log_total, starts, *tables, normed_t],
+        in_spaces=[pltpu.SMEM] * 2 + [pltpu.VMEM] * 8 + [pl.ANY],
         outs=[
             jax.ShapeDtypeStruct((seq, wide), low),
             jax.ShapeDtypeStruct((1, wide), jnp.float32),
+            jax.ShapeDtypeStruct((normed_t.shape[0], wide), low),
         ],
-        out_spaces=[pltpu.VMEM] * 2,
+        out_spaces=[pltpu.VMEM] * 3,
         scratch=[
+            pltpu.VMEM((2, 256, seq), low),
+            pltpu.SemaphoreType.DMA((2,)),
             pltpu.VMEM((cols, seq), low),
             pltpu.VMEM((seq // block, block, cols), jnp.float32),
             pltpu.VMEM((seq // block, block, cols), jnp.float32),
@@ -1876,7 +1914,7 @@
     bias_full = bias_full.reshape(3, ctx_size, cols)
     bias_here = lax.dynamic_index_in_dim(bias_full, position, 1, keepdims=False)
     bias_here = bias_here.reshape(1, 3 * cols)
-    out_full, projected, normed_all = plane(
+    out_full, projected, normed_t = plane(
         ctx_size,
         2,
         gather_op(
@@ -1889,7 +1927,6 @@
         ),
         project_op(tokens_all, qkv_here, gain_one, shift_one, bias_here, tables),
     )
-    normed_all = normed_all.reshape(seq_rows, width)
     tokens_in = tokens[0].astype(jnp.float32)
     unit_one, inverse_one = norm_rows(tokens_in, gain_one, shift_one)[1:]
     qkv_rows, attended, mixed_here, log_total = attend(
@@ -1957,9 +1994,10 @@
         places[:, 0] // half_rows,
         starts,
         tables,
+        normed_t,
         heads_here,
     )
-    down_op = gather_op(grad_down_w, ctx_size, column_half, stacked_columns)
+    down_op = gather_op(grad_down_w, ctx_size, column_half, stacked_columns, pace=2)
     if fused:
         mixed_t = jnp.transpose(
             mixed_rows.reshape(rows_here, fsdp_size, ctx_size, out_piece), (2, 1, 3, 0)
@@ -1971,7 +2009,7 @@
             mixed_t,
             grad_branch,
             batch=2,
-            late=4,
+            late=5,
             kind=jnp.bfloat16,
         )
     else:
@@ -1985,15 +2023,13 @@
             ctx_size,
         )
     if fused:
-        grad_down_w, grad_out_w, grad_projected, grad_bias = plane(
+        grad_down_w, grad_out_w, grad_projected, grad_bias, grad_qkv_w = plane(
             ctx_size, 6, down_op, out_op, attend_op
         )
     else:
-        grad_projected, grad_bias = plane(ctx_size, 6, attend_op)
+        grad_projected, grad_bias, grad_qkv_w = plane(ctx_size, 6, attend_op)
         grad_down_w, grad_out_w = plane(ctx_size, 7, down_op, out_op)
         layer_part = plane(ctx_size, 10, scatter_op(blocks(times(hidden, down_here)), ctx_size))
-    grad_qkv_w = inner(normed_all, grad_projected).astype(jnp.bfloat16)
-    grad_projected = after(grad_projected, grad_qkv_w)
     if fused:
         normed_op = produce_op(
             product_of_rows,

time: 653 us -> 646 us (0.989)
  matrix products: 11.5 us -> 0 us
  Pallas kernels: 570 us -> 577 us
    dot_general x1 -> x0, matrix products: 11.5 us -> none  [inner(): lax.dot_general(left_side, right_side, (((0,), (0,)), ((), ())), preferre...]
    pallas_call x5, Pallas kernels: 336 us -> 345 us  [plane(): pl.pallas_call(functools.partial(plane_kernel, size, parts, far, z_size),...]
  transfers between devices with their start and end apart: 7 -> 7, of which waited for: 2 -> 2; matrix products, arithmetic and copies ran while one was open for 6% -> 5% of each run, Pallas kernels for 79% -> 81%
where the time goes in v6:
time: 646 us; the launch traced here: 641 us
  Pallas kernels  577 us (89%)
  local copies, waits for them, and re-layouts  22.3 us (3%)
  other arithmetic  16.3 us (3%)
  between operations  14.9 us (2%)
  waiting for transfers between devices  10.2 us (2%)
    pallas_call x5, Pallas kernels, plane(): pl.pallas_call(functools.partial(plane_kernel, size, parts, far, z_size),...  345 us
    pallas_call x1, Pallas kernels, backward_mlp(): pl.pallas_call(functools.partial(backward_kernel, hidden_size), in_specs=...  82.7 us
    pallas_call x1, Pallas kernels, forward_mlp(): pl.pallas_call(functools.partial(forward_kernel, hidden_size), in_specs=[...  53.1 us
    pallas_call x1, Pallas kernels, attend(): pl.pallas_call(functools.partial(attend_kernel, block, heads), in_specs=[...  24.1 us
    pallas_call x1, Pallas kernels, part_rows(): pl.pallas_call(functools.partial(part_kernel, size), in_specs=[vmem] * 4...  22.2 us
    pallas_call x1, Pallas kernels, join_rows(): pl.pallas_call(functools.partial(join_kernel, size), in_specs=[any_space]...  18.2 us
    pallas_call x1, Pallas kernels, unpack_both(): pl.pallas_call(functools.partial(unpack_both_kernel, segments, count), gr...  13.1 us
  transfers between devices with their start and end apart: 7, of which 2 were waited for; matrix products, arithmetic and copies ran while one was open for 5% of the time, Pallas kernels for 81%

profile of v6, /device:TPU:0, one launch (start us, length us, event | category | flops | bytes accessed | tf_op | source)
XLA Modules:
  0.0 641.1 jit_solution(10926477394655971240)
XLA Ops:
  7.2 1.3 constant_dynamic-slice_fusion.14
  10.9 2.9 constant_dynamic-slice_fusion.5
  14.5 2.2 concatenate.32
  16.8 2.0 constant_dynamic-slice_fusion.1
  21.7 81.3 %shard_map.229 = (f32[2048,128]{1,0:T(8,128)}, f32[2048,128]{1,0:T(8,128)}, f32[2048,128]{1,0:T(8,128)}, bf16[4,32,128]{2,1,0:T(8,128)(2,1)}, bf16[8,256,2048]{2...) custom-call(f32[8,2048]{1,0:T(8,128)} %get-tuple-element.117.refs_0_, f32[8,2048]{1,0:T(8,128)} %get-tuple-element.116.refs_1_, ...), custom_call_target="tpu_custom_call" | custom-call | bytes 35684352 | tf_op jit(solution)/shard_map/pallas_call | solution.py:550
  105.7 1.3 compare_select_fusion.1.starts.refs_9_
  109.1 44.3 %shard_map.230 = (bf16[2048,2048]{1,0:T(8,128)(2,1)}, bf16[8,256,768]{2,1,0:T(8,128)(2,1)}, bf16[2048,2048]{1,0:T(8,128)(2,1)}) custom-call(bf16[2048,1024]{1,0:T(8,128)(2,1)} %all-gather.4.cloned.1.call-done.refs_0_.refs_2_, bf16[8,256,2048]{2,1,0:T(8,128)(2,1)} %get-tuple-element.51.refs_1_, ...), custom_call_target="tpu_custom_call" | custom-call | bytes 83886080 | tf_op jit(solution)/shard_map/pallas_call | solution.py:550
  153.5 24.1 %shard_map.231 = (bf16[2048,768]{1,0:T(8,128)(2,1)}, f32[2048,256]{1,0:T(8,128)S(1)}, bf16[2048,256]{1,0:T(8,128)(2,1)S(1)}, f32[8,1,1024]{2,1,0:T(1,128)S(1)}) custom-call(s32[16]{0:T(128)S(1)} %select_reduce_fusion.order.refs_3_, s32[8]{0:T(128)S(1)} %and_select_fusion.1.lowest, bf16[2048,768]{1,0:T(8,128)(2,1)} %bitcast.95, ...), custom_call_target="tpu_custom_call" | custom-call | flops 4294967296 | bytes 6291456 | tf_op jit(solution)/shard_map/pallas_call | solution.py:1570
  177.6 1.3 copy-done
  180.5 18.2 %shard_map.232 = (bf16[256,2048]{1,0:T(8,128)(2,1)}, f32[256,2048]{1,0:T(8,128)}, bf16[256,2048]{1,0:T(8,128)(2,1)}) custom-call(bf16[8,256,256]{2,1,0:T(8,128)(2,1)} %bitcast.64, bf16[2048,2048]{1,0:T(8,128)(2,1)} %get-tuple-element.58.weights, bf16[256,2048]{1,0:T(8,128)(2,1)} %bitcast.67, f32[1,2048]{1,0:T(1,128)} %bitcast.78, f32[1,2048]{1,0:T(1,128)} %bitcast.83), custom_call_target="tpu_custom_call" | custom-call | flops 2147483648 | bytes 8388608 | tf_op jit(solution)/shard_map/pallas_call | solution.py:942
  198.7 3.0 all-gather.6.cloned.1.call-done.weights
  201.7 53.1 %shard_map.233 = (bf16[2048,2048]{1,0:T(8,128)(2,1)}, f32[8,256,1408]{2,1,0:T(8,128)}, bf16[8,256,704]{2,1,0:T(8,128)(2,1)}, bf16[704,2048]{1,0:T(8,128)(2,1)}) custom-call(bf16[256,2048]{1,0:T(8,128)(2,1)} %get-tuple-element.61.normed, bf16[2048,1408]{1,0:T(8,128)(2,1)} %all-gather.6.cloned.1.call-done.weights, bf16[8,256,2048]{2,1,0:T(8,128)(2,1)} %get-tuple-element.60.grads), custom_call_target="tpu_custom_call" | custom-call | flops 17716740096 | bytes 33554432 | tf_op jit(solution)/shard_map/pallas_call | solution.py:1168
  254.9 6.5 %all-gather.8.cloned.1.call-done.down = bf16[704,2048]{1,0:T(8,128)(2,1)} async-done(((bf16[176,2048]{1,0:T(8,128)(2,1)}), bf16[704,2048]{1,0:T(8,128)(2,1)}) %all-gather.8.cloned.1.call-update) | async-done | bytes 2883600 | tf_op jit(solution)/shard_map/all_gather | solution.py:1892
  261.3 82.7 %shard_map.234 = (f32[256,2048]{1,0:T(8,128)}, bf16[2048,1408]{1,0:T(8,128)(2,1)}, f32[256,2048]{1,0:T(8,128)}) custom-call(bf16[8,256,2048]{2,1,0:T(8,128)(2,1)} %get-tuple-element.60.grads, f32[8,256,1408]{2,1,0:T(8,128)} %get-tuple-element.62.values, bf16[2048,1408]{1,0:T(8,128)(2,1)} %all-gather.6.cloned.1.call-done.weights, ...), custom_call_target="tpu_custom_call" | custom-call | flops 29527900160 | bytes 33554432 | tf_op jit(solution)/shard_map/pallas_call | solution.py:1359
  346.9 22.2 %shard_map.235 = (f32[256,2048]{1,0:T(8,128)}, bf16[256,2048]{1,0:T(8,128)(2,1)}, f32[2,2048]{1,0:T(2,128)}, bf16[8,256,256]{2,1,0:T(8,128)(2,1)}) custom-call(f32[256,2048]{1,0:T(8,128)} %get-tuple-element.66.grad_normed, f32[256,2048]{1,0:T(8,128)} %get-tuple-element.59.residual, bf16[256,2048]{1,0:T(8,128)(2,1)} %bitcast.70, f32[1,2048]{1,0:T(1,128)} %bitcast.79, ...), custom_call_target="tpu_custom_call" | custom-call | flops 2147483648 | bytes 8388608 | tf_op jit(solution)/shard_map/pallas_call | solution.py:1046
  369.2 82.4 %shard_map.236 = (bf16[8,176,2048]{2,1,0:T(8,128)(2,1)}, bf16[256,2048]{1,0:T(8,128)(2,1)}, bf16[2048,768]{1,0:T(8,128)(2,1)}, f32[1,768]{1,0:T(1,128)}, bf16[2048,768]{1,0:T(8,128)(2,1)}) custom-call(bf16[176,2048]{1,0:T(8,128)(2,1)} %reduce-scatter.7.cloned.1.call-done.refs_0_, bf16[8,256,256]{2,1,0:T(8,128)(2,1)} %bitcast.71, ...), custom_call_target="tpu_custom_call" | custom-call | bytes 38797312 | tf_op jit(solution)/shard_map/pallas_call | solution.py:550
  455.6 7.7 %shard_map.242 = f32[8,176,2048]{2,1,0:T(8,128)} custom-call(bf16[8,176,2048]{2,1,0:T(8,128)(2,1)} %get-tuple-element.89.source), custom_call_target="tpu_custom_call" | custom-call | bytes 17301504 | tf_op jit(solution)/shard_map/pallas_call | solution.py:1400
  463.3 91.4 %shard_map.237 = (bf16[8,512,1408]{2,1,0:T(8,128)(2,1)}, f32[256,2048]{1,0:T(8,128)}) custom-call(bf16[512,1408]{1,0:T(8,128)(2,1)} %reduce-scatter.5.cloned.1.call-done.refs_0_, bf16[8,256,768]{2,1,0:T(8,128)(2,1)} %bitcast.74, bf16[2048,1024]{1,0:T(8,128)(2,1)} %all-gather.4.cloned.1.call-done.refs_0_.refs_2_), custom_call_target="tpu_custom_call" | custom-call | bytes 39845888 | tf_op jit(solution)/shard_map/pallas_call | solution.py:550
  554.8 2.6 fusion.10
  557.5 13.1 %shard_map.241 = (f32[512,5632]{1,0:T(8,128)}, f32[512,5632]{1,0:T(8,128)}) custom-call(bf16[8,512,1408]{2,1,0:T(8,128)(2,1)} %get-tuple-element.86.source), custom_call_target="tpu_custom_call" | custom-call | bytes 34603008 | tf_op jit(solution)/shard_map/pallas_call | solution.py:851
  571.4 3.7 fusion.9
  575.1 45.2 %shard_map.238 = (bf16[8,512,768]{2,1,0:T(8,128)(2,1)}, bf16[8,64,2048]{2,1,0:T(8,128)(2,1)}, f32[8,8,2048]{2,1,0:T(8,128)}) custom-call(bf16[512,768]{1,0:T(8,128)(2,1)} %reduce-scatter.9.cloned.1.call-done.refs_0_, bf16[64,2048]{1,0:T(8,128)(2,1)} %reduce-scatter.11.cloned.1.call-done.refs_1_, f32[4,8,2048]{2,1,0:T(8,128)} %select_maximum_fusion.refs_2_), custom_call_target="tpu_custom_call" | custom-call | bytes 17563648 | tf_op jit(solution)/shard_map/pallas_call | solution.py:550
  622.6 7.8 %shard_map.239 = f32[512,6144]{1,0:T(8,128)} custom-call(bf16[8,512,768]{2,1,0:T(8,128)(2,1)} %get-tuple-element.84.source), custom_call_target="tpu_custom_call" | custom-call | bytes 18874368 | tf_op jit(solution)/shard_map/pallas_call | solution.py:1426
  630.4 3.4 shard_map.240
  (110 shorter events, 22.4 us)
Async XLA Ops:
  7.2 101.9 %all-gather.4.cloned.1.call-start = ((), (), s32[]{:S(2)}) async-start(), calls=%async_computation.4 | async-start | bytes 5242880 | tf_op jit(solution)/shard_map/all_gather | solution.py:1890
  9.7 192.0 %all-gather.6.cloned.1.call-start = ((), (), s32[]{:S(2)}) async-start(), calls=%async_computation.5 | async-start | bytes 7208960 | tf_op jit(solution)/shard_map/all_gather | solution.py:1891
  16.7 2.2 copy-start.18
  16.7 2.5 copy-start.14
  16.7 2.7 copy-start.15
  16.7 2.9 copy-start.16
  16.7 3.2 copy-start.17
  16.7 3.4 copy-start.12
  16.8 244.5 %all-gather.8.cloned.1.call-start = ((), (), s32[]{:S(2)}) async-start(), calls=%async_computation.6 | async-start | bytes 3604480 | tf_op jit(solution)/shard_map/all_gather | solution.py:1892
  18.9 86.2 %copy-start.10 = (s32[1,2048]{1,0:T(1,128)S(1)}, s32[1,2048]{1,0:T(1,128)}, u32[]{:S(2)}) copy-start(s32[1,2048]{1,0:T(1,128)} %param.15) | copy-start | bytes 24580
  18.9 350.3 %reduce-scatter.7.cloned.1.call-start = ((), (), s32[]{:S(2)}) async-start(), calls=%async_computation.8 | async-start | bytes 3604480 | tf_op jit(solution)/shard_map/reduce_scatter | solution.py:1983
  107.1 46.4 %copy-start.2 = (s32[1,2048]{1,0:T(1,128)}, s32[1,2048]{1,0:T(1,128)S(1)}, u32[]{:S(2)}) copy-start(s32[1,2048]{1,0:T(1,128)S(1)} %compare_select_fusion.1.starts.refs_9_) | copy-start | bytes 24580
  109.1 44.4 %copy-start.4 = (s32[16]{0:T(128)}, s32[16]{0:T(128)S(1)}, u32[]{:S(2)}) copy-start(s32[16]{0:T(128)S(1)} %select_reduce_fusion.order.refs_3_) | copy-start | bytes 196
  177.6 1.3 copy-start
  254.8 208.5 %reduce-scatter.5.cloned.1.call-start = ((), (), s32[]{:S(2)}) async-start(), calls=%async_computation.7 | async-start | bytes 7208960 | tf_op jit(solution)/shard_map/reduce_scatter | solution.py:1983
  344.0 1.2 copy-start.9
  344.0 231.0 %reduce-scatter.11.cloned.1.call-start = ((), (), s32[]{:S(2)}) async-start(), calls=%async_computation.10 | async-start | bytes 1310720 | tf_op jit(solution)/shard_map/reduce_scatter | solution.py:1983
  451.6 1.2 copy-start.5
  451.6 123.5 %reduce-scatter.9.cloned.1.call-start = ((), (), s32[]{:S(2)}) async-start(), calls=%async_computation.9 | async-start | bytes 3932160 | tf_op jit(solution)/shard_map/reduce_scatter | solution.py:1983
  451.7 1.9 copy-start.6
  452.4 1.9 copy-start.8
  454.3 1.3 copy-start.13
  554.8 2.6 copy-start.11
  557.5 13.9 %copy-start.7 = (f32[256,2048]{1,0:T(8,128)S(1)}, f32[256,2048]{1,0:T(8,128)}, u32[]{:S(2)}) copy-start(f32[256,2048]{1,0:T(8,128)} %get-tuple-element.78) | copy-start | bytes 6291460
  (2 other events, 1.6 us)
Sparse Core Ops, SparseCore 0:
  10.2 84.1 all-gather.3
  96.5 105.1 all-gather.5
  203.8 57.4 all-gather.7
  263.5 54.8 reduce-scatter.6
  344.1 100.1 reduce-scatter.4
  451.7 24.3 reduce-scatter.10
  478.6 58.8 reduce-scatter.8

commit v7 on v6

--- a/solution.py
+++ b/solution.py
@@ -801,6 +801,43 @@
     )
 
 
+def norm_produce_run(produce, *refs):
+    grads, weights, tokens, grad_residual, gain, grad_tokens, sums, grad_normed, *scratch = refs
+    yield from produce_run(produce, 1, 0, 2, grads, weights, grad_normed, *scratch)
+    sums[...] = jnp.zeros_like(sums)
+    chunk = 32
+
+    @pl.loop(0, tokens.shape[0] // chunk)
+    def _(i):
+        at = pl.ds(pl.multiple_of(i * chunk, chunk), chunk)
+        unit, inverse = centre(tokens[at].astype(jnp.float32))
+        rows = grad_normed[at]
+        sums[:1] += jnp.sum(rows * unit, 0, keepdims=True)
+        sums[1:] += jnp.sum(rows, 0, keepdims=True)
+        scaled = rows * gain[...]
+        grad_tokens[at] = grad_residual[at] + inverse * (
+            scaled
+            - jnp.mean(scaled, -1, keepdims=True)
+            - unit * jnp.mean(scaled * unit, -1, keepdims=True)
+        )
+
+
+def norm_produce_op(produce, grads, weights, tokens, grad_residual, gain):
+    rows, width = tokens.shape
+    return dict(
+        run=functools.partial(norm_produce_run, produce),
+        inputs=[grads, weights, tokens, grad_residual, gain],
+        in_space=pltpu.VMEM,
+        outs=[
+            jax.ShapeDtypeStruct((rows, width), jnp.float32),
+            jax.ShapeDtypeStruct((2, width), jnp.float32),
+        ],
+        out_space=pltpu.VMEM,
+        scratch=[pltpu.VMEM((rows, width), jnp.float32)] + scatter_scratch(rows, width),
+        moved=32 * rows * width,
+    )
+
+
 def tile_rows(ref, tile, me):
     half = ref.shape[1] // 2
     return jnp.concatenate(
@@ -994,25 +1031,16 @@
     for step in order:
         load(others[step]).start()
     greet(others[1:])
-    sums[...] = jnp.zeros_like(sums)
-    chunk = 32
-
-    @pl.loop(0, residual.shape[0] // chunk)
-    def _(i):
-        at = pl.ds(pl.multiple_of(i * chunk, chunk), chunk)
-        unit, inverse = centre(residual[at])
-        grads = grad_normed[at]
-        sums[:1] += jnp.sum(grads * unit, 0, keepdims=True)
-        sums[1:] += jnp.sum(grads, 0, keepdims=True)
-        scaled = grads * gain[...]
-        total = cotangent[at].astype(jnp.float32) + inverse * (
-            scaled
-            - jnp.mean(scaled, -1, keepdims=True)
-            - unit * jnp.mean(scaled * unit, -1, keepdims=True)
-        )
-        grad_residual[at] = total
-        grad_branch[at] = total.astype(jnp.bfloat16)
-
+    unit, inverse = centre(residual[...])
+    grads = grad_normed[...]
+    scaled = grads * gain[...]
+    total = cotangent[...].astype(jnp.float32) + inverse * (
+        scaled
+        - jnp.mean(scaled, -1, keepdims=True)
+        - unit * jnp.mean(scaled * unit, -1, keepdims=True)
+    )
+    grad_residual[...] = total
+    grad_branch[...] = total.astype(jnp.bfloat16)
     copies = []
     for step in order:
         other = others[step]
@@ -1032,6 +1060,8 @@
             )
         copy.start()
         copies.append(copy)
+    sums[:1] = jnp.sum(grads * unit, 0, keepdims=True)
+    sums[1:] = jnp.sum(grads, 0, keepdims=True)
     for copy in copies:
         copy.wait()
 
@@ -2031,32 +2061,35 @@
         grad_down_w, grad_out_w = plane(ctx_size, 7, down_op, out_op)
         layer_part = plane(ctx_size, 10, scatter_op(blocks(times(hidden, down_here)), ctx_size))
     if fused:
-        normed_op = produce_op(
-            product_of_rows,
-            rows_here,
-            width,
-            grad_projected.reshape(ctx_size, rows_here, 3 * cols),
-            qkv_here,
+        grad_both_w, grad_tokens, norm_one_sums = plane(
+            ctx_size,
+            8,
+            gather_op(grad_both_w, ctx_size, pace=3),
+            norm_produce_op(
+                product_of_rows,
+                grad_projected.reshape(ctx_size, rows_here, 3 * cols),
+                qkv_here,
+                tokens[0],
+                grad_residual,
+                gain_one,
+            ),
         )
     else:
-        normed_op = scatter_op(
-            blocks(times_transposed(grad_projected, qkv_here[:, : 3 * cols])), ctx_size
-        )
-    grad_both_w, grad_normed = plane_groups(
-        ctx_size, 8, gather_op(grad_both_w, ctx_size), normed_op
-    )
-    grad_out_w = reduced(grad_out_w)
+        grad_both_w, grad_normed = plane_groups(
+            ctx_size,
+            8,
+            gather_op(grad_both_w, ctx_size),
+            scatter_op(
+                blocks(times_transposed(grad_projected, qkv_here[:, : 3 * cols])), ctx_size
+            ),
+        )
+        grad_tokens = grad_residual + norm_back(grad_normed, unit_one, inverse_one, gain_one)
+        norm_one_sums = jnp.stack([jnp.sum(grad_normed * unit_one, 0), jnp.sum(grad_normed, 0)])
     layer_out = residual + layer_part
     grad_qkv_w = reduced(grad_qkv_w)
-    grad_tokens = grad_residual + norm_back(grad_normed, unit_one, inverse_one, gain_one)
-
-    norm_sums = jnp.concatenate(
-        [
-            jnp.sum(grad_normed * unit_one, 0, keepdims=True),
-            jnp.sum(grad_normed, 0, keepdims=True),
-            norm_two_sums,
-        ]
-    )
+    grad_out_w = reduced(grad_out_w)
+
+    norm_sums = jnp.concatenate([norm_one_sums, norm_two_sums])
     norm_sums = jnp.transpose(norm_sums.reshape(4, fsdp_size, shard_rows), (1, 0, 2)).reshape(
         fsdp_size, 1, 4 * shard_rows
     )

time: 646 us -> 642 us (level)
  transfers between devices with their start and end apart: 7 -> 7, of which waited for: 2 -> 2; matrix products, arithmetic and copies ran while one was open for 5% -> 4% of each run, Pallas kernels for 81% -> 81%
where the time goes in v7:
time: 642 us; the launch traced here: 637 us
  Pallas kernels  576 us (90%)
  local copies, waits for them, and re-layouts  23.1 us (4%)
  between operations  14.9 us (2%)
  other arithmetic  11.7 us (2%)
  waiting for transfers between devices  11.1 us (2%)
    pallas_call x5, Pallas kernels, plane(): pl.pallas_call(functools.partial(plane_kernel, size, parts, far, z_size),...  346 us
    pallas_call x1, Pallas kernels, backward_mlp(): pl.pallas_call(functools.partial(backward_kernel, hidden_size), in_specs=...  82.6 us
    pallas_call x1, Pallas kernels, forward_mlp(): pl.pallas_call(functools.partial(forward_kernel, hidden_size), in_specs=[...  53.1 us
    pallas_call x1, Pallas kernels, attend(): pl.pallas_call(functools.partial(attend_kernel, block, heads), in_specs=[...  23.4 us
    pallas_call x1, Pallas kernels, part_rows(): pl.pallas_call(functools.partial(part_kernel, size), in_specs=[vmem] * 4...  20.8 us
    pallas_call x1, Pallas kernels, join_rows(): pl.pallas_call(functools.partial(join_kernel, size), in_specs=[any_space]...  18.1 us
    pallas_call x1, Pallas kernels, unpack_both(): pl.pallas_call(functools.partial(unpack_both_kernel, segments, count), gr...  13 us
  transfers between devices with their start and end apart: 7, of which 2 were waited for; matrix products, arithmetic and copies ran while one was open for 4% of the time, Pallas kernels for 81%

profile of v7, /device:TPU:0, one launch (start us, length us, event | category | flops | bytes accessed | tf_op | source)
XLA Modules:
  0.0 637.1 jit_solution(15565324009731331279)
XLA Ops:
  7.2 1.3 constant_dynamic-slice_fusion.14
  10.9 2.9 constant_dynamic-slice_fusion.5
  14.5 2.2 concatenate.25
  16.8 2.0 constant_dynamic-slice_fusion.1
  21.7 81.3 %shard_map.229 = (f32[2048,128]{1,0:T(8,128)}, f32[2048,128]{1,0:T(8,128)}, f32[2048,128]{1,0:T(8,128)}, bf16[4,32,128]{2,1,0:T(8,128)(2,1)}, bf16[8,256,2048]{2...) custom-call(f32[8,2048]{1,0:T(8,128)} %get-tuple-element.114.refs_0_, f32[8,2048]{1,0:T(8,128)} %get-tuple-element.113.refs_1_, ...), custom_call_target="tpu_custom_call" | custom-call | bytes 35684352 | tf_op jit(solution)/shard_map/pallas_call | solution.py:550
  105.7 1.3 compare_select_fusion.1.starts.refs_9_
  109.1 44.3 %shard_map.230 = (bf16[2048,2048]{1,0:T(8,128)(2,1)}, bf16[8,256,768]{2,1,0:T(8,128)(2,1)}, bf16[2048,2048]{1,0:T(8,128)(2,1)}) custom-call(bf16[2048,1024]{1,0:T(8,128)(2,1)} %all-gather.4.cloned.1.call-done.refs_0_.refs_2_, bf16[8,256,2048]{2,1,0:T(8,128)(2,1)} %get-tuple-element.52.refs_1_, ...), custom_call_target="tpu_custom_call" | custom-call | bytes 83886080 | tf_op jit(solution)/shard_map/pallas_call | solution.py:550
  153.4 23.4 %shard_map.231 = (bf16[2048,768]{1,0:T(8,128)(2,1)}, f32[2048,256]{1,0:T(8,128)S(1)}, bf16[2048,256]{1,0:T(8,128)(2,1)S(1)}, f32[8,1,1024]{2,1,0:T(1,128)S(1)}) custom-call(s32[16]{0:T(128)S(1)} %select_reduce_fusion.order.refs_3_, s32[8]{0:T(128)S(1)} %and_select_fusion.1.lowest, bf16[2048,768]{1,0:T(8,128)(2,1)} %bitcast.83, ...), custom_call_target="tpu_custom_call" | custom-call | flops 4294967296 | bytes 6291456 | tf_op jit(solution)/shard_map/pallas_call | solution.py:1600
  176.8 1.3 copy-done
  179.7 18.1 %shard_map.232 = (bf16[256,2048]{1,0:T(8,128)(2,1)}, f32[256,2048]{1,0:T(8,128)}, bf16[256,2048]{1,0:T(8,128)(2,1)}) custom-call(bf16[8,256,256]{2,1,0:T(8,128)(2,1)} %bitcast.53, bf16[2048,2048]{1,0:T(8,128)(2,1)} %get-tuple-element.59.weights, bf16[256,2048]{1,0:T(8,128)(2,1)} %bitcast.57, f32[1,2048]{1,0:T(1,128)} %bitcast.72, f32[1,2048]{1,0:T(1,128)} %bitcast.75), custom_call_target="tpu_custom_call" | custom-call | flops 2147483648 | bytes 8388608 | tf_op jit(solution)/shard_map/pallas_call | solution.py:979
  197.9 3.8 all-gather.6.cloned.1.call-done.weights
  201.7 53.1 %shard_map.233 = (bf16[2048,2048]{1,0:T(8,128)(2,1)}, f32[8,256,1408]{2,1,0:T(8,128)}, bf16[8,256,704]{2,1,0:T(8,128)(2,1)}, bf16[704,2048]{1,0:T(8,128)(2,1)}) custom-call(bf16[256,2048]{1,0:T(8,128)(2,1)} %get-tuple-element.62.normed, bf16[2048,1408]{1,0:T(8,128)(2,1)} %all-gather.6.cloned.1.call-done.weights, bf16[8,256,2048]{2,1,0:T(8,128)(2,1)} %get-tuple-element.61.grads), custom_call_target="tpu_custom_call" | custom-call | flops 17716740096 | bytes 33554432 | tf_op jit(solution)/shard_map/pallas_call | solution.py:1198
  254.8 6.5 %all-gather.8.cloned.1.call-done.down = bf16[704,2048]{1,0:T(8,128)(2,1)} async-done(((bf16[176,2048]{1,0:T(8,128)(2,1)}), bf16[704,2048]{1,0:T(8,128)(2,1)}) %all-gather.8.cloned.1.call-update) | async-done | bytes 2883600 | tf_op jit(solution)/shard_map/all_gather | solution.py:1922
  261.3 82.6 %shard_map.234 = (f32[256,2048]{1,0:T(8,128)}, bf16[2048,1408]{1,0:T(8,128)(2,1)}, f32[256,2048]{1,0:T(8,128)}) custom-call(bf16[8,256,2048]{2,1,0:T(8,128)(2,1)} %get-tuple-element.61.grads, f32[8,256,1408]{2,1,0:T(8,128)} %get-tuple-element.63.values, bf16[2048,1408]{1,0:T(8,128)(2,1)} %all-gather.6.cloned.1.call-done.weights, ...), custom_call_target="tpu_custom_call" | custom-call | flops 29527900160 | bytes 33554432 | tf_op jit(solution)/shard_map/pallas_call | solution.py:1389
  346.9 20.8 %shard_map.235 = (f32[256,2048]{1,0:T(8,128)}, bf16[256,2048]{1,0:T(8,128)(2,1)}, f32[2,2048]{1,0:T(2,128)}, bf16[8,256,256]{2,1,0:T(8,128)(2,1)}) custom-call(f32[256,2048]{1,0:T(8,128)} %get-tuple-element.70.grad_normed, f32[256,2048]{1,0:T(8,128)} %get-tuple-element.60.residual, bf16[256,2048]{1,0:T(8,128)(2,1)} %bitcast.60, f32[1,2048]{1,0:T(1,128)} %bitcast.73, ...), custom_call_target="tpu_custom_call" | custom-call | flops 2147483648 | bytes 8388608 | tf_op jit(solution)/shard_map/pallas_call | solution.py:1076
  367.8 82.3 %shard_map.236 = (bf16[8,176,2048]{2,1,0:T(8,128)(2,1)}, bf16[256,2048]{1,0:T(8,128)(2,1)}, bf16[2048,768]{1,0:T(8,128)(2,1)}, f32[1,768]{1,0:T(1,128)}, bf16[2048,768]{1,0:T(8,128)(2,1)}) custom-call(bf16[176,2048]{1,0:T(8,128)(2,1)} %reduce-scatter.7.cloned.1.call-done.refs_0_, bf16[8,256,256]{2,1,0:T(8,128)(2,1)} %bitcast.61, ...), custom_call_target="tpu_custom_call" | custom-call | bytes 38797312 | tf_op jit(solution)/shard_map/pallas_call | solution.py:550
  451.7 2.8 fusion
  454.6 7.7 %shard_map.242 = f32[8,176,2048]{2,1,0:T(8,128)} custom-call(bf16[8,176,2048]{2,1,0:T(8,128)(2,1)} %get-tuple-element.91.source), custom_call_target="tpu_custom_call" | custom-call | bytes 17301504 | tf_op jit(solution)/shard_map/pallas_call | solution.py:1430
  462.3 92.0 %shard_map.237 = (bf16[8,512,1408]{2,1,0:T(8,128)(2,1)}, f32[256,2048]{1,0:T(8,128)}, f32[2,2048]{1,0:T(2,128)}) custom-call(bf16[512,1408]{1,0:T(8,128)(2,1)} %reduce-scatter.5.cloned.1.call-done.refs_0_, bf16[8,256,768]{2,1,0:T(8,128)(2,1)} %bitcast.64, bf16[2048,1024]{1,0:T(8,128)(2,1)} %all-gather.4.cloned.1.call-done.refs_0_.refs_2_, ...), custom_call_target="tpu_custom_call" | custom-call | bytes 39845888 | tf_op jit(solution)/shard_map/pallas_call | solution.py:550
  555.1 13.0 %shard_map.241 = (f32[512,5632]{1,0:T(8,128)}, f32[512,5632]{1,0:T(8,128)}) custom-call(bf16[8,512,1408]{2,1,0:T(8,128)(2,1)} %get-tuple-element.88.source), custom_call_target="tpu_custom_call" | custom-call | bytes 34603008 | tf_op jit(solution)/shard_map/pallas_call | solution.py:888
  568.8 45.9 %shard_map.238 = (bf16[8,512,768]{2,1,0:T(8,128)(2,1)}, bf16[8,64,2048]{2,1,0:T(8,128)(2,1)}, f32[8,8,2048]{2,1,0:T(8,128)}) custom-call(bf16[512,768]{1,0:T(8,128)(2,1)} %reduce-scatter.9.cloned.1.call-done.refs_0_, bf16[64,2048]{1,0:T(8,128)(2,1)} %reduce-scatter.11.cloned.1.call-done.refs_1_, f32[4,8,2048]{2,1,0:T(8,128)} %select_maximum_fusion.refs_2_), custom_call_target="tpu_custom_call" | custom-call | bytes 17563648 | tf_op jit(solution)/shard_map/pallas_call | solution.py:550
  617.1 7.8 %shard_map.239 = f32[512,6144]{1,0:T(8,128)} custom-call(bf16[8,512,768]{2,1,0:T(8,128)(2,1)} %get-tuple-element.86.source), custom_call_target="tpu_custom_call" | custom-call | bytes 18874368 | tf_op jit(solution)/shard_map/pallas_call | solution.py:1456
  624.9 3.5 shard_map.240
  628.4 1.3 copy.60
  (98 shorter events, 20.8 us)
Async XLA Ops:
  7.2 101.9 %all-gather.4.cloned.1.call-start = ((), (), s32[]{:S(2)}) async-start(), calls=%async_computation.4 | async-start | bytes 5242880 | tf_op jit(solution)/shard_map/all_gather | solution.py:1920
  9.7 192.0 %all-gather.6.cloned.1.call-start = ((), (), s32[]{:S(2)}) async-start(), calls=%async_computation.5 | async-start | bytes 7208960 | tf_op jit(solution)/shard_map/all_gather | solution.py:1921
  16.7 2.2 copy-start.16
  16.7 2.5 copy-start.12
  16.7 2.7 copy-start.13
  16.7 2.9 copy-start.14
  16.7 3.2 copy-start.15
  16.7 3.4 copy-start.10
  16.8 244.5 %all-gather.8.cloned.1.call-start = ((), (), s32[]{:S(2)}) async-start(), calls=%async_computation.6 | async-start | bytes 3604480 | tf_op jit(solution)/shard_map/all_gather | solution.py:1922
  18.9 86.2 %copy-start.8 = (s32[1,2048]{1,0:T(1,128)S(1)}, s32[1,2048]{1,0:T(1,128)}, u32[]{:S(2)}) copy-start(s32[1,2048]{1,0:T(1,128)} %param.15) | copy-start | bytes 24580
  18.9 348.9 %reduce-scatter.7.cloned.1.call-start = ((), (), s32[]{:S(2)}) async-start(), calls=%async_computation.8 | async-start | bytes 3604480 | tf_op jit(solution)/shard_map/reduce_scatter | solution.py:2013
  107.0 46.4 %copy-start.2 = (s32[1,2048]{1,0:T(1,128)}, s32[1,2048]{1,0:T(1,128)S(1)}, u32[]{:S(2)}) copy-start(s32[1,2048]{1,0:T(1,128)S(1)} %compare_select_fusion.1.starts.refs_9_) | copy-start | bytes 24580
  109.1 44.4 %copy-start.4 = (s32[16]{0:T(128)}, s32[16]{0:T(128)S(1)}, u32[]{:S(2)}) copy-start(s32[16]{0:T(128)S(1)} %select_reduce_fusion.order.refs_3_) | copy-start | bytes 196
  176.8 1.3 copy-start
  178.1 1.0 copy-start.1
  179.1 0.6 copy-start.3
  254.8 207.5 %reduce-scatter.5.cloned.1.call-start = ((), (), s32[]{:S(2)}) async-start(), calls=%async_computation.7 | async-start | bytes 7208960 | tf_op jit(solution)/shard_map/reduce_scatter | solution.py:2013
  344.0 1.2 copy-start.7
  344.0 224.8 %reduce-scatter.11.cloned.1.call-start = ((), (), s32[]{:S(2)}) async-start(), calls=%async_computation.10 | async-start | bytes 1310720 | tf_op jit(solution)/shard_map/reduce_scatter | solution.py:2013
  450.1 1.6 copy-start.5
  450.2 118.7 %reduce-scatter.9.cloned.1.call-start = ((), (), s32[]{:S(2)}) async-start(), calls=%async_computation.9 | async-start | bytes 3932160 | tf_op jit(solution)/shard_map/reduce_scatter | solution.py:2013
  451.7 2.8 copy-start.11
  462.3 92.0 %copy-start.9 = (f32[2,2048]{1,0:T(2,128)S(1)}, f32[2,2048]{1,0:T(2,128)}, u32[]{:S(2)}) copy-start(f32[2,2048]{1,0:T(2,128)} %get-tuple-element.83) | copy-start | bytes 49156
  624.9 3.5 copy-start.6
Sparse Core Ops, SparseCore 0:
  10.2 84.1 all-gather.3
  96.5 105.1 all-gather.5
  203.8 57.4 all-gather.7
  263.5 54.8 reduce-scatter.6
  344.1 100.1 reduce-scatter.4
  450.3 24.3 reduce-scatter.10
  477.1 58.8 reduce-scatter.8

commit v8 on v7

--- a/solution.py
+++ b/solution.py
@@ -812,8 +812,9 @@
         at = pl.ds(pl.multiple_of(i * chunk, chunk), chunk)
         unit, inverse = centre(tokens[at].astype(jnp.float32))
         rows = grad_normed[at]
-        sums[:1] += jnp.sum(rows * unit, 0, keepdims=True)
-        sums[1:] += jnp.sum(rows, 0, keepdims=True)
+        sums[...] += two_rows(
+            jnp.sum(rows * unit, 0, keepdims=True), jnp.sum(rows, 0, keepdims=True)
+        )
         scaled = rows * gain[...]
         grad_tokens[at] = grad_residual[at] + inverse * (
             scaled
@@ -902,6 +903,11 @@
     me = lax.axis_index("ctx")
     bits = size.bit_length() - 1
     greet([flipped(me, 1 << bit, bits) for bit in range(bits)])
+
+
+def two_rows(first, second):
+    row = lax.broadcasted_iota(jnp.int32, (2, first.shape[1]), 0)
+    return jnp.where(row == 0, first, second)
 
 
 def centre(values):
@@ -1060,8 +1066,9 @@
             )
         copy.start()
         copies.append(copy)
-    sums[:1] = jnp.sum(grads * unit, 0, keepdims=True)
-    sums[1:] = jnp.sum(grads, 0, keepdims=True)
+    sums[...] = two_rows(
+        jnp.sum(grads * unit, 0, keepdims=True), jnp.sum(grads, 0, keepdims=True)
+    )
     for copy in copies:
         copy.wait()
 

time: 642 us -> 642 us (level)
  transfers between devices with their start and end apart: 7 -> 7, of which waited for: 2 -> 2; matrix products, arithmetic and copies ran while one was open for 4% -> 4% of each run, Pallas kernels for 81% -> 82%
where the time goes in v8:
time: 642 us; the launch traced here: 637 us
  Pallas kernels  577 us (90%)
  local copies, waits for them, and re-layouts  23.1 us (4%)
  between operations  14.9 us (2%)
  other arithmetic  11.7 us (2%)
  waiting for transfers between devices  9.65 us (2%)
    pallas_call x5, Pallas kernels, plane(): pl.pallas_call(functools.partial(plane_kernel, size, parts, far, z_size),...  346 us
    pallas_call x1, Pallas kernels, backward_mlp(): pl.pallas_call(functools.partial(backward_kernel, hidden_size), in_specs=...  82.6 us
    pallas_call x1, Pallas kernels, forward_mlp(): pl.pallas_call(functools.partial(forward_kernel, hidden_size), in_specs=[...  53.1 us
    pallas_call x1, Pallas kernels, attend(): pl.pallas_call(functools.partial(attend_kernel, block, heads), in_specs=[...  24.8 us
    pallas_call x1, Pallas kernels, part_rows(): pl.pallas_call(functools.partial(part_kernel, size), in_specs=[vmem] * 4...  20.8 us
    pallas_call x1, Pallas kernels, join_rows(): pl.pallas_call(functools.partial(join_kernel, size), in_specs=[any_space]...  18.2 us
    pallas_call x1, Pallas kernels, unpack_both(): pl.pallas_call(functools.partial(unpack_both_kernel, segments, count), gr...  13 us
  transfers between devices with their start and end apart: 7, of which 2 were waited for; matrix products, arithmetic and copies ran while one was open for 4% of the time, Pallas kernels for 82%

profile of v8, /device:TPU:0, one launch (start us, length us, event | category | flops | bytes accessed | tf_op | source)
XLA Modules:
  0.0 637.0 jit_solution(3979564459211110063)
XLA Ops:
  7.2 1.3 constant_dynamic-slice_fusion.14
  10.9 2.9 constant_dynamic-slice_fusion.5
  14.5 2.2 concatenate.25
  16.8 2.0 constant_dynamic-slice_fusion.1
  21.7 81.3 %shard_map.229 = (f32[2048,128]{1,0:T(8,128)}, f32[2048,128]{1,0:T(8,128)}, f32[2048,128]{1,0:T(8,128)}, bf16[4,32,128]{2,1,0:T(8,128)(2,1)}, bf16[8,256,2048]{2...) custom-call(f32[8,2048]{1,0:T(8,128)} %get-tuple-element.114.refs_0_, f32[8,2048]{1,0:T(8,128)} %get-tuple-element.113.refs_1_, ...), custom_call_target="tpu_custom_call" | custom-call | bytes 35684352 | tf_op jit(solution)/shard_map/pallas_call | solution.py:550
  105.7 1.3 compare_select_fusion.1.starts.refs_9_
  109.1 44.3 %shard_map.230 = (bf16[2048,2048]{1,0:T(8,128)(2,1)}, bf16[8,256,768]{2,1,0:T(8,128)(2,1)}, bf16[2048,2048]{1,0:T(8,128)(2,1)}) custom-call(bf16[2048,1024]{1,0:T(8,128)(2,1)} %all-gather.4.cloned.1.call-done.refs_0_.refs_2_, bf16[8,256,2048]{2,1,0:T(8,128)(2,1)} %get-tuple-element.52.refs_1_, ...), custom_call_target="tpu_custom_call" | custom-call | bytes 83886080 | tf_op jit(solution)/shard_map/pallas_call | solution.py:550
  153.4 24.8 %shard_map.231 = (bf16[2048,768]{1,0:T(8,128)(2,1)}, f32[2048,256]{1,0:T(8,128)S(1)}, bf16[2048,256]{1,0:T(8,128)(2,1)S(1)}, f32[8,1,1024]{2,1,0:T(1,128)S(1)}) custom-call(s32[16]{0:T(128)S(1)} %select_reduce_fusion.order.refs_3_, s32[8]{0:T(128)S(1)} %and_select_fusion.1.lowest, bf16[2048,768]{1,0:T(8,128)(2,1)} %bitcast.83, ...), custom_call_target="tpu_custom_call" | custom-call | flops 4294967296 | bytes 6291456 | tf_op jit(solution)/shard_map/pallas_call | solution.py:1607
  178.3 1.3 copy-done
  181.2 18.2 %shard_map.232 = (bf16[256,2048]{1,0:T(8,128)(2,1)}, f32[256,2048]{1,0:T(8,128)}, bf16[256,2048]{1,0:T(8,128)(2,1)}) custom-call(bf16[8,256,256]{2,1,0:T(8,128)(2,1)} %bitcast.53, bf16[2048,2048]{1,0:T(8,128)(2,1)} %get-tuple-element.59.weights, bf16[256,2048]{1,0:T(8,128)(2,1)} %bitcast.57, f32[1,2048]{1,0:T(1,128)} %bitcast.72, f32[1,2048]{1,0:T(1,128)} %bitcast.75), custom_call_target="tpu_custom_call" | custom-call | flops 2147483648 | bytes 8388608 | tf_op jit(solution)/shard_map/pallas_call | solution.py:985
  199.3 2.3 all-gather.6.cloned.1.call-done.weights
  201.7 53.1 %shard_map.233 = (bf16[2048,2048]{1,0:T(8,128)(2,1)}, f32[8,256,1408]{2,1,0:T(8,128)}, bf16[8,256,704]{2,1,0:T(8,128)(2,1)}, bf16[704,2048]{1,0:T(8,128)(2,1)}) custom-call(bf16[256,2048]{1,0:T(8,128)(2,1)} %get-tuple-element.62.normed, bf16[2048,1408]{1,0:T(8,128)(2,1)} %all-gather.6.cloned.1.call-done.weights, bf16[8,256,2048]{2,1,0:T(8,128)(2,1)} %get-tuple-element.61.grads), custom_call_target="tpu_custom_call" | custom-call | flops 17716740096 | bytes 33554432 | tf_op jit(solution)/shard_map/pallas_call | solution.py:1205
  254.8 6.5 %all-gather.8.cloned.1.call-done.down = bf16[704,2048]{1,0:T(8,128)(2,1)} async-done(((bf16[176,2048]{1,0:T(8,128)(2,1)}), bf16[704,2048]{1,0:T(8,128)(2,1)}) %all-gather.8.cloned.1.call-update) | async-done | bytes 2883600 | tf_op jit(solution)/shard_map/all_gather | solution.py:1929
  261.3 82.6 %shard_map.234 = (f32[256,2048]{1,0:T(8,128)}, bf16[2048,1408]{1,0:T(8,128)(2,1)}, f32[256,2048]{1,0:T(8,128)}) custom-call(bf16[8,256,2048]{2,1,0:T(8,128)(2,1)} %get-tuple-element.61.grads, f32[8,256,1408]{2,1,0:T(8,128)} %get-tuple-element.63.values, bf16[2048,1408]{1,0:T(8,128)(2,1)} %all-gather.6.cloned.1.call-done.weights, ...), custom_call_target="tpu_custom_call" | custom-call | flops 29527900160 | bytes 33554432 | tf_op jit(solution)/shard_map/pallas_call | solution.py:1396
  346.9 20.8 %shard_map.235 = (f32[256,2048]{1,0:T(8,128)}, bf16[256,2048]{1,0:T(8,128)(2,1)}, f32[2,2048]{1,0:T(2,128)}, bf16[8,256,256]{2,1,0:T(8,128)(2,1)}) custom-call(f32[256,2048]{1,0:T(8,128)} %get-tuple-element.70.grad_normed, f32[256,2048]{1,0:T(8,128)} %get-tuple-element.60.residual, bf16[256,2048]{1,0:T(8,128)(2,1)} %bitcast.60, f32[1,2048]{1,0:T(1,128)} %bitcast.73, ...), custom_call_target="tpu_custom_call" | custom-call | flops 2147483648 | bytes 8388608 | tf_op jit(solution)/shard_map/pallas_call | solution.py:1083
  367.8 82.3 %shard_map.236 = (bf16[8,176,2048]{2,1,0:T(8,128)(2,1)}, bf16[256,2048]{1,0:T(8,128)(2,1)}, bf16[2048,768]{1,0:T(8,128)(2,1)}, f32[1,768]{1,0:T(1,128)}, bf16[2048,768]{1,0:T(8,128)(2,1)}) custom-call(bf16[176,2048]{1,0:T(8,128)(2,1)} %reduce-scatter.7.cloned.1.call-done.refs_0_, bf16[8,256,256]{2,1,0:T(8,128)(2,1)} %bitcast.61, ...), custom_call_target="tpu_custom_call" | custom-call | bytes 38797312 | tf_op jit(solution)/shard_map/pallas_call | solution.py:550
  451.7 2.8 fusion
  454.6 7.7 %shard_map.242 = f32[8,176,2048]{2,1,0:T(8,128)} custom-call(bf16[8,176,2048]{2,1,0:T(8,128)(2,1)} %get-tuple-element.91.source), custom_call_target="tpu_custom_call" | custom-call | bytes 17301504 | tf_op jit(solution)/shard_map/pallas_call | solution.py:1437
  462.3 92.0 %shard_map.237 = (bf16[8,512,1408]{2,1,0:T(8,128)(2,1)}, f32[256,2048]{1,0:T(8,128)}, f32[2,2048]{1,0:T(2,128)}) custom-call(bf16[512,1408]{1,0:T(8,128)(2,1)} %reduce-scatter.5.cloned.1.call-done.refs_0_, bf16[8,256,768]{2,1,0:T(8,128)(2,1)} %bitcast.64, bf16[2048,1024]{1,0:T(8,128)(2,1)} %all-gather.4.cloned.1.call-done.refs_0_.refs_2_, ...), custom_call_target="tpu_custom_call" | custom-call | bytes 39845888 | tf_op jit(solution)/shard_map/pallas_call | solution.py:550
  555.1 13.0 %shard_map.241 = (f32[512,5632]{1,0:T(8,128)}, f32[512,5632]{1,0:T(8,128)}) custom-call(bf16[8,512,1408]{2,1,0:T(8,128)(2,1)} %get-tuple-element.88.source), custom_call_target="tpu_custom_call" | custom-call | bytes 34603008 | tf_op jit(solution)/shard_map/pallas_call | solution.py:889
  568.8 45.9 %shard_map.238 = (bf16[8,512,768]{2,1,0:T(8,128)(2,1)}, bf16[8,64,2048]{2,1,0:T(8,128)(2,1)}, f32[8,8,2048]{2,1,0:T(8,128)}) custom-call(bf16[512,768]{1,0:T(8,128)(2,1)} %reduce-scatter.9.cloned.1.call-done.refs_0_, bf16[64,2048]{1,0:T(8,128)(2,1)} %reduce-scatter.11.cloned.1.call-done.refs_1_, f32[4,8,2048]{2,1,0:T(8,128)} %select_maximum_fusion.refs_2_), custom_call_target="tpu_custom_call" | custom-call | bytes 17563648 | tf_op jit(solution)/shard_map/pallas_call | solution.py:550
  617.1 7.8 %shard_map.239 = f32[512,6144]{1,0:T(8,128)} custom-call(bf16[8,512,768]{2,1,0:T(8,128)(2,1)} %get-tuple-element.86.source), custom_call_target="tpu_custom_call" | custom-call | bytes 18874368 | tf_op jit(solution)/shard_map/pallas_call | solution.py:1463
  624.9 3.5 shard_map.240
  628.4 1.3 copy.60
  (98 shorter events, 20.8 us)
Async XLA Ops:
  7.2 101.9 %all-gather.4.cloned.1.call-start = ((), (), s32[]{:S(2)}) async-start(), calls=%async_computation.4 | async-start | bytes 5242880 | tf_op jit(solution)/shard_map/all_gather | solution.py:1927
  9.7 192.0 %all-gather.6.cloned.1.call-start = ((), (), s32[]{:S(2)}) async-start(), calls=%async_computation.5 | async-start | bytes 7208960 | tf_op jit(solution)/shard_map/all_gather | solution.py:1928
  16.7 2.2 copy-start.16
  16.7 2.5 copy-start.12
  16.7 2.7 copy-start.13
  16.7 2.9 copy-start.14
  16.7 3.2 copy-start.15
  16.7 3.4 copy-start.10
  16.8 244.5 %all-gather.8.cloned.1.call-start = ((), (), s32[]{:S(2)}) async-start(), calls=%async_computation.6 | async-start | bytes 3604480 | tf_op jit(solution)/shard_map/all_gather | solution.py:1929
  18.9 86.2 %copy-start.8 = (s32[1,2048]{1,0:T(1,128)S(1)}, s32[1,2048]{1,0:T(1,128)}, u32[]{:S(2)}) copy-start(s32[1,2048]{1,0:T(1,128)} %param.15) | copy-start | bytes 24580
  18.9 348.9 %reduce-scatter.7.cloned.1.call-start = ((), (), s32[]{:S(2)}) async-start(), calls=%async_computation.8 | async-start | bytes 3604480 | tf_op jit(solution)/shard_map/reduce_scatter | solution.py:2020
  107.0 46.4 %copy-start.2 = (s32[1,2048]{1,0:T(1,128)}, s32[1,2048]{1,0:T(1,128)S(1)}, u32[]{:S(2)}) copy-start(s32[1,2048]{1,0:T(1,128)S(1)} %compare_select_fusion.1.starts.refs_9_) | copy-start | bytes 24580
  109.1 44.4 %copy-start.4 = (s32[16]{0:T(128)}, s32[16]{0:T(128)S(1)}, u32[]{:S(2)}) copy-start(s32[16]{0:T(128)S(1)} %select_reduce_fusion.order.refs_3_) | copy-start | bytes 196
  178.3 1.3 copy-start
  179.6 1.0 copy-start.1
  180.5 0.6 copy-start.3
  254.8 207.5 %reduce-scatter.5.cloned.1.call-start = ((), (), s32[]{:S(2)}) async-start(), calls=%async_computation.7 | async-start | bytes 7208960 | tf_op jit(solution)/shard_map/reduce_scatter | solution.py:2020
  344.0 1.2 copy-start.7
  344.0 224.8 %reduce-scatter.11.cloned.1.call-start = ((), (), s32[]{:S(2)}) async-start(), calls=%async_computation.10 | async-start | bytes 1310720 | tf_op jit(solution)/shard_map/reduce_scatter | solution.py:2020
  450.1 1.6 copy-start.5
  450.2 118.7 %reduce-scatter.9.cloned.1.call-start = ((), (), s32[]{:S(2)}) async-start(), calls=%async_computation.9 | async-start | bytes 3932160 | tf_op jit(solution)/shard_map/reduce_scatter | solution.py:2020
  451.7 2.8 copy-start.11
  462.3 92.0 %copy-start.9 = (f32[2,2048]{1,0:T(2,128)S(1)}, f32[2,2048]{1,0:T(2,128)}, u32[]{:S(2)}) copy-start(f32[2,2048]{1,0:T(2,128)} %get-tuple-element.83) | copy-start | bytes 49156
  624.9 3.5 copy-start.6
Sparse Core Ops, SparseCore 0:
  10.2 84.1 all-gather.3
  96.5 105.1 all-gather.5
  203.8 57.4 all-gather.7
  263.5 54.8 reduce-scatter.6
  344.1 100.1 reduce-scatter.4
  450.3 24.3 reduce-scatter.10
  477.1 58.8 reduce-scatter.8
